TPU v7x, 32 devices: a whole 2x2x4 slice. The times are simulated.
32 devices in a mesh: dp: 16 (over z, y, x), feat: 2 (over core).
Axes of the slice: x: 2, y: 2, z: 4, core: 2. Of those that a mesh axis runs over, the one named last changes fastest.
Arguments:
- teacher: bfloat16 [2048, 1024], P('dp'), may hold values from -6 to 6
- student: bfloat16 [2048, 768], P('dp'), may hold values from -6 to 6
- head: bfloat16 [768, 1024], P(None, 'feat'), may hold values from -0.21875 to 0.21875
- freqs: bfloat16 [1024, 2048], P(None, 'feat'), may hold values from -0.1875 to 0.1875
- labels: int32 [2048], P('dp'), may hold values from 0 to 5455, as said below
- class_slot: int32 [5456], replicated, may hold values from 0 to 5455, as said below
Outputs:
- head_grad: float32 [1024, 768], P(('dp', 'feat'))
- class_loss: float32 [5456], P('dp')
Inputs may be any that keep to these rules, and one draw needn't show every extreme that they name: class_slot is a permutation of the classes. Of the 128 labels of one dp index, at most 16 have class_slot[label] // 341 equal to any one dp index; for one dp index that bound is reached from every dp index.
All inputs are finite; a program needn't handle non-finite values.
Results may differ from a plain program's by a relative error of at most 0.005.
Values may be sent and summed in bfloat16 or wider, within the bound.
No kernel may reach another device: no remote copies, remote signals or barrier semaphores. Data moves between devices by JAX's collectives and lax.ppermute only.
A program may use at most 64 MiB of HBM per device.

v0:
```python
import math

import jax
import jax.numpy as jnp
from jax import lax
from jax.sharding import PartitionSpec as P


def split_parts(values):
    upper = values.astype(jnp.bfloat16)
    lower = (values - upper.astype(jnp.float32)).astype(jnp.bfloat16)
    return (upper, lower)


def on_device(teacher, student, head, freqs, labels, class_slot):
    n_dp = lax.axis_size("dp")
    n_feat = lax.axis_size("feat")
    images = labels.shape[0]
    half = freqs.shape[1]
    cls_dev = class_slot.shape[0] // n_dp
    capacity = 2 * images // n_dp
    projected = jnp.dot(student, head, preferred_element_type=jnp.float32).astype(jnp.bfloat16)
    weight_rows = freqs
    student_z = jnp.dot(
        lax.all_gather(projected, "feat", axis=1, tiled=True),
        weight_rows,
        preferred_element_type=jnp.float32,
    )
    teacher_z = jnp.dot(teacher, freqs, preferred_element_type=jnp.float32)
    delta = jnp.concatenate(
        [jnp.cos(student_z) - jnp.cos(teacher_z), jnp.sin(student_z) - jnp.sin(teacher_z)], axis=1
    )
    position = jnp.take(class_slot, labels)
    owner = position // cls_dev
    local_cls = position % cls_dev
    marks = owner[:, None] == jnp.arange(n_dp, dtype=jnp.int32)[None, :]
    running = jnp.cumsum(marks.astype(jnp.int32), axis=0) - 1
    rank = jnp.sum(jnp.where(marks, running, 0), axis=1)
    slot = owner * capacity + rank
    outgoing = jnp.zeros((n_dp * capacity, 2 * half), jnp.float32).at[slot].set(delta)
    outgoing = outgoing.reshape(n_dp, capacity, 2 * half)
    tags = (
        jnp.full((n_dp * capacity,), -1.0, jnp.float32).at[slot].set(local_cls.astype(jnp.float32))
    )
    tags = tags.reshape(n_dp, capacity)
    rows_in, tags_in = (
        lax.all_to_all(outgoing, "dp", split_axis=0, concat_axis=0, tiled=True),
        lax.all_to_all(tags, "dp", split_axis=0, concat_axis=0, tiled=True),
    )
    rows_in = rows_in.reshape(n_dp * capacity, 2 * half)
    tag_ids = tags_in.reshape(n_dp * capacity).astype(jnp.int32)
    member_mask = jnp.arange(cls_dev, dtype=jnp.int32)[:, None] == tag_ids[None, :]
    member = member_mask.astype(jnp.bfloat16)
    rows_upper, rows_lower = split_parts(rows_in)
    sums = jnp.dot(member, rows_upper, preferred_element_type=jnp.float32) + jnp.dot(
        member, rows_lower, preferred_element_type=jnp.float32
    )
    floor_counts = jnp.maximum(jnp.sum(member_mask.astype(jnp.float32), axis=1), 1.0)
    means = sums / floor_counts[:, None]
    partial_norm = jnp.sum(sums * sums, axis=1)
    returned = jnp.take(means, jnp.maximum(tag_ids, 0), axis=0).reshape(n_dp, capacity, 2 * half)
    back = lax.all_to_all(returned, "dp", split_axis=0, concat_axis=0, tiled=True)
    picked = jnp.take(back.reshape(n_dp * capacity, 2 * half), slot, axis=0)
    norm_total = lax.psum(partial_norm, "feat")
    class_loss = norm_total / floor_counts / (2.0 * half * n_feat)
    grad_z = (
        -jnp.sin(student_z) * picked[:, :half] + jnp.cos(student_z) * picked[:, half:]
    ).astype(jnp.bfloat16)
    scale = 1.0 / math.sqrt(images * n_dp)
    inner = lax.dot_general(
        grad_z, student, (((0,), (0,)), ((), ())), preferred_element_type=jnp.float32
    )
    inner_upper, inner_lower = split_parts(inner)
    weight_rows = freqs
    head_grad = (
        lax.psum_scatter(
            jnp.dot(weight_rows, inner_upper, preferred_element_type=jnp.float32)
            + jnp.dot(weight_rows, inner_lower, preferred_element_type=jnp.float32),
            ("dp", "feat"),
            scatter_dimension=0,
            tiled=True,
        )
        * scale
    )
    return (head_grad, class_loss)


def solution(mesh):
    in_specs = (P("dp", None), P("dp", None), P(None, "feat"), P(None, "feat"), P("dp"), P())
    out_specs = (P(("dp", "feat"), None), P("dp"))
    return jax.shard_map(
        on_device, mesh=mesh, in_specs=in_specs, out_specs=out_specs, check_vma=False
    )
```

profile of v0, /device:TPU:0, one launch (start us, length us, event | category | flops | bytes accessed | tf_op | source)
XLA Modules:
  0.0 282.1 jit_solution(9930648233080652052)
XLA Ops:
  8.0 1.7 gather_fusion
  10.8 1.0 scatter_custom_fusion
  12.5 8.3 %all-to-all-start = ((f32[16,1,16]{2,1,0:T(1,128)}), f32[16,1,16]{2,1,0:T(1,128)S(1)}, u32[]{:S(2)}, u32[]{:S(2)}) async-start(f32[16,1,16]{2,1,0:T(1,128)} %all_to_all.12), calls=%async_computation | async-start | bytes 16384 | tf_op jit(solution)/shard_map/all_to_all | solution.py:48
  20.8 1.5 convolution_convert_fusion
  22.3 2.1 all_gather.3
  24.5 4.9 %fusion.20 = (f32[128,1024]{1,0:T(8,128)S(1)}, f32[128,1024]{1,0:T(8,128)S(1)}) fusion(bf16[128,1024]{1,0:T(8,128)(2,1)S(1)} %all_gather.3, bf16[1024,1024]{1,0:T(8,128)(2,1)S(1)} %copy-done), kind=kOutput, calls=%fused_computation.56 | convolution fusion | flops 268435456 | bytes 3407872 | tf_op jit(solution)/shard_map/dot_general | solution.py:24
  29.4 3.3 %cosine_subtract_fusion = (f32[128,1024]{1,0:T(8,128)}, f32[128,1024]{1,0:T(8,128)}) fusion(f32[128,1024]{1,0:T(8,128)S(1)} %get-tuple-element.23, f32[128,1024]{1,0:T(8,128)S(1)} %get-tuple-element.22, bf16[128,1024]{1,0:T(8,128)(2,1)S(1)} %copy-done.2, bf16[1024,1024]{1,0:T(8,128)(2,1)S(1)} %copy-done), kind=kOutput, calls=%fused_computation.29 | convolution fusion | flops 268697600 | bytes 4456448 | tf_op jit(solution)/shard_map/dot_general | solution.py:29
  32.7 3.4 %scatter_custom_fusion.1 = f32[256,2048]{1,0:T(8,128)} fusion(s32[128]{0:T(128)S(1)} %get-tuple-element.13, f32[128,1024]{1,0:T(8,128)} %get-tuple-element.21, f32[]{:T(128)} %constant.88, f32[128,1024]{1,0:T(8,128)} %get-tuple-element.20, f32[]{:T(128)} %constant.83.clone.1), kind=kCustom, calls=%fused_computation.14 | custom fusion | flops 262144 | bytes 3145736 | tf_op jit(solution)/shard_map/scatter | solution.py:40
  36.1 7.0 %all-to-all-start.1 = ((f32[16,16,2048]{2,1,0:T(8,128)}), f32[16,16,2048]{2,1,0:T(8,128)}, u32[]{:S(2)}, u32[]{:S(2)}) async-start(f32[16,16,2048]{2,1,0:T(8,128)} %bitcast.33), calls=%async_computation.1 | async-start | bytes 4194304 | tf_op jit(solution)/shard_map/all_to_all | solution.py:47
  43.4 43.0 %all-to-all-done.1 = f32[16,16,2048]{2,1,0:T(8,128)} async-done(((f32[16,16,2048]{2,1,0:T(8,128)}), f32[16,16,2048]{2,1,0:T(8,128)}, u32[]{:S(2)}, u32[]{:S(2)}) %all-to-all-start.1) | async-done | bytes 2097184 | tf_op jit(solution)/shard_map/all_to_all | solution.py:47
  86.4 1.9 fusion
  88.9 2.2 multiply_reduce_fusion
  91.1 5.4 %gather_fusion.1 = f32[256,2048]{1,0:T(8,128)} fusion(f32[341,2048]{1,0:T(8,128)} %get-tuple-element.19, s32[1024]{0:T(1024)S(1)} %pad_clamp_fusion.1), kind=kCustom, calls=%fused_computation.1 | custom fusion | bytes 4195328 | tf_op jit(solution)/shard_map/jit(_take)/gather | solution.py:61
  96.5 3.1 %broadcast_select_fusion = f32[16,16,2048]{2,1,0:T(8,128)} fusion(f32[16,16,2048]{2,1,0:T(8,128)} %bitcast.32, pred[16,16]{1,0:T(8,128)(4,1)S(1)} %compare_bitcast_fusion), kind=kLoop, calls=%fused_computation.18 | loop fusion | flops 524288 | bytes 4194560 | tf_op jit(solution)/shard_map/jit(_take)/select_n | solution.py:61
  99.6 10.2 %all-to-all-start.2 = ((f32[16,16,2048]{2,1,0:T(8,128)}), f32[16,16,2048]{2,1,0:T(8,128)}, u32[]{:S(2)}, u32[]{:S(2)}) async-start(f32[16,16,2048]{2,1,0:T(8,128)} %broadcast_select_fusion), calls=%async_computation.2 | async-start | bytes 4194304 | tf_op jit(solution)/shard_map/all_to_all | solution.py:62
  110.0 42.5 %all-to-all-done.2 = f32[16,16,2048]{2,1,0:T(8,128)} async-done(((f32[16,16,2048]{2,1,0:T(8,128)}), f32[16,16,2048]{2,1,0:T(8,128)}, u32[]{:S(2)}, u32[]{:S(2)}) %all-to-all-start.2) | async-done | bytes 2097184 | tf_op jit(solution)/shard_map/all_to_all | solution.py:62
  152.5 4.0 %gather_fusion.2 = f32[128,2048]{1,0:T(8,128)} fusion(f32[256,2048]{1,0:T(8,128)} %bitcast.5, s32[1024]{0:T(1024)S(1)} %pad_clamp_fusion), kind=kCustom, calls=%fused_computation.2 | custom fusion | bytes 2097664 | tf_op jit(solution)/shard_map/jit(_take)/gather | solution.py:63
  156.5 1.4 broadcast_select_fusion.1
  158.6 1.8 fusion.7
  160.5 3.5 %add_bitcast_fusion = f32[1024,768]{0,1:T(8,128)} fusion(f32[768,1024]{1,0:T(8,128)S(1)} %fusion.7, bf16[1024,1024]{1,0:T(8,128)(2,1)S(1)} %copy-done, f32[1024,768]{1,0:T(8,128)S(1)} %fusion.12), kind=kOutput, calls=%fused_computation.5 | convolution fusion | flops 1614544896 | bytes 11534336 | tf_op jit(solution)/shard_map/dot_general | solution.py:78
  164.0 3.5 %copy.15 = f32[1024,768]{1,0:T(8,128)} copy(f32[1024,768]{0,1:T(8,128)} %add_bitcast_fusion) | data formatting | bytes 6291456
  167.6 2.5 psum.7
  170.7 102.7 %reduce-scatter.4.cloned.1.call-done = f32[32,768]{1,0:T(8,128)} async-done(((f32[1024,768]{1,0:T(8,128)}), f32[32,768]{1,0:T(8,128)}) %reduce-scatter.4.cloned.1.call-update) | async-done | bytes 98320
  273.3 1.1 copy.16
  (32 shorter events, 5.9 us)
Async XLA Ops:
  7.2 17.3 %copy-start = (bf16[1024,1024]{1,0:T(8,128)(2,1)S(1)}, bf16[1024,1024]{1,0:T(8,128)(2,1)}, u32[]{:S(2)}) copy-start(bf16[1024,1024]{1,0:T(8,128)(2,1)} %param.9) | copy-start | bytes 6291460
  12.5 23.6 %all-to-all-start = ((f32[16,1,16]{2,1,0:T(1,128)}), f32[16,1,16]{2,1,0:T(1,128)S(1)}, u32[]{:S(2)}, u32[]{:S(2)}) async-start(f32[16,1,16]{2,1,0:T(1,128)} %all_to_all.12), calls=%async_computation | async-start | bytes 16384 | tf_op jit(solution)/shard_map/all_to_all | solution.py:48
  22.3 7.1 %copy-start.2 = (bf16[128,1024]{1,0:T(8,128)(2,1)S(1)}, bf16[128,1024]{1,0:T(8,128)(2,1)}, u32[]{:S(2)}) copy-start(bf16[128,1024]{1,0:T(8,128)(2,1)} %param.6) | copy-start | bytes 786436
  36.1 50.3 %all-to-all-start.1 = ((f32[16,16,2048]{2,1,0:T(8,128)}), f32[16,16,2048]{2,1,0:T(8,128)}, u32[]{:S(2)}, u32[]{:S(2)}) async-start(f32[16,16,2048]{2,1,0:T(8,128)} %bitcast.33), calls=%async_computation.1 | async-start | bytes 4194304 | tf_op jit(solution)/shard_map/all_to_all | solution.py:47
  99.6 52.9 %all-to-all-start.2 = ((f32[16,16,2048]{2,1,0:T(8,128)}), f32[16,16,2048]{2,1,0:T(8,128)}, u32[]{:S(2)}, u32[]{:S(2)}) async-start(f32[16,16,2048]{2,1,0:T(8,128)} %broadcast_select_fusion), calls=%async_computation.2 | async-start | bytes 4194304 | tf_op jit(solution)/shard_map/all_to_all | solution.py:62
  109.8 163.5 %reduce-scatter.4.cloned.1.call-start = ((), (), s32[]{:S(2)}) async-start(), calls=%async_computation.4 | async-start | bytes 3244032
  156.5 1.4 copy-start.1
Sparse Core Ops, SparseCore 0:
  167.7 105.5 reduce-scatter.3
where the time goes:
time: 283 us; the launch traced here: 282 us
  waiting for transfers between devices  188 us (66%)
  starting transfers between devices  25.7 us (9%)
  matrix products  18.6 us (7%)
  local copies, waits for them, and re-layouts  18.3 us (6%)
  between operations  14.2 us (5%)
  other arithmetic  12.5 us (4%)
  blocking collectives  4.6 us (2%)
    unnamed x2, waiting for transfers between devices  103 us
    all_to_all x1, waiting for transfers between devices, on_device(): lax.all_to_all(outgoing, 'dp', split_axis=0, concat_axis=0, tiled=True)  43 us
    all_to_all x1, waiting for transfers between devices, on_device(): lax.all_to_all(returned, 'dp', split_axis=0, concat_axis=0, tiled=True)  42.5 us
    all_to_all x1, starting transfers between devices, on_device(): lax.all_to_all(returned, 'dp', split_axis=0, concat_axis=0, tiled=True)  10.2 us
    all_to_all x1, starting transfers between devices, on_device(): lax.all_to_all(tags, 'dp', split_axis=0, concat_axis=0, tiled=True)  8.31 us
    all_to_all x1, starting transfers between devices, on_device(): lax.all_to_all(outgoing, 'dp', split_axis=0, concat_axis=0, tiled=True)  6.96 us
  transfers between devices with their start and end apart: 4, of which 3 were waited for; matrix products, arithmetic and copies ran while one was open for 5% of the time, Pallas kernels for 0%

commit v1 on v0

v1 whole, which is shorter than its diff:
```python
import functools
import math

import jax
import jax.numpy as jnp
from jax import lax
from jax.experimental import pallas as pl
from jax.experimental.pallas import tpu as pltpu
from jax.sharding import PartitionSpec as P

LANES = 128
TURN = 1.0 / (2.0 * math.pi)
ROUNDER = 1.5 * 2.0**23
SINE = (
    6.283185160088887,
    -41.34165503126523,
    81.60100406312206,
    -76.54978204660544,
    39.5367040910771,
)


def up_to(value, multiple):
    return -(-value // multiple) * multiple


def quarter_sine(turns):
    part = turns - ((turns + ROUNDER) - ROUNDER)
    angle = 0.25 - jnp.abs(part)
    square = angle * angle
    value = jnp.float32(SINE[4])
    for factor in SINE[3::-1]:
        value = value * square + factor
    return value * angle


def cos_sin(z):
    turns = z * TURN
    return quarter_sine(turns), quarter_sine(turns - 0.25)


def to_row(column, size):
    first = lax.broadcasted_iota(jnp.int32, (size, size), 0)
    second = lax.broadcasted_iota(jnp.int32, (size, size), 1)
    return jnp.sum(jnp.where(first == second, column, 0.0), axis=0, keepdims=True)


def to_column(row, size):
    first = lax.broadcasted_iota(jnp.int32, (size, size), 0)
    second = lax.broadcasted_iota(jnp.int32, (size, size), 1)
    return jnp.sum(jnp.where(first == second, row, 0.0), axis=1, keepdims=True)


def route_kernel(cls_dev, capacity, labels, table, teacher, student, out, rows):
    images = teacher.shape[0]
    slots, width = out.shape
    d_t, d_s = teacher.shape[1], student.shape[1]
    label = to_column(labels[...].astype(jnp.float32), images)
    lane = lax.broadcasted_iota(jnp.int32, (images, LANES), 1)
    lane_f = lane.astype(jnp.float32)
    label = jnp.broadcast_to(label, (images, LANES))
    found = jnp.zeros((images, LANES), jnp.float32)
    for chunk in range(table.shape[0]):
        entry = table[chunk : chunk + 1, :].astype(jnp.float32)
        found += jnp.where(lane_f + float(chunk * LANES) == label, entry, 0.0)
    position = jnp.sum(found, axis=1, keepdims=True)
    owner = jnp.floor((position + 0.5) * (1.0 / cls_dev))
    tag = position - owner * cls_dev + 1.0
    owner_row = to_row(owner, images)
    first = lax.broadcasted_iota(jnp.int32, (images, images), 0)
    second = lax.broadcasted_iota(jnp.int32, (images, images), 1)
    before = jnp.logical_and(first < second, owner == owner_row)
    rank = jnp.sum(jnp.where(before, 1.0, 0.0), axis=0, keepdims=True)
    slot = owner_row * float(capacity) + rank
    slot_id = lax.broadcasted_iota(jnp.int32, (slots, images), 0).astype(jnp.float32)
    pick = jnp.where(slot_id == slot, 1.0, 0.0).astype(jnp.bfloat16)
    high = jnp.floor(tag * (1.0 / 32.0))
    tags = jnp.where(lane == 0, high, jnp.where(lane == 1, tag - 32.0 * high, 0.0))
    rows[:, :d_t] = teacher[...]
    rows[:, d_t : d_t + d_s] = student[...]
    rows[:, d_t + d_s : d_t + d_s + LANES] = tags.astype(jnp.bfloat16)
    rows[:, d_t + d_s + LANES :] = jnp.zeros(
        (images, rows.shape[1] - d_t - d_s - LANES), jnp.bfloat16
    )
    start = pl.multiple_of(lax.axis_index("feat") * width, LANES)
    out[...] = jnp.dot(
        pick, rows[:, pl.ds(start, width)], preferred_element_type=jnp.float32
    ).astype(jnp.bfloat16)


def class_kernel(n_feat, n_dp, cls_pad, d_t, d_s, permuted, *refs):
    parts, heads = refs[:n_feat], refs[n_feat : 2 * n_feat]
    freqs, picked_rows = refs[2 * n_feat], refs[2 * n_feat + 1]
    grads, norms, student, rows, projected, grad_z, weight = refs[2 * n_feat + 2 :]
    feat = lax.axis_index("feat")
    slots, width = parts[0].shape
    half = freqs.shape[1]
    for offset in range(n_feat):
        index = lax.rem(feat + (n_feat - offset), n_feat)
        rows[:, pl.ds(pl.multiple_of(index * width, LANES), width)] = parts[offset][...]
    s_rows = rows[:, d_t : d_t + d_s]
    student[...] = s_rows
    part = d_t // n_feat
    for offset in range(n_feat):
        index = lax.rem(feat + (n_feat - offset), n_feat)
        projected[:, pl.ds(pl.multiple_of(index * part, LANES), part)] = jnp.dot(
            s_rows, heads[offset][...], preferred_element_type=jnp.float32
        ).astype(jnp.bfloat16)
    tags = rows[:, d_t + d_s : d_t + d_s + LANES].astype(jnp.float32)
    lane = lax.broadcasted_iota(jnp.int32, (slots, LANES), 1)
    tag = jnp.sum(
        tags * jnp.where(lane == 0, 32.0, jnp.where(lane == 1, 1.0, 0.0)), axis=1, keepdims=True
    )
    tag_row = to_row(tag, slots)
    same = jnp.where(jnp.logical_and(tag == tag_row, tag > 0.0), 1.0, 0.0)
    inverse = 1.0 / jnp.maximum(jnp.sum(same, axis=1, keepdims=True), 1.0)
    same = same.astype(jnp.bfloat16)
    step = min(half, 256)
    norm = jnp.zeros((slots, 1), jnp.float32)
    for column in range(0, half, step):
        block = slice(column, column + step)
        student_z = jnp.dot(
            projected[...], freqs[:, block], preferred_element_type=jnp.float32
        )
        teacher_z = jnp.dot(
            rows[:, :d_t], freqs[:, block], preferred_element_type=jnp.float32
        )
        cos_s, sin_s = cos_sin(student_z)
        cos_t, sin_t = cos_sin(teacher_z)
        mean_c = inverse * jnp.dot(
            same, (cos_s - cos_t).astype(jnp.bfloat16), preferred_element_type=jnp.float32
        )
        mean_s = inverse * jnp.dot(
            same, (sin_s - sin_t).astype(jnp.bfloat16), preferred_element_type=jnp.float32
        )
        norm += jnp.sum(mean_c * mean_c + mean_s * mean_s, axis=1, keepdims=True)
        grad_z[:, block] = (cos_s * mean_s - sin_s * mean_c).astype(jnp.bfloat16)
    cls = lax.broadcasted_iota(jnp.int32, (slots, cls_pad), 1).astype(jnp.float32) + 1.0
    norms[...] = jnp.sum(jnp.where(cls == tag, norm, 0.0), axis=0, keepdims=True)
    out_rows = d_t // (n_dp * n_feat)
    for offset in range(n_feat):
        index = lax.rem(feat + offset, n_feat)
        if permuted:
            source = picked_rows[index]
        else:
            for group in range(n_dp):
                start = pl.multiple_of((group * n_feat + index) * out_rows, out_rows)
                weight[group * out_rows : (group + 1) * out_rows, :] = freqs[
                    pl.ds(start, out_rows), :
                ]
            source = weight[...]
        grads[offset] = lax.dot_general(
            source, grad_z[...], (((1,), (1,)), ((), ())), preferred_element_type=jnp.float32
        ).astype(jnp.bfloat16)


def head_kernel(n_feat, divisor, *refs):
    grads, norms = refs[:n_feat], refs[n_feat : 2 * n_feat]
    student, head, loss = refs[2 * n_feat :]
    total, norm = grads[0][0].astype(jnp.float32), norms[0][...]
    for offset in range(1, n_feat):
        total += grads[offset][...].astype(jnp.float32)
        norm += norms[offset][...]
    head[...] = jnp.dot(
        total.astype(jnp.bfloat16), student[...], preferred_element_type=jnp.float32
    ).astype(jnp.bfloat16)
    loss[...] = (norm * (1.0 / divisor))[:, : loss.shape[1]]


def on_device(teacher, student, head, freqs, labels, class_slot):
    n_dp = lax.axis_size("dp")
    n_feat = lax.axis_size("feat")
    images, d_t = teacher.shape
    d_s = student.shape[1]
    half = freqs.shape[1]
    classes = class_slot.shape[0]
    cls_dev = classes // n_dp
    cls_pad = up_to(cls_dev, LANES)
    capacity = 2 * images // n_dp
    slots = n_dp * capacity
    width = up_to(d_t + d_s + LANES, LANES * n_feat) // n_feat
    out_rows = d_t // (n_dp * n_feat)
    permuted = out_rows % 16 != 0
    vmem = pltpu.CompilerParams(vmem_limit_bytes=32 * 2**20)

    def shifted(value, offset):
        return lax.ppermute(
            value, "feat", [(i, (i + offset) % n_feat) for i in range(n_feat)]
        )

    heads = [head] + [shifted(head, k) for k in range(1, n_feat)]
    table = jnp.pad(class_slot, (0, up_to(classes, 8 * LANES) - classes)).reshape(-1, LANES)
    sent = pl.pallas_call(
        functools.partial(route_kernel, cls_dev, capacity),
        out_shape=jax.ShapeDtypeStruct((slots, width), jnp.bfloat16),
        scratch_shapes=[pltpu.VMEM((images, width * n_feat), jnp.bfloat16)],
        compiler_params=vmem,
        name="route",
    )(labels.reshape(1, images), table, teacher, student)
    mine = lax.all_to_all(
        sent.reshape(n_dp, capacity, width), "dp", split_axis=0, concat_axis=0, tiled=True
    ).reshape(slots, width)
    parts = [mine] + [shifted(mine, k) for k in range(1, n_feat)]
    if permuted:
        picked = jnp.swapaxes(freqs.reshape(n_dp, n_feat, out_rows, half), 0, 1)
        picked = picked.reshape(n_feat, n_dp * out_rows, half)
    else:
        picked = jnp.zeros((8, LANES), jnp.bfloat16)
    grads, norms, s_rows = pl.pallas_call(
        functools.partial(class_kernel, n_feat, n_dp, cls_pad, d_t, d_s, permuted),
        out_shape=(
            jax.ShapeDtypeStruct((n_feat, n_dp * out_rows, slots), jnp.bfloat16),
            jax.ShapeDtypeStruct((1, cls_pad), jnp.float32),
            jax.ShapeDtypeStruct((slots, d_s), jnp.bfloat16),
        ),
        scratch_shapes=[
            pltpu.VMEM((slots, width * n_feat), jnp.bfloat16),
            pltpu.VMEM((slots, d_t), jnp.bfloat16),
            pltpu.VMEM((slots, half), jnp.bfloat16),
            pltpu.VMEM((n_dp * out_rows, half), jnp.bfloat16),
        ],
        compiler_params=vmem,
        name="classes",
    )(*parts, *heads, freqs, picked)
    all_grads = [grads] + [shifted(grads[k], k) for k in range(1, n_feat)]
    all_norms = [norms] + [shifted(norms, k) for k in range(1, n_feat)]
    partial_head, loss = pl.pallas_call(
        functools.partial(head_kernel, n_feat, 2.0 * half * n_feat),
        out_shape=(
            jax.ShapeDtypeStruct((n_dp * out_rows, d_s), jnp.bfloat16),
            jax.ShapeDtypeStruct((1, cls_dev), jnp.float32),
        ),
        compiler_params=vmem,
        name="head",
    )(*all_grads, *all_norms, s_rows)
    received = lax.all_to_all(
        partial_head.reshape(n_dp, out_rows, d_s), "dp", split_axis=0, concat_axis=0, tiled=True
    )
    scale = 1.0 / math.sqrt(images * n_dp)
    head_grad = jnp.sum(received.astype(jnp.float32), axis=0) * scale
    return (head_grad, loss.reshape(cls_dev))


def solution(mesh):
    in_specs = (P("dp", None), P("dp", None), P(None, "feat"), P(None, "feat"), P("dp"), P())
    out_specs = (P(("dp", "feat"), None), P("dp"))
    return jax.shard_map(
        on_device, mesh=mesh, in_specs=in_specs, out_specs=out_specs, check_vma=False
    )
```

time: 283 us -> 65.8 us (0.23)
  waiting for transfers between devices: 188 us -> 37.4 us
  matrix products: 18.6 us -> 0 us
  local copies, waits for them, and re-layouts: 18.3 us -> 4.58 us
  between operations: 14.2 us -> 0.69 us
  starting transfers between devices: 25.7 us -> 12.9 us
  other arithmetic: 12.5 us -> 1.36 us
  Pallas kernels: 0 us -> 8.45 us
  blocking collectives: 4.6 us -> 0 us
    unnamed x2 -> x0, waiting for transfers between devices: 103 us -> none
    all_to_all x3 -> x2, waiting for transfers between devices: 85.4 us -> 34.5 us  [the longest x1 19.4 us: on_device(): lax.all_to_all(partial_head.reshape(n_dp, out_rows, d_s), 'dp', split_axi...]
    dot_general x8 -> x0, matrix products: 18.6 us -> none  [the longest x1 4.9 us: on_device(): jnp.dot(lax.all_gather(projected, 'feat', axis=1, tiled=True), weight_row...]
    all_to_all x3 -> x2, starting transfers between devices: 25.5 us -> 12.2 us  [the longest x1 8.31 us: on_device(): lax.all_to_all(sent.reshape(n_dp, capacity, width), 'dp', split_axis=0, c...]
    gather x3 -> x0, local copies, waits for them, and re-layouts: 11.1 us -> none  [the longest x1 5.43 us: on_device(): jnp.take(means, jnp.maximum(tag_ids, 0), axis=0)]
    pallas_call x0 -> x3, Pallas kernels: none -> 8.45 us  [the longest x1 5.42 us: on_device(): pl.pallas_call(functools.partial(class_kernel, n_feat, n_dp, cls_pad, d_t...]
    select_n x4 -> x0, other arithmetic: 5.31 us -> none  [the longest x1 3.09 us: on_device(): jnp.take(means, jnp.maximum(tag_ids, 0), axis=0)]
    scatter x1 -> x0, other arithmetic: 3.39 us -> none  [on_device(): jnp.zeros((n_dp * capacity, 2 * half), jnp.float32).at[slot].set(delta)]
  transfers between devices with their start and end apart: 4 -> 6, of which waited for: 3 -> 4; matrix products, arithmetic and copies ran while one was open for 5% -> 1% of each run, Pallas kernels for 0% -> 0%
where the time goes in v1:
time: 65.8 us; the launch traced here: 65.3 us
  waiting for transfers between devices  37.4 us (57%)
  starting transfers between devices  12.9 us (20%)
  Pallas kernels  8.45 us (13%)
  local copies, waits for them, and re-layouts  4.58 us (7%)
  other arithmetic  1.36 us (2%)
  between operations  0.69 us (1%)
    all_to_all x1, waiting for transfers between devices, on_device(): lax.all_to_all(partial_head.reshape(n_dp, out_rows, d_s), 'dp', split_axi...  19.4 us
    all_to_all x1, waiting for transfers between devices, on_device(): lax.all_to_all(sent.reshape(n_dp, capacity, width), 'dp', split_axis=0, c...  15.1 us
    all_to_all x1, starting transfers between devices, on_device(): lax.all_to_all(sent.reshape(n_dp, capacity, width), 'dp', split_axis=0, c...  8.31 us
    pallas_call x1, Pallas kernels, on_device(): pl.pallas_call(functools.partial(class_kernel, n_feat, n_dp, cls_pad, d_t...  5.42 us
    all_to_all x1, starting transfers between devices, on_device(): lax.all_to_all(partial_head.reshape(n_dp, out_rows, d_s), 'dp', split_axi...  3.89 us
    unnamed x10, local copies, waits for them, and re-layouts  3.67 us
    ppermute x4, waiting for transfers between devices, shifted(): lax.ppermute(value, 'feat', [(i, (i + offset) % n_feat) for i in range(n_...  2.93 us
    pallas_call x1, Pallas kernels, on_device(): pl.pallas_call(functools.partial(route_kernel, cls_dev, capacity), out_sh...  1.77 us
  transfers between devices with their start and end apart: 6, of which 4 were waited for; matrix products, arithmetic and copies ran while one was open for 1% of the time, Pallas kernels for 0%

profile of v1, /device:TPU:0, one launch (start us, length us, event | category | flops | bytes accessed | tf_op | source)
XLA Modules:
  0.0 65.3 jit_solution(7726825326921540152)
XLA Ops:
  0.6 0.9 %pad_bitcast_fusion.table = s32[48,128]{1,0:T(8,128)S(1)} fusion(s32[5456]{0:T(1024)} %param.11), kind=kLoop, calls=%fused_computation.3 | loop fusion | bytes 46400 | tf_op jit(solution)/shard_map/reshape | solution.py:192
  1.5 0.9 %copy-done.2 = bf16[128,1024]{1,0:T(8,128)(2,1)S(1)} copy-done((bf16[128,1024]{1,0:T(8,128)(2,1)S(1)}, bf16[128,1024]{1,0:T(8,128)(2,1)}, u32[]{:S(2)}) %copy-start.2) | copy-done | bytes 262168
  2.5 0.9 %copy-done.3 = bf16[128,768]{1,0:T(8,128)(2,1)S(1)} copy-done((bf16[128,768]{1,0:T(8,128)(2,1)S(1)}, bf16[128,768]{1,0:T(8,128)(2,1)}, u32[]{:S(2)}) %copy-start.3) | copy-done | bytes 196632
  3.4 0.7 copy-done.4
  4.1 1.8 %route.1 = bf16[256,1024]{1,0:T(8,128)(2,1)} custom-call(s32[1,128]{1,0:T(1,128)S(1)} %bitcast.10, s32[48,128]{1,0:T(8,128)S(1)} %pad_bitcast_fusion.table, bf16[128,1024]{1,0:T(8,128)(2,1)S(1)} %copy-done.2, bf16[128,768]{1,0:T(8,128)(2,1)S(1)} %copy-done.3), custom_call_target="tpu_custom_call" | custom-call | tf_op jit(solution)/shard_map/route/pallas_call | solution.py:193
  5.8 8.3 %all-to-all-start = ((bf16[16,16,1024]{2,1,0:T(8,128)(2,1)}), bf16[16,16,1024]{2,1,0:T(8,128)(2,1)S(1)}, u32[]{:S(2)}, u32[]{:S(2)}) async-start(bf16[16,16,1024]{2,1,0:T(8,128)(2,1)} %bitcast.2), calls=%async_computation | async-start | bytes 1048576 | tf_op jit(solution)/shard_map/all_to_all | solution.py:200
  14.2 0.1 collective-permute-start.1
  14.2 15.1 %all-to-all-done = bf16[16,16,1024]{2,1,0:T(8,128)(2,1)S(1)} async-done(((bf16[16,16,1024]{2,1,0:T(8,128)(2,1)}), bf16[16,16,1024]{2,1,0:T(8,128)(2,1)S(1)}, u32[]{:S(2)}, u32[]{:S(2)}) %all-to-all-start) | async-done | bytes 524320 | tf_op jit(solution)/shard_map/all_to_all | solution.py:200
  29.3 0.0 collective-permute-start
  29.3 0.0 collective-permute-done.1.refs_3_
  29.3 1.9 %collective-permute-done.refs_1_ = bf16[256,1024]{1,0:T(8,128)(2,1)S(1)} collective-permute-done((bf16[256,1024]{1,0:T(8,128)(2,1)S(1)}, bf16[256,1024]{1,0:T(8,128)(2,1)S(1)}, u32[]{:S(2)}, u32[]{:S(2)}) %collective-permute-start) | collective-permute-done | bytes 524320 | tf_op jit(solution)/shard_map/ppermute | solution.py:187
  31.2 0.0 copy-done
  31.2 1.1 %copy-done.1 = bf16[768,512]{1,0:T(8,128)(2,1)S(1)} copy-done((bf16[768,512]{1,0:T(8,128)(2,1)S(1)}, bf16[768,512]{1,0:T(8,128)(2,1)}, u32[]{:S(2)}) %copy-start.1) | copy-done | bytes 786456
  32.3 5.4 %classes.1 = (bf16[2,512,256]{2,1,0:T(8,128)(2,1)S(1)}, f32[1,384]{1,0:T(1,128)S(1)}, bf16[256,768]{1,0:T(8,128)(2,1)S(1)}) custom-call(bf16[256,1024]{1,0:T(8,128)(2,1)S(1)} %bitcast.9, bf16[256,1024]{1,0:T(8,128)(2,1)S(1)} %collective-permute-done.refs_1_, bf16[768,512]{1,0:T(8,128)(2,1)S(1)} %copy-done.1, ...), custom_call_target="tpu_custom_call" | custom-call | tf_op jit(solution)/shard_map/classes/pallas_call | solution.py:209
  37.8 0.2 collective-permute-start.2
  38.0 0.4 collective-permute-start.3
  38.4 1.0 %collective-permute-done.3.refs_3_ = f32[1,384]{1,0:T(1,128)S(1)} collective-permute-done((f32[1,384]{1,0:T(1,128)S(1)}, f32[1,384]{1,0:T(1,128)S(1)}, u32[]{:S(2)}, u32[]{:S(2)}) %collective-permute-start.3) | collective-permute-done | bytes 1568 | tf_op jit(solution)/shard_map/ppermute | solution.py:187
  39.4 0.0 collective-permute-done.2.refs_1_
  39.4 1.3 %head.1 = (bf16[512,768]{1,0:T(8,128)(2,1)}, f32[1,341]{1,0:T(1,128)S(1)}) custom-call(bf16[2,512,256]{2,1,0:T(8,128)(2,1)S(1)} %get-tuple-element.7.refs_0_, bf16[512,256]{1,0:T(8,128)(2,1)S(1)} %collective-permute-done.2.refs_1_, f32[1,384]{1,0:T(1,128)S(1)} %get-tuple-element.8.refs_2_, f32[1,384]{1,0:T(1,128)S(1)} %collective-permute-done.3.refs_3_, ...), custom_call_target="tpu_custom_call" | custom-call | tf_op jit(solution)/shard_map/head/pallas_call | solution.py:227
  40.7 3.9 %all-to-all-start.1 = ((bf16[16,32,768]{2,1,0:T(8,128)(2,1)}), bf16[16,32,768]{2,1,0:T(8,128)(2,1)S(1)}, u32[]{:S(2)}, u32[]{:S(2)}) async-start(bf16[16,32,768]{2,1,0:T(8,128)(2,1)} %bitcast.5), calls=%async_computation.1 | async-start | bytes 1572864 | tf_op jit(solution)/shard_map/all_to_all | solution.py:236
  44.6 0.6 reduce
  45.2 19.4 %all-to-all-done.1 = bf16[16,32,768]{2,1,0:T(8,128)(2,1)S(1)} async-done(((bf16[16,32,768]{2,1,0:T(8,128)(2,1)}), bf16[16,32,768]{2,1,0:T(8,128)(2,1)S(1)}, u32[]{:S(2)}, u32[]{:S(2)}) %all-to-all-start.1) | async-done | bytes 786464 | tf_op jit(solution)/shard_map/all_to_all | solution.py:236
  64.6 0.1 convert_reduce_fusion
  64.7 0.7 broadcast_multiply_fusion
  (7 shorter events, 0.0 us)
Async XLA Ops:
  0.6 30.6 %copy-start = (bf16[1024,1024]{1,0:T(8,128)(2,1)S(1)}, bf16[1024,1024]{1,0:T(8,128)(2,1)}, u32[]{:S(2)}) copy-start(bf16[1024,1024]{1,0:T(8,128)(2,1)} %refs_4_.1) | copy-start | bytes 6291460
  1.5 0.9 %copy-start.2 = (bf16[128,1024]{1,0:T(8,128)(2,1)S(1)}, bf16[128,1024]{1,0:T(8,128)(2,1)}, u32[]{:S(2)}) copy-start(bf16[128,1024]{1,0:T(8,128)(2,1)} %teacher.1) | copy-start | bytes 786436
  2.5 0.9 %copy-start.3 = (bf16[128,768]{1,0:T(8,128)(2,1)S(1)}, bf16[128,768]{1,0:T(8,128)(2,1)}, u32[]{:S(2)}) copy-start(bf16[128,768]{1,0:T(8,128)(2,1)} %student.1) | copy-start | bytes 589828
  3.4 0.7 %copy-start.4 = (s32[128]{0:T(128)S(1)}, s32[128]{0:T(128)}, u32[]{:S(2)}) copy-start(s32[128]{0:T(128)} %param.10) | copy-start | bytes 1540
  5.8 23.5 %all-to-all-start = ((bf16[16,16,1024]{2,1,0:T(8,128)(2,1)}), bf16[16,16,1024]{2,1,0:T(8,128)(2,1)S(1)}, u32[]{:S(2)}, u32[]{:S(2)}) async-start(bf16[16,16,1024]{2,1,0:T(8,128)(2,1)} %bitcast.2), calls=%async_computation | async-start | bytes 1048576 | tf_op jit(solution)/shard_map/all_to_all | solution.py:200
  14.2 15.1 %collective-permute-start.1 = (bf16[768,512]{1,0:T(8,128)(2,1)}, bf16[768,512]{1,0:T(8,128)(2,1)S(1)}, u32[]{:S(2)}, u32[]{:S(2)}) collective-permute-start(bf16[768,512]{1,0:T(8,128)(2,1)} %refs_2_.1), channel_id=1, source_target_pairs={{0,1},{1,0},{2,3},{3,2},{4,5},{5,4},{6,7},{7,6},{8,9},{9,8},{10,11... | collective-permute-start | bytes 2359304 | tf_op jit(solution)/shard_map/ppermute | solution.py:187
  29.3 1.9 %collective-permute-start = (bf16[256,1024]{1,0:T(8,128)(2,1)S(1)}, bf16[256,1024]{1,0:T(8,128)(2,1)S(1)}, u32[]{:S(2)}, u32[]{:S(2)}) collective-permute-start(bf16[256,1024]{1,0:T(8,128)(2,1)S(1)} %bitcast.8), channel_id=1, source_target_pairs={{0,1},{1,0},{2,3},{3,2},{4,5},{5,4},{6,7},{7,6},{8,9},{9,8},{10,11... | collective-permute-start | bytes 1572872 | tf_op jit(solution)/shard_map/ppermute | solution.py:187
  31.2 1.1 %copy-start.1 = (bf16[768,512]{1,0:T(8,128)(2,1)S(1)}, bf16[768,512]{1,0:T(8,128)(2,1)}, u32[]{:S(2)}) copy-start(bf16[768,512]{1,0:T(8,128)(2,1)} %refs_2_.1) | copy-start | bytes 2359300
  37.8 1.6 %collective-permute-start.2 = (bf16[512,256]{1,0:T(8,128)(2,1)S(1)}, bf16[512,256]{1,0:T(8,128)(2,1)S(1)}, u32[]{:S(2)}, u32[]{:S(2)}) collective-permute-start(bf16[512,256]{1,0:T(8,128)(2,1)S(1)} %slice_bitcast_fusion), channel_id=1, source_target_pairs={{0,1},{1,0},{2,3},{3,2},{4,5},{5,4},{6,7},{7,6},{8,9},{9,8},{10,11... | collective-permute-start | bytes 786440 | tf_op jit(solution)/shard_map/ppermute | solution.py:187
  38.0 1.4 %collective-permute-start.3 = (f32[1,384]{1,0:T(1,128)S(1)}, f32[1,384]{1,0:T(1,128)S(1)}, u32[]{:S(2)}, u32[]{:S(2)}) collective-permute-start(f32[1,384]{1,0:T(1,128)S(1)} %get-tuple-element.8.refs_2_), channel_id=1, source_target_pairs={{0,1},{1,0},{2,3},{3,2},{4,5},{5,4},{6,7},{7,6},{8,9},{9,8},{10,11... | collective-permute-start | bytes 4616 | tf_op jit(solution)/shard_map/ppermute | solution.py:187
  40.7 23.9 %all-to-all-start.1 = ((bf16[16,32,768]{2,1,0:T(8,128)(2,1)}), bf16[16,32,768]{2,1,0:T(8,128)(2,1)S(1)}, u32[]{:S(2)}, u32[]{:S(2)}) async-start(bf16[16,32,768]{2,1,0:T(8,128)(2,1)} %bitcast.5), calls=%async_computation.1 | async-start | bytes 1572864 | tf_op jit(solution)/shard_map/all_to_all | solution.py:236

commit v2 on v1

v2 whole, which is shorter than its diff:
```python
import functools
import math

import jax
import jax.numpy as jnp
from jax import lax
from jax.experimental import pallas as pl
from jax.experimental.pallas import tpu as pltpu
from jax.sharding import PartitionSpec as P

LANES = 128
TURN = 1.0 / (2.0 * math.pi)
ROUNDER = 1.5 * 2.0**23
SINE = (6.283164044217864, -41.337142357601536, 81.3407683703199, -70.9934277613874)


def up_to(value, multiple):
    return -(-value // multiple) * multiple


def quarter_sine(angle):
    square = angle * angle
    value = jnp.float32(SINE[-1])
    for factor in SINE[-2::-1]:
        value = value * square + factor
    return value * angle


def cos_sin(z):
    turns = z * TURN
    part = turns - ((turns + ROUNDER) - ROUNDER)
    wave = jnp.minimum(jnp.maximum(part, -0.5 - part), 0.5 - part)
    return quarter_sine(0.25 - jnp.abs(part)), quarter_sine(wave)


def to_row(column, size):
    first = lax.broadcasted_iota(jnp.int32, (size, size), 0)
    second = lax.broadcasted_iota(jnp.int32, (size, size), 1)
    return jnp.sum(jnp.where(first == second, column, 0.0), axis=0, keepdims=True)


def to_column(row, size):
    first = lax.broadcasted_iota(jnp.int32, (size, size), 0)
    second = lax.broadcasted_iota(jnp.int32, (size, size), 1)
    return jnp.sum(jnp.where(first == second, row, 0.0), axis=1, keepdims=True)


def table_entries(table, chunk):
    start = chunk * LANES
    size = min(LANES, table.shape[0] - start)
    entries = table[pl.ds(start, size)].astype(jnp.float32)
    if size < LANES:
        entries = jnp.concatenate([entries, jnp.zeros((LANES - size,), jnp.float32)])
    return entries.reshape(1, LANES)


def route_kernel(
    cls_dev, capacity, labels_in, table_in, teacher, student, out, token, labels, table, rows, sems
):
    images, d_t = teacher.shape
    d_s = student.shape[1]
    slots, width = out.shape
    copies = [
        pltpu.make_async_copy(labels_in, labels, sems.at[0]),
        pltpu.make_async_copy(table_in, table, sems.at[1]),
        pltpu.make_async_copy(teacher, rows.at[:, :d_t], sems.at[2]),
        pltpu.make_async_copy(student, rows.at[:, d_t : d_t + d_s], sems.at[3]),
    ]
    for copy in copies:
        copy.start()
    lane = lax.broadcasted_iota(jnp.int32, (images, LANES), 1)
    lane_f = lane.astype(jnp.float32)
    copies[0].wait()
    label = to_column(labels[...].astype(jnp.float32).reshape(1, images), images)
    label = jnp.broadcast_to(label, (images, LANES))
    copies[1].wait()
    found = jnp.zeros((images, LANES), jnp.float32)
    for chunk in range(pl.cdiv(table.shape[0], LANES)):
        entries = table_entries(table, chunk)
        found += jnp.where(lane_f + float(chunk * LANES) == label, entries, 0.0)
    position = jnp.sum(found, axis=1, keepdims=True)
    owner = jnp.floor((position + 0.5) * (1.0 / cls_dev))
    tag = position - owner * cls_dev + 1.0
    owner_row = to_row(owner, images)
    first = lax.broadcasted_iota(jnp.int32, (images, images), 0)
    second = lax.broadcasted_iota(jnp.int32, (images, images), 1)
    before = jnp.logical_and(first < second, owner == owner_row)
    rank = jnp.sum(jnp.where(before, 1.0, 0.0), axis=0, keepdims=True)
    slot = owner_row * float(capacity) + rank
    slot_id = lax.broadcasted_iota(jnp.int32, (slots, images), 0).astype(jnp.float32)
    pick = jnp.where(slot_id == slot, 1.0, 0.0).astype(jnp.bfloat16)
    high = jnp.floor(tag * (1.0 / 32.0))
    tags = jnp.where(lane == 0, high, jnp.where(lane == 1, tag - 32.0 * high, 0.0))
    rows[:, d_t + d_s : d_t + d_s + LANES] = tags.astype(jnp.bfloat16)
    rows[:, d_t + d_s + LANES :] = jnp.zeros(
        (images, rows.shape[1] - d_t - d_s - LANES), jnp.bfloat16
    )
    token[...] = jnp.zeros_like(token)
    copies[2].wait()
    copies[3].wait()
    start = pl.multiple_of(lax.axis_index("feat") * width, LANES)
    out[...] = jnp.dot(
        pick, rows[:, pl.ds(start, width)], preferred_element_type=jnp.float32
    ).astype(jnp.bfloat16)


def load_kernel(head_in, freqs_in, _, head, freqs, sems):
    copies = [
        pltpu.make_async_copy(head_in, head, sems.at[0]),
        pltpu.make_async_copy(freqs_in, freqs, sems.at[1]),
    ]
    for copy in copies:
        copy.start()
    for copy in copies:
        copy.wait()


def class_kernel(n_feat, n_dp, pair, cls_pad, d_t, d_s, permuted, *refs):
    parts, heads, refs = refs[:n_feat], refs[n_feat : 2 * n_feat], refs[2 * n_feat :]
    freqs, refs = refs[0], refs[1:]
    if permuted:
        weights, refs = refs[0], refs[1:]
    grads, refs = refs[:n_feat], refs[n_feat:]
    norms, student, rows, projected, grad_z, picked, near, sems = refs
    feat = lax.axis_index("feat")
    side = lax.rem(lax.axis_index("dp"), pair)
    copies = [
        pltpu.make_async_copy(heads[k], near.at[k - 1], sems.at[k - 1]) for k in range(1, n_feat)
    ]
    for copy in copies:
        copy.start()
    slots, width = parts[0].shape
    half = freqs.shape[1]
    for offset in range(n_feat):
        index = lax.rem(feat + (n_feat - offset), n_feat)
        rows[:, pl.ds(pl.multiple_of(index * width, LANES), width)] = parts[offset][...]
    s_rows = rows[:, d_t : d_t + d_s]
    student[...] = s_rows
    tags = rows[:, d_t + d_s : d_t + d_s + LANES].astype(jnp.float32)
    lane = lax.broadcasted_iota(jnp.int32, (slots, LANES), 1)
    tag = jnp.sum(
        tags * jnp.where(lane == 0, 32.0, jnp.where(lane == 1, 1.0, 0.0)), axis=1, keepdims=True
    )
    tag_row = to_row(tag, slots)
    same = jnp.where(jnp.logical_and(tag == tag_row, tag > 0.0), 1.0, 0.0)
    inverse = 1.0 / jnp.maximum(jnp.sum(same, axis=1, keepdims=True), 1.0)
    same = same.astype(jnp.bfloat16)
    part = d_t // n_feat
    for offset in range(n_feat):
        if offset:
            copies[offset - 1].wait()
        weight = near[offset - 1] if offset else heads[0][...]
        index = lax.rem(feat + (n_feat - offset), n_feat)
        projected[:, pl.ds(pl.multiple_of(index * part, LANES), part)] = jnp.dot(
            s_rows, weight, preferred_element_type=jnp.float32
        ).astype(jnp.bfloat16)
    step = min(half, 256)
    norm = jnp.zeros((slots, 1), jnp.float32)
    for column in range(0, half, step):
        block = slice(column, column + step)
        student_z = jnp.dot(
            projected[...], freqs[:, block], preferred_element_type=jnp.float32
        )
        teacher_z = jnp.dot(
            rows[:, :d_t], freqs[:, block], preferred_element_type=jnp.float32
        )
        cos_s, sin_s = cos_sin(student_z)
        cos_t, sin_t = cos_sin(teacher_z)
        mean_c = inverse * jnp.dot(
            same, (cos_s - cos_t).astype(jnp.bfloat16), preferred_element_type=jnp.float32
        )
        mean_s = inverse * jnp.dot(
            same, (sin_s - sin_t).astype(jnp.bfloat16), preferred_element_type=jnp.float32
        )
        norm += jnp.sum(mean_c * mean_c + mean_s * mean_s, axis=1, keepdims=True)
        grad_z[:, block] = (cos_s * mean_s - sin_s * mean_c).astype(jnp.bfloat16)
    cls = lax.broadcasted_iota(jnp.int32, (slots, cls_pad), 1).astype(jnp.float32) + 1.0
    norms[...] = jnp.sum(jnp.where(cls == tag, norm, 0.0), axis=0, keepdims=True)
    out_rows = d_t // (n_dp * n_feat)
    block = n_dp // pair * out_rows
    for offset in range(n_feat):
        for across in range(pair):
            index = lax.rem(side + across, pair) * n_feat + lax.rem(feat + offset, n_feat)
            target = slice(across * block, (across + 1) * block)
            if permuted:
                picked[target, :] = weights[index]
            else:
                for group in range(n_dp // pair):
                    start = pl.multiple_of((group * pair * n_feat + index) * out_rows, out_rows)
                    first = across * block + group * out_rows
                    picked[first : first + out_rows, :] = freqs[pl.ds(start, out_rows), :]
        out = grads[offset]
        out[...] = lax.dot_general(
            picked[...], grad_z[...], (((1,), (1,)), ((), ())), preferred_element_type=jnp.float32
        ).astype(out.dtype)


def summed(refs, start, size):
    total = refs[0][start : start + size, :].astype(jnp.float32)
    for ref in refs[1:]:
        total += ref[start : start + size, :].astype(jnp.float32)
    return total.astype(jnp.bfloat16)


def fold_kernel(*refs):
    size = refs[-1].shape[0]
    refs[-1][...] = summed(refs[:-1], size, size)


def own_kernel(n_feat, scale, divisor, d_t, d_s, *refs):
    grads, norms, student = refs[:n_feat], refs[n_feat : 2 * n_feat], refs[2 * n_feat]
    parts, refs = refs[2 * n_feat + 1 : -4], refs[-4:]
    head, loss, partner, rows = refs
    feat = lax.axis_index("feat")
    head[...] = scale * jnp.dot(
        summed(grads, 0, head.shape[0]), student[...], preferred_element_type=jnp.float32
    )
    norm = norms[0][...]
    for offset in range(1, n_feat):
        norm += norms[offset][...]
    loss[...] = (norm * (1.0 / divisor))[0, : loss.shape[0]]
    for offset, part in enumerate(parts):
        width = part.shape[1]
        index = lax.rem(feat + (n_feat - offset), n_feat)
        rows[:, pl.ds(pl.multiple_of(index * width, LANES), width)] = part[...]
    if parts:
        partner[...] = rows[:, d_t : d_t + d_s]


def head_kernel(scale, own, grads, partner, head):
    product = jnp.dot(grads[...], partner[...], preferred_element_type=jnp.float32)
    head[...] = (own[...] + product * scale).astype(jnp.bfloat16)


def on_device(teacher, student, head, freqs, labels, class_slot):
    n_dp = lax.axis_size("dp")
    n_feat = lax.axis_size("feat")
    images, d_t = teacher.shape
    d_s = student.shape[1]
    half = freqs.shape[1]
    classes = class_slot.shape[0]
    cls_dev = classes // n_dp
    cls_pad = up_to(cls_dev, LANES)
    capacity = 2 * images // n_dp
    slots = n_dp * capacity
    width = up_to(d_t + d_s + LANES, LANES * n_feat) // n_feat
    out_rows = d_t // (n_dp * n_feat)
    pair = 2 if n_dp % 2 == 0 else 1
    groups = n_dp // pair
    vmem = pltpu.CompilerParams(vmem_limit_bytes=20 * 2**20)
    hbm = pl.BlockSpec(memory_space=pltpu.HBM)
    near = pl.BlockSpec(memory_space=pltpu.VMEM)

    def moved(value, across, offset, feats=None):
        moves = [
            (d * n_feat + f, (d ^ across) * n_feat + (f + offset) % n_feat)
            for d in range(n_dp)
            for f in (range(n_feat) if feats is None else feats)
        ]
        return lax.ppermute(value, ("dp", "feat"), moves)

    def all_parts(value):
        return [value] + [moved(value, 0, k) for k in range(1, n_feat)]

    sent, token = pl.pallas_call(
        functools.partial(route_kernel, cls_dev, capacity),
        out_shape=(
            jax.ShapeDtypeStruct((slots, width), jnp.bfloat16),
            jax.ShapeDtypeStruct((8, LANES), jnp.float32),
        ),
        in_specs=[hbm] * 4,
        scratch_shapes=[
            pltpu.VMEM((images,), jnp.int32),
            pltpu.VMEM((classes,), jnp.int32),
            pltpu.VMEM((images, width * n_feat), jnp.bfloat16),
            pltpu.SemaphoreType.DMA((4,)),
        ],
        compiler_params=pltpu.CompilerParams(vmem_limit_bytes=60 * 2**20),
        name="route",
    )(labels, class_slot, teacher, student)
    permuted = out_rows % 16 != 0
    weights = []
    if permuted:
        weights = jnp.swapaxes(freqs.reshape(groups, pair * n_feat, out_rows, half), 0, 1)
        weights = [weights.reshape(pair * n_feat, groups * out_rows, half)]
    head_near, freqs_near = pl.pallas_call(
        load_kernel,
        out_shape=(
            jax.ShapeDtypeStruct(head.shape, jnp.bfloat16),
            jax.ShapeDtypeStruct(freqs.shape, jnp.bfloat16),
        ),
        in_specs=[hbm] * 3,
        scratch_shapes=[pltpu.SemaphoreType.DMA((2,))],
        compiler_params=vmem,
        name="load",
    )(head, freqs, token)
    heads = all_parts(head_near)
    mine = lax.all_to_all(
        sent.reshape(n_dp, capacity, width), "dp", split_axis=0, concat_axis=0, tiled=True
    ).reshape(slots, width)
    parts = all_parts(mine)
    block = groups * out_rows
    *grads, norms, s_rows = pl.pallas_call(
        functools.partial(class_kernel, n_feat, n_dp, pair, cls_pad, d_t, d_s, permuted),
        out_shape=tuple(
            jax.ShapeDtypeStruct((pair * block, slots), jnp.bfloat16 if k else jnp.float32)
            for k in range(n_feat)
        )
        + (
            jax.ShapeDtypeStruct((1, cls_pad), jnp.float32),
            jax.ShapeDtypeStruct((slots, d_s), jnp.bfloat16),
        ),
        scratch_shapes=[
            pltpu.VMEM((slots, width * n_feat), jnp.bfloat16),
            pltpu.VMEM((slots, d_t), jnp.bfloat16),
            pltpu.VMEM((slots, half), jnp.bfloat16),
            pltpu.VMEM((pair * block, half), jnp.bfloat16),
            pltpu.VMEM((n_feat - 1, *head.shape), jnp.bfloat16),
            pltpu.SemaphoreType.DMA((n_feat - 1,)),
        ],
        in_specs=[near] * (n_feat + 1) + [hbm] * (n_feat - 1) + [near] * (1 + len(weights)),
        compiler_params=vmem,
        name="classes",
    )(*parts, *heads, freqs_near, *weights)
    partner = []
    if pair > 1:
        holders = [
            f for f in range(n_feat) if f * width < d_t + d_s and (f + 1) * width > d_t
        ]
        across = moved(mine, 1, 0, holders)
    all_grads = [grads[0]] + [moved(grads[k], 0, k) for k in range(1, n_feat)]
    all_norms = all_parts(norms)
    if pair > 1:
        all_grads, all_norms, across = lax.optimization_barrier((all_grads, all_norms, across))
        partner = all_parts(across)
    scale = 1.0 / math.sqrt(images * n_dp)
    own, loss, partner_rows = pl.pallas_call(
        functools.partial(own_kernel, n_feat, scale, 2.0 * half * n_feat, d_t, d_s),
        out_shape=(
            jax.ShapeDtypeStruct((block, d_s), jnp.float32),
            jax.ShapeDtypeStruct((cls_dev,), jnp.float32),
            jax.ShapeDtypeStruct((slots, d_s), jnp.bfloat16),
        ),
        scratch_shapes=[pltpu.VMEM((slots, width * n_feat), jnp.bfloat16)],
        compiler_params=vmem,
        name="own",
    )(*all_grads, *all_norms, s_rows, *partner)
    if pair > 1:
        folded = pl.pallas_call(
            fold_kernel,
            out_shape=jax.ShapeDtypeStruct((block, slots), jnp.bfloat16),
            compiler_params=vmem,
            name="fold",
        )(*all_grads)
        partial_head = pl.pallas_call(
            functools.partial(head_kernel, scale),
            out_shape=jax.ShapeDtypeStruct((block, d_s), jnp.bfloat16),
            compiler_params=vmem,
            name="head",
        )(own, moved(folded, 1, 0), partner_rows)
    else:
        partial_head = own.astype(jnp.bfloat16)
    received = lax.all_to_all(
        partial_head.reshape(groups, out_rows, d_s),
        "dp",
        split_axis=0,
        concat_axis=0,
        tiled=True,
        axis_index_groups=[list(range(p, n_dp, pair)) for p in range(pair)],
    )
    head_grad = jnp.sum(received.astype(jnp.float32), axis=0)
    return (head_grad, loss)


def solution(mesh):
    in_specs = (P("dp", None), P("dp", None), P(None, "feat"), P(None, "feat"), P("dp"), P())
    out_specs = (P(("dp", "feat"), None), P("dp"))
    return jax.shard_map(
        on_device, mesh=mesh, in_specs=in_specs, out_specs=out_specs, check_vma=False
    )
```

time: 65.8 us -> 58.8 us (0.89)
  waiting for transfers between devices: 37.4 us -> 17.3 us
  blocking collectives: 0 us -> 15 us
  local copies, waits for them, and re-layouts: 4.58 us -> 3.41 us
  Pallas kernels: 8.45 us -> 9.35 us
  starting transfers between devices: 12.9 us -> 12 us
  other arithmetic: 1.36 us -> 0.69 us
    all_to_all x1 -> x0, waiting for transfers between devices: 19.4 us -> none  [on_device(): lax.all_to_all(partial_head.reshape(n_dp, out_rows, d_s), 'dp', split_axi...]
    all_to_all x0 -> x1, blocking collectives: none -> 15 us  [on_device(): lax.all_to_all(partial_head.reshape(groups, out_rows, d_s), 'dp', split_a...]
    all_to_all x1 -> x0, starting transfers between devices: 3.89 us -> none  [on_device(): lax.all_to_all(partial_head.reshape(n_dp, out_rows, d_s), 'dp', split_axi...]
    all_to_all x1, waiting for transfers between devices: 15.1 us -> 11.4 us  [on_device(): lax.all_to_all(sent.reshape(n_dp, capacity, width), 'dp', split_axis=0, c...]
    ppermute x4 -> x7, starting transfers between devices: 0.65 us -> 3.62 us  [moved(): return lax.ppermute(value, ('dp', 'feat'), moves)]
    ppermute x4 -> x7, waiting for transfers between devices: 2.93 us -> 5.88 us  [moved(): return lax.ppermute(value, ('dp', 'feat'), moves)]
    reshape x1 -> x0, local copies, waits for them, and re-layouts: 0.89 us -> none  [on_device(): jnp.pad(class_slot, (0, up_to(classes, 8 * LANES) - classes))]
    pallas_call x2 -> x5, Pallas kernels: 6.68 us -> 6.96 us  [the longest x1 5.69 us: on_device(): pl.pallas_call(functools.partial(class_kernel, n_feat, n_dp, pair, cls_pa...]
  transfers between devices with their start and end apart: 6 -> 8, of which waited for: 4 -> 5; matrix products, arithmetic and copies ran while one was open for 1% -> 0% of each run, Pallas kernels for 0% -> 11%
where the time goes in v2:
time: 58.8 us; the launch traced here: 58.4 us
  waiting for transfers between devices  17.3 us (29%)
  blocking collectives  15 us (26%)
  starting transfers between devices  12 us (20%)
  Pallas kernels  9.35 us (16%)
  local copies, waits for them, and re-layouts  3.41 us (6%)
  between operations  0.71 us (1%)
  other arithmetic  0.69 us (1%)
    all_to_all x1, blocking collectives, on_device(): lax.all_to_all(partial_head.reshape(groups, out_rows, d_s), 'dp', split_a...  15 us
    all_to_all x1, waiting for transfers between devices, on_device(): lax.all_to_all(sent.reshape(n_dp, capacity, width), 'dp', split_axis=0, c...  11.4 us
    all_to_all x1, starting transfers between devices, on_device(): lax.all_to_all(sent.reshape(n_dp, capacity, width), 'dp', split_axis=0, c...  8.33 us
    ppermute x7, waiting for transfers between devices, moved(): return lax.ppermute(value, ('dp', 'feat'), moves)  5.88 us
    pallas_call x1, Pallas kernels, on_device(): pl.pallas_call(functools.partial(class_kernel, n_feat, n_dp, pair, cls_pa...  5.69 us
    ppermute x7, starting transfers between devices, moved(): return lax.ppermute(value, ('dp', 'feat'), moves)  3.62 us
    unnamed x6, local copies, waits for them, and re-layouts  3.41 us
    pallas_call x1, Pallas kernels, on_device(): pl.pallas_call(functools.partial(route_kernel, cls_dev, capacity), out_sh...  2.39 us
  transfers between devices with their start and end apart: 8, of which 5 were waited for; matrix products, arithmetic and copies ran while one was open for 0% of the time, Pallas kernels for 11%

profile of v2, /device:TPU:0, one launch (start us, length us, event | category | flops | bytes accessed | tf_op | source)
XLA Modules:
  0.0 58.4 jit_solution(6737395921680833749)
XLA Ops:
  0.6 2.4 %route.1 = (bf16[256,1024]{1,0:T(8,128)(2,1)}, f32[8,128]{1,0:T(8,128)}) custom-call(s32[128]{0:T(128)} %labels_in.1, s32[5456]{0:T(1024)} %table_in.1, bf16[128,1024]{1,0:T(8,128)(2,1)} %teacher.1, bf16[128,768]{1,0:T(8,128)(2,1)} %student.1), custom_call_target="tpu_custom_call" | custom-call | tf_op jit(solution)/shard_map/route/pallas_call | solution.py:265
  3.0 8.3 %all-to-all-start = ((bf16[16,16,1024]{2,1,0:T(8,128)(2,1)}), bf16[16,16,1024]{2,1,0:T(8,128)(2,1)S(1)}, u32[]{:S(2)}, u32[]{:S(2)}) async-start(bf16[16,16,1024]{2,1,0:T(8,128)(2,1)} %bitcast.7), calls=%async_computation | async-start | bytes 1048576 | tf_op jit(solution)/shard_map/all_to_all | solution.py:298
  11.4 0.0 copy-start
  11.4 1.6 %copy-done = bf16[1024,1024]{1,0:T(8,128)(2,1)S(1)} copy-done((bf16[1024,1024]{1,0:T(8,128)(2,1)S(1)}, bf16[1024,1024]{1,0:T(8,128)(2,1)}, u32[]{:S(2)}) %copy-start) | copy-done | bytes 2097176
  13.0 1.1 %copy-done.1 = bf16[768,512]{1,0:T(8,128)(2,1)S(1)} copy-done((bf16[768,512]{1,0:T(8,128)(2,1)S(1)}, bf16[768,512]{1,0:T(8,128)(2,1)}, u32[]{:S(2)}) %copy-start.1) | copy-done | bytes 786456
  14.1 0.7 %copy-done.2 = f32[8,128]{1,0:T(8,128)S(1)} copy-done((f32[8,128]{1,0:T(8,128)S(1)}, f32[8,128]{1,0:T(8,128)}, u32[]{:S(2)}) %copy-start.2) | copy-done | bytes 4120
  14.8 0.2 load.1
  15.0 0.1 collective-permute-start.1
  15.1 11.4 %all-to-all-done = bf16[16,16,1024]{2,1,0:T(8,128)(2,1)S(1)} async-done(((bf16[16,16,1024]{2,1,0:T(8,128)(2,1)}), bf16[16,16,1024]{2,1,0:T(8,128)(2,1)S(1)}, u32[]{:S(2)}, u32[]{:S(2)}) %all-to-all-start) | async-done | bytes 524320 | tf_op jit(solution)/shard_map/all_to_all | solution.py:298
  26.5 0.0 collective-permute-start
  26.5 0.7 %collective-permute-start.4 = (bf16[256,1024]{1,0:T(8,128)(2,1)S(1)}, bf16[256,1024]{1,0:T(8,128)(2,1)S(1)}, u32[]{:S(2)}, u32[]{:S(2)}) collective-permute-start(bf16[256,1024]{1,0:T(8,128)(2,1)S(1)} %bitcast.4), channel_id=1, source_target_pairs={{1,3},{3,1},{5,7},{7,5},{9,11},{11,9},{13,15},{15,13},{17,19},{19,... | collective-permute-start | bytes 1572872 | tf_op jit(solution)/shard_map/ppermute | solution.py:260
  27.2 1.2 %collective-permute-done.refs_1_ = bf16[256,1024]{1,0:T(8,128)(2,1)S(1)} collective-permute-done((bf16[256,1024]{1,0:T(8,128)(2,1)S(1)}, bf16[256,1024]{1,0:T(8,128)(2,1)S(1)}, u32[]{:S(2)}, u32[]{:S(2)}) %collective-permute-start) | collective-permute-done | bytes 524320 | tf_op jit(solution)/shard_map/ppermute | solution.py:260
  28.4 5.7 %classes.1 = (f32[512,256]{1,0:T(8,128)S(1)}, bf16[512,256]{1,0:T(8,128)(2,1)S(1)}, f32[1,384]{1,0:T(1,128)S(1)}, bf16[256,768]{1,0:T(8,128)(2,1)S(1)}) custom-call(bf16[256,1024]{1,0:T(8,128)(2,1)S(1)} %bitcast.5, bf16[256,1024]{1,0:T(8,128)(2,1)S(1)} %collective-permute-done.refs_1_, bf16[768,512]{1,0:T(8,128)(2,1)S(1)} %get-tuple-element.20.refs_2_, ...), custom_call_target="tpu_custom_call" | custom-call | tf_op jit(solution)/shard_map/classes/pallas_call | solution.py:303
  34.1 0.9 %collective-permute-start.2 = (bf16[512,256]{1,0:T(8,128)(2,1)S(1)}, bf16[512,256]{1,0:T(8,128)(2,1)S(1)}, u32[]{:S(2)}, u32[]{:S(2)}) collective-permute-start(bf16[512,256]{1,0:T(8,128)(2,1)S(1)} %get-tuple-element.23), channel_id=1, source_target_pairs={{0,1},{1,0},{2,3},{3,2},{4,5},{5,4},{6,7},{7,6},{8,9},{9,8},{10,11... | collective-permute-start | bytes 786440 | tf_op jit(solution)/shard_map/ppermute | solution.py:260
  35.0 0.1 collective-permute-start.3
  35.1 1.1 %collective-permute-done.3.refs_3_ = f32[1,384]{1,0:T(1,128)S(1)} collective-permute-done((f32[1,384]{1,0:T(1,128)S(1)}, f32[1,384]{1,0:T(1,128)S(1)}, u32[]{:S(2)}, u32[]{:S(2)}) %collective-permute-start.3) | collective-permute-done | bytes 1568 | tf_op jit(solution)/shard_map/ppermute | solution.py:260
  36.2 0.8 %collective-permute-start.5 = (bf16[256,1024]{1,0:T(8,128)(2,1)S(1)}, bf16[256,1024]{1,0:T(8,128)(2,1)S(1)}, u32[]{:S(2)}, u32[]{:S(2)}) collective-permute-start(bf16[256,1024]{1,0:T(8,128)(2,1)S(1)} %collective-permute-done.4.refs_5_), channel_id=1, source_target_pairs={{0,1},{1,0},{2,3},{3,2},{4,5},{5,4},{6,7},{7,6},{8,9},{9,8},{10,11... | collective-permute-start | bytes 1572872 | tf_op jit(solution)/shard_map/ppermute | solution.py:260
  37.0 1.1 %collective-permute-start.6 = (bf16[256,256]{1,0:T(8,128)(2,1)S(1)}, bf16[256,256]{1,0:T(8,128)(2,1)S(1)}, u32[]{:S(2)}, u32[]{:S(2)}) collective-permute-start(bf16[256,256]{1,0:T(8,128)(2,1)S(1)} %fold.1), channel_id=1, source_target_pairs={{0,2},{1,3},{2,0},{3,1},{4,6},{5,7},{6,4},{7,5},{8,10},{9,11},{10,... | collective-permute-start | bytes 393224 | tf_op jit(solution)/shard_map/ppermute | solution.py:260
  38.1 0.4 collective-permute-done.5.refs_6_
  38.5 0.8 %own.1 = (f32[256,768]{1,0:T(8,128)S(1)}, f32[341]{0:T(512)}, bf16[256,768]{1,0:T(8,128)(2,1)S(1)}) custom-call(f32[512,256]{1,0:T(8,128)S(1)} %get-tuple-element.25.refs_0_, bf16[512,256]{1,0:T(8,128)(2,1)S(1)} %collective-permute-done.2.refs_1_, f32[1,384]{1,0:T(1,128)S(1)} %get-tuple-element.27.refs_2_, f32[1,384]{1,0:T(1,128)S(1)} %collective-permute-done.3.refs_3_, ...), custom_call_target="tpu_custom_call" | custom-call | tf_op jit(solution)/shard_map/own/pallas_call | solution.py:337
  39.2 3.2 %collective-permute-done.6.grads = bf16[256,256]{1,0:T(8,128)(2,1)S(1)} collective-permute-done((bf16[256,256]{1,0:T(8,128)(2,1)S(1)}, bf16[256,256]{1,0:T(8,128)(2,1)S(1)}, u32[]{:S(2)}, u32[]{:S(2)}) %collective-permute-start.6) | collective-permute-done | bytes 131104 | tf_op jit(solution)/shard_map/ppermute | solution.py:260
  42.4 0.3 head.1
  42.7 15.0 %all_to_all.10 = bf16[8,32,768]{2,1,0:T(8,128)(2,1)S(1)} all-to-all(bf16[8,32,768]{2,1,0:T(8,128)(2,1)S(1)} %bitcast.6), channel_id=1, replica_groups={{0,4,8,12,16,20,24,28},{2,6,10,14,18,22,26,30},{1,5,9,13,17,21,25,29},{..., dimensions={0} | all-to-all | bytes 786432 | tf_op jit(solution)/shard_map/all_to_all | solution.py:363
  57.7 0.7 %convert_reduce_fusion = f32[32,768]{1,0:T(8,128)} fusion(bf16[8,32,768]{2,1,0:T(8,128)(2,1)S(1)} %all_to_all.10), kind=kLoop, calls=%fused_computation | loop fusion | flops 368640 | bytes 491520 | tf_op jit(solution)/shard_map/reduce_sum | solution.py:371
  (6 shorter events, 0.0 us)
Async XLA Ops:
  3.0 23.5 %all-to-all-start = ((bf16[16,16,1024]{2,1,0:T(8,128)(2,1)}), bf16[16,16,1024]{2,1,0:T(8,128)(2,1)S(1)}, u32[]{:S(2)}, u32[]{:S(2)}) async-start(bf16[16,16,1024]{2,1,0:T(8,128)(2,1)} %bitcast.7), calls=%async_computation | async-start | bytes 1048576 | tf_op jit(solution)/shard_map/all_to_all | solution.py:298
  11.4 1.6 %copy-start = (bf16[1024,1024]{1,0:T(8,128)(2,1)S(1)}, bf16[1024,1024]{1,0:T(8,128)(2,1)}, u32[]{:S(2)}) copy-start(bf16[1024,1024]{1,0:T(8,128)(2,1)} %freqs_in.1) | copy-start | bytes 6291460
  13.0 1.1 %copy-start.1 = (bf16[768,512]{1,0:T(8,128)(2,1)S(1)}, bf16[768,512]{1,0:T(8,128)(2,1)}, u32[]{:S(2)}) copy-start(bf16[768,512]{1,0:T(8,128)(2,1)} %head_in.1) | copy-start | bytes 2359300
  14.1 0.7 %copy-start.2 = (f32[8,128]{1,0:T(8,128)S(1)}, f32[8,128]{1,0:T(8,128)}, u32[]{:S(2)}) copy-start(f32[8,128]{1,0:T(8,128)} %get-tuple-element.19._) | copy-start | bytes 12292
  15.0 12.2 %collective-permute-start.1 = (bf16[768,512]{1,0:T(8,128)(2,1)S(1)}, bf16[768,512]{1,0:T(8,128)(2,1)}, u32[]{:S(2)}, u32[]{:S(2)}) collective-permute-start(bf16[768,512]{1,0:T(8,128)(2,1)S(1)} %get-tuple-element.20.refs_2_), channel_id=1, source_target_pairs={{0,1},{1,0},{2,3},{3,2},{4,5},{5,4},{6,7},{7,6},{8,9},{9,8},{10,11... | collective-permute-start | bytes 2359304 | tf_op jit(solution)/shard_map/ppermute | solution.py:260
  26.5 1.9 %collective-permute-start = (bf16[256,1024]{1,0:T(8,128)(2,1)S(1)}, bf16[256,1024]{1,0:T(8,128)(2,1)S(1)}, u32[]{:S(2)}, u32[]{:S(2)}) collective-permute-start(bf16[256,1024]{1,0:T(8,128)(2,1)S(1)} %bitcast.3), channel_id=1, source_target_pairs={{0,1},{1,0},{2,3},{3,2},{4,5},{5,4},{6,7},{7,6},{8,9},{9,8},{10,11... | collective-permute-start | bytes 1572872 | tf_op jit(solution)/shard_map/ppermute | solution.py:260
  26.5 8.6 %collective-permute-start.4 = (bf16[256,1024]{1,0:T(8,128)(2,1)S(1)}, bf16[256,1024]{1,0:T(8,128)(2,1)S(1)}, u32[]{:S(2)}, u32[]{:S(2)}) collective-permute-start(bf16[256,1024]{1,0:T(8,128)(2,1)S(1)} %bitcast.4), channel_id=1, source_target_pairs={{1,3},{3,1},{5,7},{7,5},{9,11},{11,9},{13,15},{15,13},{17,19},{19,... | collective-permute-start | bytes 1572872 | tf_op jit(solution)/shard_map/ppermute | solution.py:260
  34.1 2.1 %collective-permute-start.2 = (bf16[512,256]{1,0:T(8,128)(2,1)S(1)}, bf16[512,256]{1,0:T(8,128)(2,1)S(1)}, u32[]{:S(2)}, u32[]{:S(2)}) collective-permute-start(bf16[512,256]{1,0:T(8,128)(2,1)S(1)} %get-tuple-element.23), channel_id=1, source_target_pairs={{0,1},{1,0},{2,3},{3,2},{4,5},{5,4},{6,7},{7,6},{8,9},{9,8},{10,11... | collective-permute-start | bytes 786440 | tf_op jit(solution)/shard_map/ppermute | solution.py:260
  35.0 1.2 %collective-permute-start.3 = (f32[1,384]{1,0:T(1,128)S(1)}, f32[1,384]{1,0:T(1,128)S(1)}, u32[]{:S(2)}, u32[]{:S(2)}) collective-permute-start(f32[1,384]{1,0:T(1,128)S(1)} %get-tuple-element.27.refs_2_), channel_id=1, source_target_pairs={{0,1},{1,0},{2,3},{3,2},{4,5},{5,4},{6,7},{7,6},{8,9},{9,8},{10,11... | collective-permute-start | bytes 4616 | tf_op jit(solution)/shard_map/ppermute | solution.py:260
  36.2 2.3 %collective-permute-start.5 = (bf16[256,1024]{1,0:T(8,128)(2,1)S(1)}, bf16[256,1024]{1,0:T(8,128)(2,1)S(1)}, u32[]{:S(2)}, u32[]{:S(2)}) collective-permute-start(bf16[256,1024]{1,0:T(8,128)(2,1)S(1)} %collective-permute-done.4.refs_5_), channel_id=1, source_target_pairs={{0,1},{1,0},{2,3},{3,2},{4,5},{5,4},{6,7},{7,6},{8,9},{9,8},{10,11... | collective-permute-start | bytes 1572872 | tf_op jit(solution)/shard_map/ppermute | solution.py:260
  37.0 5.5 %collective-permute-start.6 = (bf16[256,256]{1,0:T(8,128)(2,1)S(1)}, bf16[256,256]{1,0:T(8,128)(2,1)S(1)}, u32[]{:S(2)}, u32[]{:S(2)}) collective-permute-start(bf16[256,256]{1,0:T(8,128)(2,1)S(1)} %fold.1), channel_id=1, source_target_pairs={{0,2},{1,3},{2,0},{3,1},{4,6},{5,7},{6,4},{7,5},{8,10},{9,11},{10,... | collective-permute-start | bytes 393224 | tf_op jit(solution)/shard_map/ppermute | solution.py:260

commit v3 on v2

--- a/solution.py
+++ b/solution.py
@@ -9,6 +9,8 @@
 from jax.sharding import PartitionSpec as P
 
 LANES = 128
+CARRIED = 16
+PIECES = 3
 TURN = 1.0 / (2.0 * math.pi)
 ROUNDER = 1.5 * 2.0**23
 SINE = (6.283164044217864, -41.337142357601536, 81.3407683703199, -70.9934277613874)
@@ -115,28 +117,64 @@
         copy.wait()
 
 
-def class_kernel(n_feat, n_dp, pair, cls_pad, d_t, d_s, permuted, *refs):
-    parts, heads, refs = refs[:n_feat], refs[n_feat : 2 * n_feat], refs[2 * n_feat :]
-    freqs, refs = refs[0], refs[1:]
+def carry(norm, lanes):
+    row = lax.broadcasted_iota(jnp.int32, (CARRIED, lanes), 0)
+    block, index = jnp.zeros((CARRIED, lanes), jnp.float32), 0
+    for _ in range(PIECES):
+        piece = norm.astype(jnp.bfloat16).astype(jnp.float32)
+        norm = norm - piece
+        for start in range(0, norm.shape[1], lanes):
+            block = jnp.where(row == index, piece[:, start : start + lanes], block)
+            index += 1
+    return block.astype(jnp.bfloat16)
+
+
+def carried_norm(block, size):
+    lanes = block.shape[1]
+    values = block.astype(jnp.float32)
+    width = size // lanes
+    found = []
+    for part in range(width):
+        rows = [values[p * width + part : p * width + part + 1, :] for p in range(PIECES)]
+        found.append(sum(rows[1:], rows[0]))
+    return jnp.concatenate(found, axis=1) if width > 1 else found[0]
+
+
+def sort_kernel(mine, other, teacher, student, tags):
+    d_s = student.shape[1]
+    holds_student = lax.axis_index("feat") == 1
+
+    def split(first, second):
+        teacher[...] = first[...]
+        student[...] = second[:, :d_s]
+        tags[...] = second[:, d_s : d_s + LANES]
+
+    pl.when(holds_student)(lambda: split(other, mine))
+    pl.when(jnp.logical_not(holds_student))(lambda: split(mine, other))
+
+
+def member_of(group, bit, side):
+    low = group * 2 + side
+    high = group // 2 * 4 + side * 2 + group % 2
+    return jnp.where(bit == 0, low, high)
+
+
+def class_kernel(n_feat, n_dp, bits, cls_pad, permuted, teacher, student, tags_in, *refs):
+    heads, freqs, refs = refs[:n_feat], refs[n_feat], refs[n_feat + 1 :]
     if permuted:
         weights, refs = refs[0], refs[1:]
     grads, refs = refs[:n_feat], refs[n_feat:]
-    norms, student, rows, projected, grad_z, picked, near, sems = refs
+    norms, projected, grad_z, picked, near, sems = refs
     feat = lax.axis_index("feat")
-    side = lax.rem(lax.axis_index("dp"), pair)
+    holder = lax.axis_index("dp")
     copies = [
         pltpu.make_async_copy(heads[k], near.at[k - 1], sems.at[k - 1]) for k in range(1, n_feat)
     ]
     for copy in copies:
         copy.start()
-    slots, width = parts[0].shape
+    slots, d_t = teacher.shape
     half = freqs.shape[1]
-    for offset in range(n_feat):
-        index = lax.rem(feat + (n_feat - offset), n_feat)
-        rows[:, pl.ds(pl.multiple_of(index * width, LANES), width)] = parts[offset][...]
-    s_rows = rows[:, d_t : d_t + d_s]
-    student[...] = s_rows
-    tags = rows[:, d_t + d_s : d_t + d_s + LANES].astype(jnp.float32)
+    tags = tags_in[...].astype(jnp.float32)
     lane = lax.broadcasted_iota(jnp.int32, (slots, LANES), 1)
     tag = jnp.sum(
         tags * jnp.where(lane == 0, 32.0, jnp.where(lane == 1, 1.0, 0.0)), axis=1, keepdims=True
@@ -152,20 +190,22 @@
         weight = near[offset - 1] if offset else heads[0][...]
         index = lax.rem(feat + (n_feat - offset), n_feat)
         projected[:, pl.ds(pl.multiple_of(index * part, LANES), part)] = jnp.dot(
-            s_rows, weight, preferred_element_type=jnp.float32
+            student[...], weight, preferred_element_type=jnp.float32
         ).astype(jnp.bfloat16)
     step = min(half, 256)
+    blocks = [slice(column, column + step) for column in range(0, half, step)]
+    teacher_z = [
+        jnp.dot(teacher[...], freqs[:, block], preferred_element_type=jnp.float32)
+        for block in blocks
+    ]
+    student_z = [
+        jnp.dot(projected[...], freqs[:, block], preferred_element_type=jnp.float32)
+        for block in blocks
+    ]
     norm = jnp.zeros((slots, 1), jnp.float32)
-    for column in range(0, half, step):
-        block = slice(column, column + step)
-        student_z = jnp.dot(
-            projected[...], freqs[:, block], preferred_element_type=jnp.float32
-        )
-        teacher_z = jnp.dot(
-            rows[:, :d_t], freqs[:, block], preferred_element_type=jnp.float32
-        )
-        cos_s, sin_s = cos_sin(student_z)
-        cos_t, sin_t = cos_sin(teacher_z)
+    for index, block in enumerate(blocks):
+        cos_s, sin_s = cos_sin(student_z[index])
+        cos_t, sin_t = cos_sin(teacher_z[index])
         mean_c = inverse * jnp.dot(
             same, (cos_s - cos_t).astype(jnp.bfloat16), preferred_element_type=jnp.float32
         )
@@ -175,24 +215,31 @@
         norm += jnp.sum(mean_c * mean_c + mean_s * mean_s, axis=1, keepdims=True)
         grad_z[:, block] = (cos_s * mean_s - sin_s * mean_c).astype(jnp.bfloat16)
     cls = lax.broadcasted_iota(jnp.int32, (slots, cls_pad), 1).astype(jnp.float32) + 1.0
-    norms[...] = jnp.sum(jnp.where(cls == tag, norm, 0.0), axis=0, keepdims=True)
+    total_norm = jnp.sum(jnp.where(cls == tag, norm, 0.0), axis=0, keepdims=True)
+    norms[...] = total_norm
+    carried = carry(total_norm, slots)
     out_rows = d_t // (n_dp * n_feat)
-    block = n_dp // pair * out_rows
+    block = n_dp // 2 * out_rows
     for offset in range(n_feat):
-        for across in range(pair):
-            index = lax.rem(side + across, pair) * n_feat + lax.rem(feat + offset, n_feat)
-            target = slice(across * block, (across + 1) * block)
-            if permuted:
-                picked[target, :] = weights[index]
-            else:
-                for group in range(n_dp // pair):
-                    start = pl.multiple_of((group * pair * n_feat + index) * out_rows, out_rows)
-                    first = across * block + group * out_rows
-                    picked[first : first + out_rows, :] = freqs[pl.ds(start, out_rows), :]
+        target = lax.rem(feat + offset, n_feat)
+        bit = lax.rem(target, bits)
+        side = jnp.where(bit == 0, lax.rem(holder, 2), lax.rem(holder // 2, 2))
+        if permuted:
+            picked[...] = weights[offset]
+        else:
+            for index in range(n_dp):
+                across, group = divmod(index, n_dp // 2)
+                member = member_of(group, bit, 1 - side if across else side)
+                start = pl.multiple_of((member * n_feat + target) * out_rows, out_rows)
+                picked[index * out_rows : (index + 1) * out_rows, :] = freqs[
+                    pl.ds(start, out_rows), :
+                ]
         out = grads[offset]
-        out[...] = lax.dot_general(
+        out[: 2 * block, :] = lax.dot_general(
             picked[...], grad_z[...], (((1,), (1,)), ((), ())), preferred_element_type=jnp.float32
         ).astype(out.dtype)
+        if offset:
+            out[2 * block :, :] = carried
 
 
 def summed(refs, start, size):
@@ -207,28 +254,19 @@
     refs[-1][...] = summed(refs[:-1], size, size)
 
 
-def own_kernel(n_feat, scale, divisor, d_t, d_s, *refs):
-    grads, norms, student = refs[:n_feat], refs[n_feat : 2 * n_feat], refs[2 * n_feat]
-    parts, refs = refs[2 * n_feat + 1 : -4], refs[-4:]
-    head, loss, partner, rows = refs
-    feat = lax.axis_index("feat")
+def own_kernel(scale, divisor, *refs):
+    grads, (norms, student, head, loss) = refs[:-4], refs[-4:]
     head[...] = scale * jnp.dot(
         summed(grads, 0, head.shape[0]), student[...], preferred_element_type=jnp.float32
     )
-    norm = norms[0][...]
-    for offset in range(1, n_feat):
-        norm += norms[offset][...]
+    norm = norms[...]
+    for ref in grads[1:]:
+        norm += carried_norm(ref[ref.shape[0] - CARRIED :, :], norm.shape[1])
     loss[...] = (norm * (1.0 / divisor))[0, : loss.shape[0]]
-    for offset, part in enumerate(parts):
-        width = part.shape[1]
-        index = lax.rem(feat + (n_feat - offset), n_feat)
-        rows[:, pl.ds(pl.multiple_of(index * width, LANES), width)] = part[...]
-    if parts:
-        partner[...] = rows[:, d_t : d_t + d_s]
-
-
-def head_kernel(scale, own, grads, partner, head):
-    product = jnp.dot(grads[...], partner[...], preferred_element_type=jnp.float32)
+
+
+def head_kernel(scale, own, grads, student, head):
+    product = jnp.dot(grads[...], student[...], preferred_element_type=jnp.float32)
     head[...] = (own[...] + product * scale).astype(jnp.bfloat16)
 
 
@@ -240,27 +278,29 @@
     half = freqs.shape[1]
     classes = class_slot.shape[0]
     cls_dev = classes // n_dp
-    cls_pad = up_to(cls_dev, LANES)
     capacity = 2 * images // n_dp
     slots = n_dp * capacity
+    cls_pad = up_to(cls_dev, slots)
     width = up_to(d_t + d_s + LANES, LANES * n_feat) // n_feat
     out_rows = d_t // (n_dp * n_feat)
-    pair = 2 if n_dp % 2 == 0 else 1
-    groups = n_dp // pair
+    bits = 2 if n_dp % 4 == 0 else 1
+    block = n_dp // 2 * out_rows
     vmem = pltpu.CompilerParams(vmem_limit_bytes=20 * 2**20)
     hbm = pl.BlockSpec(memory_space=pltpu.HBM)
     near = pl.BlockSpec(memory_space=pltpu.VMEM)
 
-    def moved(value, across, offset, feats=None):
+    def across(value):
         moves = [
-            (d * n_feat + f, (d ^ across) * n_feat + (f + offset) % n_feat)
+            (d * n_feat + f, (d ^ (1 << f % bits)) * n_feat + f)
             for d in range(n_dp)
-            for f in (range(n_feat) if feats is None else feats)
+            for f in range(n_feat)
         ]
         return lax.ppermute(value, ("dp", "feat"), moves)
 
-    def all_parts(value):
-        return [value] + [moved(value, 0, k) for k in range(1, n_feat)]
+    def shifted(value, offset):
+        return lax.ppermute(
+            value, "feat", [(f, (f + offset) % n_feat) for f in range(n_feat)]
+        )
 
     sent, token = pl.pallas_call(
         functools.partial(route_kernel, cls_dev, capacity),
@@ -281,8 +321,14 @@
     permuted = out_rows % 16 != 0
     weights = []
     if permuted:
-        weights = jnp.swapaxes(freqs.reshape(groups, pair * n_feat, out_rows, half), 0, 1)
-        weights = [weights.reshape(pair * n_feat, groups * out_rows, half)]
+        targets = (lax.axis_index("feat") + jnp.arange(n_feat)) % n_feat
+        bit = (targets % bits)[:, None]
+        group = jnp.tile(jnp.arange(n_dp // 2), 2)[None, :]
+        side = (lax.axis_index("dp") >> bit) % 2
+        side = jnp.where(jnp.arange(n_dp)[None, :] >= n_dp // 2, 1 - side, side)
+        member = member_of(group, bit, side)
+        lines = (member * n_feat + targets[:, None])[:, :, None] * out_rows + jnp.arange(out_rows)
+        weights = [jnp.take(freqs, lines.reshape(n_feat, 2 * block), axis=0)]
     head_near, freqs_near = pl.pallas_call(
         load_kernel,
         out_shape=(
@@ -294,79 +340,83 @@
         compiler_params=vmem,
         name="load",
     )(head, freqs, token)
-    heads = all_parts(head_near)
+    heads = [head_near] + [shifted(head_near, k) for k in range(1, n_feat)]
     mine = lax.all_to_all(
         sent.reshape(n_dp, capacity, width), "dp", split_axis=0, concat_axis=0, tiled=True
     ).reshape(slots, width)
-    parts = all_parts(mine)
-    block = groups * out_rows
-    *grads, norms, s_rows = pl.pallas_call(
-        functools.partial(class_kernel, n_feat, n_dp, pair, cls_pad, d_t, d_s, permuted),
+    if n_feat == 2 and width == d_t:
+        teacher_in, student_in, tags_in = pl.pallas_call(
+            sort_kernel,
+            out_shape=(
+                jax.ShapeDtypeStruct((slots, d_t), jnp.bfloat16),
+                jax.ShapeDtypeStruct((slots, d_s), jnp.bfloat16),
+                jax.ShapeDtypeStruct((slots, LANES), jnp.bfloat16),
+            ),
+            compiler_params=vmem,
+            name="sort",
+        )(mine, shifted(mine, 1))
+    else:
+        everything = lax.all_gather(mine, "feat", axis=1, tiled=True)
+        teacher_in, student_in, tags_in = jnp.split(
+            everything[:, : d_t + d_s + LANES], [d_t, d_t + d_s], axis=1
+        )
+    student_across = across(student_in)
+    *grads, norms = pl.pallas_call(
+        functools.partial(class_kernel, n_feat, n_dp, bits, cls_pad, permuted),
         out_shape=tuple(
-            jax.ShapeDtypeStruct((pair * block, slots), jnp.bfloat16 if k else jnp.float32)
+            jax.ShapeDtypeStruct((2 * block + CARRIED, slots), jnp.bfloat16)
+            if k
+            else jax.ShapeDtypeStruct((2 * block, slots), jnp.float32)
             for k in range(n_feat)
         )
-        + (
-            jax.ShapeDtypeStruct((1, cls_pad), jnp.float32),
-            jax.ShapeDtypeStruct((slots, d_s), jnp.bfloat16),
-        ),
+        + (jax.ShapeDtypeStruct((1, cls_pad), jnp.float32),),
+        in_specs=[near] * 4 + [hbm] * (n_feat - 1) + [near] * (1 + len(weights)),
         scratch_shapes=[
-            pltpu.VMEM((slots, width * n_feat), jnp.bfloat16),
             pltpu.VMEM((slots, d_t), jnp.bfloat16),
             pltpu.VMEM((slots, half), jnp.bfloat16),
-            pltpu.VMEM((pair * block, half), jnp.bfloat16),
+            pltpu.VMEM((2 * block, half), jnp.bfloat16),
             pltpu.VMEM((n_feat - 1, *head.shape), jnp.bfloat16),
             pltpu.SemaphoreType.DMA((n_feat - 1,)),
         ],
-        in_specs=[near] * (n_feat + 1) + [hbm] * (n_feat - 1) + [near] * (1 + len(weights)),
         compiler_params=vmem,
         name="classes",
-    )(*parts, *heads, freqs_near, *weights)
-    partner = []
-    if pair > 1:
-        holders = [
-            f for f in range(n_feat) if f * width < d_t + d_s and (f + 1) * width > d_t
-        ]
-        across = moved(mine, 1, 0, holders)
-    all_grads = [grads[0]] + [moved(grads[k], 0, k) for k in range(1, n_feat)]
-    all_norms = all_parts(norms)
-    if pair > 1:
-        all_grads, all_norms, across = lax.optimization_barrier((all_grads, all_norms, across))
-        partner = all_parts(across)
+    )(teacher_in, student_in, tags_in, *heads, freqs_near, *weights)
+    all_grads = [grads[0]] + [shifted(grads[k], k) for k in range(1, n_feat)]
+    all_grads, student_across = lax.optimization_barrier((all_grads, student_across))
     scale = 1.0 / math.sqrt(images * n_dp)
-    own, loss, partner_rows = pl.pallas_call(
-        functools.partial(own_kernel, n_feat, scale, 2.0 * half * n_feat, d_t, d_s),
+    folded = pl.pallas_call(
+        fold_kernel,
+        out_shape=jax.ShapeDtypeStruct((block, slots), jnp.bfloat16),
+        compiler_params=vmem,
+        name="fold",
+    )(*all_grads)
+    folded, all_grads = lax.optimization_barrier((folded, all_grads))
+    own, loss = pl.pallas_call(
+        functools.partial(own_kernel, scale, 2.0 * half * n_feat),
         out_shape=(
             jax.ShapeDtypeStruct((block, d_s), jnp.float32),
             jax.ShapeDtypeStruct((cls_dev,), jnp.float32),
-            jax.ShapeDtypeStruct((slots, d_s), jnp.bfloat16),
         ),
-        scratch_shapes=[pltpu.VMEM((slots, width * n_feat), jnp.bfloat16)],
         compiler_params=vmem,
         name="own",
-    )(*all_grads, *all_norms, s_rows, *partner)
-    if pair > 1:
-        folded = pl.pallas_call(
-            fold_kernel,
-            out_shape=jax.ShapeDtypeStruct((block, slots), jnp.bfloat16),
-            compiler_params=vmem,
-            name="fold",
-        )(*all_grads)
-        partial_head = pl.pallas_call(
-            functools.partial(head_kernel, scale),
-            out_shape=jax.ShapeDtypeStruct((block, d_s), jnp.bfloat16),
-            compiler_params=vmem,
-            name="head",
-        )(own, moved(folded, 1, 0), partner_rows)
-    else:
-        partial_head = own.astype(jnp.bfloat16)
+    )(*all_grads, norms, student_in)
+    partial_head = pl.pallas_call(
+        functools.partial(head_kernel, scale),
+        out_shape=jax.ShapeDtypeStruct((block, d_s), jnp.bfloat16),
+        compiler_params=vmem,
+        name="head",
+    )(own, across(folded), student_across)
     received = lax.all_to_all(
-        partial_head.reshape(groups, out_rows, d_s),
-        "dp",
+        partial_head.reshape(n_dp // 2, out_rows, d_s),
+        ("dp", "feat"),
         split_axis=0,
         concat_axis=0,
         tiled=True,
-        axis_index_groups=[list(range(p, n_dp, pair)) for p in range(pair)],
+        axis_index_groups=[
+            [d * n_feat + f for d in range(n_dp) if (d >> f % bits) % 2 == side]
+            for f in range(n_feat)
+            for side in range(2)
+        ],
     )
     head_grad = jnp.sum(received.astype(jnp.float32), axis=0)
     return (head_grad, loss)

time: 58.8 us -> 57.2 us (0.973)
  starting transfers between devices: 12 us -> 10.2 us
  waiting for transfers between devices: 17.3 us -> 18.7 us
  Pallas kernels: 9.35 us -> 8.67 us
  blocking collectives: 15 us -> 14.4 us
    ppermute x7 -> x5, starting transfers between devices: 3.62 us -> 1.88 us  [the longest x2 1.52 us: across(): return lax.ppermute(value, ('dp', 'feat'), moves)]
    ppermute x7 -> x5, waiting for transfers between devices: 5.88 us -> 7.28 us  [the longest x2 4.04 us: across(): return lax.ppermute(value, ('dp', 'feat'), moves)]
    pallas_call x2 -> x3, Pallas kernels: 6.45 us -> 5.77 us  [the longest x1 4.94 us: on_device(): pl.pallas_call(functools.partial(class_kernel, n_feat, n_dp, bits, cls_pa...]
  transfers between devices with their start and end apart: 8 -> 6, of which waited for: 5 -> 5; matrix products, arithmetic and copies ran while one was open for 0% -> 0% of each run, Pallas kernels for 11% -> 11%
where the time goes in v3:
time: 57.2 us; the launch traced here: 56.8 us
  waiting for transfers between devices  18.7 us (33%)
  blocking collectives  14.4 us (25%)
  starting transfers between devices  10.2 us (18%)
  Pallas kernels  8.67 us (15%)
  local copies, waits for them, and re-layouts  3.41 us (6%)
  between operations  0.7 us (1%)
  other arithmetic  0.69 us (1%)
    all_to_all x1, blocking collectives, on_device(): lax.all_to_all(partial_head.reshape(n_dp // 2, out_rows, d_s), ('dp', 'fe...  14.4 us
    all_to_all x1, waiting for transfers between devices, on_device(): lax.all_to_all(sent.reshape(n_dp, capacity, width), 'dp', split_axis=0, c...  11.4 us
    all_to_all x1, starting transfers between devices, on_device(): lax.all_to_all(sent.reshape(n_dp, capacity, width), 'dp', split_axis=0, c...  8.33 us
    pallas_call x1, Pallas kernels, on_device(): pl.pallas_call(functools.partial(class_kernel, n_feat, n_dp, bits, cls_pa...  4.94 us
    ppermute x2, waiting for transfers between devices, across(): return lax.ppermute(value, ('dp', 'feat'), moves)  4.04 us
    unnamed x6, local copies, waits for them, and re-layouts  3.41 us
    ppermute x3, waiting for transfers between devices, shifted(): lax.ppermute(value, 'feat', [(f, (f + offset) % n_feat) for f in range(n_...  3.24 us
    pallas_call x1, Pallas kernels, on_device(): pl.pallas_call(functools.partial(route_kernel, cls_dev, capacity), out_sh...  2.39 us
  transfers between devices with their start and end apart: 6, of which 5 were waited for; matrix products, arithmetic and copies ran while one was open for 0% of the time, Pallas kernels for 11%

profile of v3, /device:TPU:0, one launch (start us, length us, event | category | flops | bytes accessed | tf_op | source)
XLA Modules:
  0.0 56.8 jit_solution(16058715226809299490)
XLA Ops:
  0.6 2.4 %route.1 = (bf16[256,1024]{1,0:T(8,128)(2,1)}, f32[8,128]{1,0:T(8,128)}) custom-call(s32[128]{0:T(128)} %labels_in.1, s32[5456]{0:T(1024)} %table_in.1, bf16[128,1024]{1,0:T(8,128)(2,1)} %teacher.1, bf16[128,768]{1,0:T(8,128)(2,1)} %student.1), custom_call_target="tpu_custom_call" | custom-call | tf_op jit(solution)/shard_map/route/pallas_call | solution.py:305
  3.0 8.3 %all-to-all-start = ((bf16[16,16,1024]{2,1,0:T(8,128)(2,1)}), bf16[16,16,1024]{2,1,0:T(8,128)(2,1)S(1)}, u32[]{:S(2)}, u32[]{:S(2)}) async-start(bf16[16,16,1024]{2,1,0:T(8,128)(2,1)} %bitcast.6), calls=%async_computation | async-start | bytes 1048576 | tf_op jit(solution)/shard_map/all_to_all | solution.py:344
  11.4 0.0 copy-start
  11.4 1.6 %copy-done = bf16[1024,1024]{1,0:T(8,128)(2,1)S(1)} copy-done((bf16[1024,1024]{1,0:T(8,128)(2,1)S(1)}, bf16[1024,1024]{1,0:T(8,128)(2,1)}, u32[]{:S(2)}) %copy-start) | copy-done | bytes 2097176
  13.0 1.1 %copy-done.1 = bf16[768,512]{1,0:T(8,128)(2,1)S(1)} copy-done((bf16[768,512]{1,0:T(8,128)(2,1)S(1)}, bf16[768,512]{1,0:T(8,128)(2,1)}, u32[]{:S(2)}) %copy-start.1) | copy-done | bytes 786456
  14.1 0.7 %copy-done.2 = f32[8,128]{1,0:T(8,128)S(1)} copy-done((f32[8,128]{1,0:T(8,128)S(1)}, f32[8,128]{1,0:T(8,128)}, u32[]{:S(2)}) %copy-start.2) | copy-done | bytes 4120
  14.8 0.2 load.1
  15.0 0.1 collective-permute-start.1
  15.1 11.4 %all-to-all-done = bf16[16,16,1024]{2,1,0:T(8,128)(2,1)S(1)} async-done(((bf16[16,16,1024]{2,1,0:T(8,128)(2,1)}), bf16[16,16,1024]{2,1,0:T(8,128)(2,1)S(1)}, u32[]{:S(2)}, u32[]{:S(2)}) %all-to-all-start) | async-done | bytes 524320 | tf_op jit(solution)/shard_map/all_to_all | solution.py:344
  26.5 0.0 collective-permute-start
  26.5 1.9 %collective-permute-done.other = bf16[256,1024]{1,0:T(8,128)(2,1)S(1)} collective-permute-done((bf16[256,1024]{1,0:T(8,128)(2,1)S(1)}, bf16[256,1024]{1,0:T(8,128)(2,1)S(1)}, u32[]{:S(2)}, u32[]{:S(2)}) %collective-permute-start) | collective-permute-done | bytes 524320 | tf_op jit(solution)/shard_map/ppermute | solution.py:301
  28.4 0.1 sort.1
  28.5 0.6 %collective-permute-start.3 = (bf16[256,768]{1,0:T(8,128)(2,1)S(1)}, bf16[256,768]{1,0:T(8,128)(2,1)S(1)}, u32[]{:S(2)}, u32[]{:S(2)}) collective-permute-start(bf16[256,768]{1,0:T(8,128)(2,1)S(1)} %get-tuple-element.22.student.refs_3_), channel_id=1, source_target_pairs={{0,2},{1,5},{2,0},{3,7},{4,6},{5,1},{6,4},{7,3},{8,10},{9,13},{10,... | collective-permute-start | bytes 1179656 | tf_op jit(solution)/shard_map/ppermute | solution.py:298
  29.1 0.0 collective-permute-done.1.refs_1_
  29.1 4.9 %classes.1 = (f32[512,256]{1,0:T(8,128)S(1)}, bf16[528,256]{1,0:T(8,128)(2,1)S(1)}, f32[1,512]{1,0:T(1,128)S(1)}) custom-call(bf16[256,1024]{1,0:T(8,128)(2,1)S(1)} %get-tuple-element.21.teacher, bf16[256,768]{1,0:T(8,128)(2,1)S(1)} %get-tuple-element.22.student.refs_3_, bf16[256,128]{1,0:T(8,128)(2,1)S(1)} %get-tuple-element.23.tags_in, ...), custom_call_target="tpu_custom_call" | custom-call | tf_op jit(solution)/shard_map/classes/pallas_call | solution.py:364
  34.1 0.3 collective-permute-start.2
  34.4 1.3 %collective-permute-done.2.refs_1_ = bf16[528,256]{1,0:T(8,128)(2,1)S(1)} collective-permute-done((bf16[528,256]{1,0:T(8,128)(2,1)S(1)}, bf16[528,256]{1,0:T(8,128)(2,1)S(1)}, u32[]{:S(2)}, u32[]{:S(2)}) %collective-permute-start.2) | collective-permute-done | bytes 270368 | tf_op jit(solution)/shard_map/ppermute | solution.py:301
  35.7 0.7 %collective-permute-done.3.student = bf16[256,768]{1,0:T(8,128)(2,1)S(1)} collective-permute-done((bf16[256,768]{1,0:T(8,128)(2,1)S(1)}, bf16[256,768]{1,0:T(8,128)(2,1)S(1)}, u32[]{:S(2)}, u32[]{:S(2)}) %collective-permute-start.3) | collective-permute-done | bytes 393248 | tf_op jit(solution)/shard_map/ppermute | solution.py:298
  36.4 0.9 %collective-permute-start.4 = (bf16[256,256]{1,0:T(8,128)(2,1)S(1)}, bf16[256,256]{1,0:T(8,128)(2,1)S(1)}, u32[]{:S(2)}, u32[]{:S(2)}) collective-permute-start(bf16[256,256]{1,0:T(8,128)(2,1)S(1)} %fold.1), channel_id=1, source_target_pairs={{0,2},{1,5},{2,0},{3,7},{4,6},{5,1},{6,4},{7,3},{8,10},{9,13},{10,... | collective-permute-start | bytes 393224 | tf_op jit(solution)/shard_map/ppermute | solution.py:298
  37.3 0.8 %own.1 = (f32[256,768]{1,0:T(8,128)S(1)}, f32[341]{0:T(512)}) custom-call(f32[512,256]{1,0:T(8,128)S(1)} %get-tuple-element.31.refs_0_, bf16[528,256]{1,0:T(8,128)(2,1)S(1)} %collective-permute-done.2.refs_1_, f32[1,512]{1,0:T(1,128)S(1)} %get-tuple-element.33.refs_2_, bf16[256,768]{1,0:T(8,128)(2,1)S(1)} %get-tuple-element.22.student.refs_3_), custom_call_target="tpu_custom_call" | custom-call | tf_op jit(solution)/shard_map/own/pallas_call | solution.py:394
  38.0 3.4 %collective-permute-done.4.grads = bf16[256,256]{1,0:T(8,128)(2,1)S(1)} collective-permute-done((bf16[256,256]{1,0:T(8,128)(2,1)S(1)}, bf16[256,256]{1,0:T(8,128)(2,1)S(1)}, u32[]{:S(2)}, u32[]{:S(2)}) %collective-permute-start.4) | collective-permute-done | bytes 131104 | tf_op jit(solution)/shard_map/ppermute | solution.py:298
  41.4 0.3 head.1
  41.7 14.4 %all_to_all.10 = bf16[8,32,768]{2,1,0:T(8,128)(2,1)S(1)} all-to-all(bf16[8,32,768]{2,1,0:T(8,128)(2,1)S(1)} %bitcast.5), channel_id=1, replica_groups={{0,4,8,12,16,20,24,28},{2,6,10,14,18,22,26,30},{1,3,9,11,17,19,25,27},{..., dimensions={0} | all-to-all | bytes 786432 | tf_op jit(solution)/shard_map/all_to_all | solution.py:409
  56.1 0.7 %convert_reduce_fusion = f32[32,768]{1,0:T(8,128)} fusion(bf16[8,32,768]{2,1,0:T(8,128)(2,1)S(1)} %all_to_all.10), kind=kLoop, calls=%fused_computation | loop fusion | flops 368640 | bytes 491520 | tf_op jit(solution)/shard_map/reduce_sum | solution.py:421
  (3 shorter events, 0.0 us)
Async XLA Ops:
  3.0 23.5 %all-to-all-start = ((bf16[16,16,1024]{2,1,0:T(8,128)(2,1)}), bf16[16,16,1024]{2,1,0:T(8,128)(2,1)S(1)}, u32[]{:S(2)}, u32[]{:S(2)}) async-start(bf16[16,16,1024]{2,1,0:T(8,128)(2,1)} %bitcast.6), calls=%async_computation | async-start | bytes 1048576 | tf_op jit(solution)/shard_map/all_to_all | solution.py:344
  11.4 1.6 %copy-start = (bf16[1024,1024]{1,0:T(8,128)(2,1)S(1)}, bf16[1024,1024]{1,0:T(8,128)(2,1)}, u32[]{:S(2)}) copy-start(bf16[1024,1024]{1,0:T(8,128)(2,1)} %freqs_in.1) | copy-start | bytes 6291460
  13.0 1.1 %copy-start.1 = (bf16[768,512]{1,0:T(8,128)(2,1)S(1)}, bf16[768,512]{1,0:T(8,128)(2,1)}, u32[]{:S(2)}) copy-start(bf16[768,512]{1,0:T(8,128)(2,1)} %head_in.1) | copy-start | bytes 2359300
  14.1 0.7 %copy-start.2 = (f32[8,128]{1,0:T(8,128)S(1)}, f32[8,128]{1,0:T(8,128)}, u32[]{:S(2)}) copy-start(f32[8,128]{1,0:T(8,128)} %get-tuple-element.24._) | copy-start | bytes 12292
  15.0 14.1 %collective-permute-start.1 = (bf16[768,512]{1,0:T(8,128)(2,1)S(1)}, bf16[768,512]{1,0:T(8,128)(2,1)}, u32[]{:S(2)}, u32[]{:S(2)}) collective-permute-start(bf16[768,512]{1,0:T(8,128)(2,1)S(1)} %get-tuple-element.25.refs_0_), channel_id=1, source_target_pairs={{0,1},{1,0},{2,3},{3,2},{4,5},{5,4},{6,7},{7,6},{8,9},{9,8},{10,11... | collective-permute-start | bytes 2359304 | tf_op jit(solution)/shard_map/ppermute | solution.py:301
  26.5 1.9 %collective-permute-start = (bf16[256,1024]{1,0:T(8,128)(2,1)S(1)}, bf16[256,1024]{1,0:T(8,128)(2,1)S(1)}, u32[]{:S(2)}, u32[]{:S(2)}) collective-permute-start(bf16[256,1024]{1,0:T(8,128)(2,1)S(1)} %bitcast.3), channel_id=1, source_target_pairs={{0,1},{1,0},{2,3},{3,2},{4,5},{5,4},{6,7},{7,6},{8,9},{9,8},{10,11... | collective-permute-start | bytes 1572872 | tf_op jit(solution)/shard_map/ppermute | solution.py:301
  28.5 7.8 %collective-permute-start.3 = (bf16[256,768]{1,0:T(8,128)(2,1)S(1)}, bf16[256,768]{1,0:T(8,128)(2,1)S(1)}, u32[]{:S(2)}, u32[]{:S(2)}) collective-permute-start(bf16[256,768]{1,0:T(8,128)(2,1)S(1)} %get-tuple-element.22.student.refs_3_), channel_id=1, source_target_pairs={{0,2},{1,5},{2,0},{3,7},{4,6},{5,1},{6,4},{7,3},{8,10},{9,13},{10,... | collective-permute-start | bytes 1179656 | tf_op jit(solution)/shard_map/ppermute | solution.py:298
  34.1 1.6 %collective-permute-start.2 = (bf16[528,256]{1,0:T(8,128)(2,1)S(1)}, bf16[528,256]{1,0:T(8,128)(2,1)S(1)}, u32[]{:S(2)}, u32[]{:S(2)}) collective-permute-start(bf16[528,256]{1,0:T(8,128)(2,1)S(1)} %get-tuple-element.28), channel_id=1, source_target_pairs={{0,1},{1,0},{2,3},{3,2},{4,5},{5,4},{6,7},{7,6},{8,9},{9,8},{10,11... | collective-permute-start | bytes 811016 | tf_op jit(solution)/shard_map/ppermute | solution.py:301
  36.4 5.0 %collective-permute-start.4 = (bf16[256,256]{1,0:T(8,128)(2,1)S(1)}, bf16[256,256]{1,0:T(8,128)(2,1)S(1)}, u32[]{:S(2)}, u32[]{:S(2)}) collective-permute-start(bf16[256,256]{1,0:T(8,128)(2,1)S(1)} %fold.1), channel_id=1, source_target_pairs={{0,2},{1,5},{2,0},{3,7},{4,6},{5,1},{6,4},{7,3},{8,10},{9,13},{10,... | collective-permute-start | bytes 393224 | tf_op jit(solution)/shard_map/ppermute | solution.py:298

commit v4 on v3

--- a/solution.py
+++ b/solution.py
@@ -140,17 +140,95 @@
     return jnp.concatenate(found, axis=1) if width > 1 else found[0]
 
 
-def sort_kernel(mine, other, teacher, student, tags):
+def place_of(own, offset, count):
+    return lax.rem(own + (count - offset), count)
+
+
+def load_heads(heads, near, sems):
+    return [
+        pltpu.make_async_copy(heads[k], near.at[k - 1], sems.at[k - 1])
+        for k in range(1, len(heads))
+    ]
+
+
+def project(student, heads, near, copies, projected):
+    feat = lax.axis_index("feat")
+    part = projected.shape[1] // len(heads)
+    for offset in range(len(heads)):
+        if offset:
+            copies[offset - 1].wait()
+        weight = near[offset - 1] if offset else heads[0][...]
+        start = pl.multiple_of(place_of(feat, offset, len(heads)) * part, LANES)
+        projected[:, pl.ds(start, part)] = jnp.dot(
+            student, weight, preferred_element_type=jnp.float32
+        ).astype(jnp.bfloat16)
+
+
+def products(inputs, freqs, step):
+    return [
+        jnp.dot(
+            inputs[...], freqs[:, column : column + step], preferred_element_type=jnp.float32
+        )
+        for column in range(0, freqs.shape[1], step)
+    ]
+
+
+def is_role(role, index):
+    return (lax.axis_index("feat") if role is None else role) == index
+
+
+def first_kernel(role, n_feat, d_s, rows, *refs):
+    heads, (freqs, cos, sin, inputs, near, sems) = refs[:n_feat], refs[n_feat:]
+    is_student = is_role(role, 1)
+    copies = load_heads(heads, near, sems)
+    part = freqs.shape[0] // n_feat
+    own = pl.multiple_of(lax.axis_index("feat") * part, LANES)
+
+    @pl.when(is_student)
+    def _():
+        for copy in copies:
+            copy.start()
+        inputs[:, pl.ds(own, part)] = jnp.dot(
+            rows[:, :d_s], heads[0][...], preferred_element_type=jnp.float32
+        ).astype(jnp.bfloat16)
+
+    @pl.when(jnp.logical_not(is_student))
+    def _():
+        inputs[...] = rows[...]
+
+    step = min(freqs.shape[1], 256)
+    blocks = [slice(c, c + step) for c in range(0, freqs.shape[1], step)]
+    found = [0.0] * len(blocks)
+    for offset in range(n_feat):
+        start = pl.multiple_of(place_of(lax.axis_index("feat"), offset, n_feat) * part, LANES)
+        if offset:
+
+            @pl.when(is_student)
+            def _():
+                copies[offset - 1].wait()
+                inputs[:, pl.ds(start, part)] = jnp.dot(
+                    rows[:, :d_s], near[offset - 1], preferred_element_type=jnp.float32
+                ).astype(jnp.bfloat16)
+
+        for index, block in enumerate(blocks):
+            found[index] += jnp.dot(
+                inputs[:, pl.ds(start, part)],
+                freqs[pl.ds(start, part), block],
+                preferred_element_type=jnp.float32,
+            )
+    for index, block in enumerate(blocks):
+        cos[:, block], sin[:, block] = cos_sin(found[index])
+
+
+def sort_kernel(mine, other, student, tags):
     d_s = student.shape[1]
-    holds_student = lax.axis_index("feat") == 1
-
-    def split(first, second):
-        teacher[...] = first[...]
-        student[...] = second[:, :d_s]
-        tags[...] = second[:, d_s : d_s + LANES]
-
-    pl.when(holds_student)(lambda: split(other, mine))
-    pl.when(jnp.logical_not(holds_student))(lambda: split(mine, other))
+
+    def split(rows):
+        student[...] = rows[:, :d_s]
+        tags[...] = rows[:, d_s : d_s + LANES]
+
+    pl.when(is_role(None, 1))(lambda: split(mine))
+    pl.when(is_role(None, 0))(lambda: split(other))
 
 
 def member_of(group, bit, side):
@@ -159,21 +237,27 @@
     return jnp.where(bit == 0, low, high)
 
 
-def class_kernel(n_feat, n_dp, bits, cls_pad, permuted, teacher, student, tags_in, *refs):
+def class_kernel(
+    role, n_feat, n_dp, bits, cls_pad, permuted, other, student, tags_in, cos, sin, *refs
+):
     heads, freqs, refs = refs[:n_feat], refs[n_feat], refs[n_feat + 1 :]
     if permuted:
         weights, refs = refs[0], refs[1:]
-    grads, refs = refs[:n_feat], refs[n_feat:]
-    norms, projected, grad_z, picked, near, sems = refs
+    grads, refs = refs[: 2 * n_feat], refs[2 * n_feat :]
+    norms, inputs, grad_z, picked, near, sems = refs
     feat = lax.axis_index("feat")
     holder = lax.axis_index("dp")
-    copies = [
-        pltpu.make_async_copy(heads[k], near.at[k - 1], sems.at[k - 1]) for k in range(1, n_feat)
-    ]
-    for copy in copies:
-        copy.start()
-    slots, d_t = teacher.shape
+    mine_student = is_role(role, 1)
+    slots, d_t = inputs.shape
     half = freqs.shape[1]
+
+    copies = load_heads(heads, near, sems)
+
+    @pl.when(jnp.logical_not(mine_student))
+    def _():
+        for copy in copies:
+            copy.start()
+
     tags = tags_in[...].astype(jnp.float32)
     lane = lax.broadcasted_iota(jnp.int32, (slots, LANES), 1)
     tag = jnp.sum(
@@ -182,37 +266,32 @@
     tag_row = to_row(tag, slots)
     same = jnp.where(jnp.logical_and(tag == tag_row, tag > 0.0), 1.0, 0.0)
     inverse = 1.0 / jnp.maximum(jnp.sum(same, axis=1, keepdims=True), 1.0)
+    inverse = jnp.where(mine_student, -inverse, inverse)
     same = same.astype(jnp.bfloat16)
-    part = d_t // n_feat
-    for offset in range(n_feat):
-        if offset:
-            copies[offset - 1].wait()
-        weight = near[offset - 1] if offset else heads[0][...]
-        index = lax.rem(feat + (n_feat - offset), n_feat)
-        projected[:, pl.ds(pl.multiple_of(index * part, LANES), part)] = jnp.dot(
-            student[...], weight, preferred_element_type=jnp.float32
-        ).astype(jnp.bfloat16)
+
+    @pl.when(mine_student)
+    def _():
+        inputs[...] = other[...]
+
+    @pl.when(jnp.logical_not(mine_student))
+    def _():
+        project(student[...], heads, near, copies, inputs)
+
     step = min(half, 256)
-    blocks = [slice(column, column + step) for column in range(0, half, step)]
-    teacher_z = [
-        jnp.dot(teacher[...], freqs[:, block], preferred_element_type=jnp.float32)
-        for block in blocks
-    ]
-    student_z = [
-        jnp.dot(projected[...], freqs[:, block], preferred_element_type=jnp.float32)
-        for block in blocks
-    ]
     norm = jnp.zeros((slots, 1), jnp.float32)
-    for index, block in enumerate(blocks):
-        cos_s, sin_s = cos_sin(student_z[index])
-        cos_t, sin_t = cos_sin(teacher_z[index])
+    for index, z in enumerate(products(inputs, freqs, step)):
+        block = slice(index * step, (index + 1) * step)
+        cos_mine, sin_mine = cos[:, block], sin[:, block]
+        cos_other, sin_other = cos_sin(z)
         mean_c = inverse * jnp.dot(
-            same, (cos_s - cos_t).astype(jnp.bfloat16), preferred_element_type=jnp.float32
+            same, (cos_other - cos_mine).astype(jnp.bfloat16), preferred_element_type=jnp.float32
         )
         mean_s = inverse * jnp.dot(
-            same, (sin_s - sin_t).astype(jnp.bfloat16), preferred_element_type=jnp.float32
+            same, (sin_other - sin_mine).astype(jnp.bfloat16), preferred_element_type=jnp.float32
         )
         norm += jnp.sum(mean_c * mean_c + mean_s * mean_s, axis=1, keepdims=True)
+        cos_s = jnp.where(mine_student, cos_mine, cos_other)
+        sin_s = jnp.where(mine_student, sin_mine, sin_other)
         grad_z[:, block] = (cos_s * mean_s - sin_s * mean_c).astype(jnp.bfloat16)
     cls = lax.broadcasted_iota(jnp.int32, (slots, cls_pad), 1).astype(jnp.float32) + 1.0
     total_norm = jnp.sum(jnp.where(cls == tag, norm, 0.0), axis=0, keepdims=True)
@@ -234,30 +313,27 @@
                 picked[index * out_rows : (index + 1) * out_rows, :] = freqs[
                     pl.ds(start, out_rows), :
                 ]
-        out = grads[offset]
-        out[: 2 * block, :] = lax.dot_general(
+        product = lax.dot_general(
             picked[...], grad_z[...], (((1,), (1,)), ((), ())), preferred_element_type=jnp.float32
-        ).astype(out.dtype)
+        )
+        here, there = grads[offset], grads[n_feat + offset]
+        here[:block, :] = product[:block].astype(here.dtype)
+        there[...] = product[block:].astype(there.dtype)
         if offset:
-            out[2 * block :, :] = carried
-
-
-def summed(refs, start, size):
-    total = refs[0][start : start + size, :].astype(jnp.float32)
+            here[block:, :] = carried
+
+
+def summed(refs, size):
+    total = refs[0][:size, :].astype(jnp.float32)
     for ref in refs[1:]:
-        total += ref[start : start + size, :].astype(jnp.float32)
+        total += ref[:size, :].astype(jnp.float32)
     return total.astype(jnp.bfloat16)
-
-
-def fold_kernel(*refs):
-    size = refs[-1].shape[0]
-    refs[-1][...] = summed(refs[:-1], size, size)
 
 
 def own_kernel(scale, divisor, *refs):
     grads, (norms, student, head, loss) = refs[:-4], refs[-4:]
     head[...] = scale * jnp.dot(
-        summed(grads, 0, head.shape[0]), student[...], preferred_element_type=jnp.float32
+        summed(grads, head.shape[0]), student[...], preferred_element_type=jnp.float32
     )
     norm = norms[...]
     for ref in grads[1:]:
@@ -265,9 +341,16 @@
     loss[...] = (norm * (1.0 / divisor))[0, : loss.shape[0]]
 
 
-def head_kernel(scale, own, grads, student, head):
-    product = jnp.dot(grads[...], student[...], preferred_element_type=jnp.float32)
+def head_kernel(scale, *refs):
+    grads, (own, student, head) = refs[:-3], refs[-3:]
+    product = jnp.dot(
+        summed(grads, head.shape[0]), student[...], preferred_element_type=jnp.float32
+    )
     head[...] = (own[...] + product * scale).astype(jnp.bfloat16)
+
+
+def total_kernel(parts, out):
+    out[...] = jnp.sum(parts[...].astype(jnp.float32), axis=0)
 
 
 def on_device(teacher, student, head, freqs, labels, class_slot):
@@ -289,9 +372,9 @@
     hbm = pl.BlockSpec(memory_space=pltpu.HBM)
     near = pl.BlockSpec(memory_space=pltpu.VMEM)
 
-    def across(value):
+    def across(value, offset=0):
         moves = [
-            (d * n_feat + f, (d ^ (1 << f % bits)) * n_feat + f)
+            (d * n_feat + f, (d ^ (1 << (f + offset) % n_feat % bits)) * n_feat + (f + offset) % n_feat)
             for d in range(n_dp)
             for f in range(n_feat)
         ]
@@ -344,53 +427,64 @@
     mine = lax.all_to_all(
         sent.reshape(n_dp, capacity, width), "dp", split_axis=0, concat_axis=0, tiled=True
     ).reshape(slots, width)
+    role = None
     if n_feat == 2 and width == d_t:
-        teacher_in, student_in, tags_in = pl.pallas_call(
+        other = shifted(mine, 1)
+        student_in, tags_in = pl.pallas_call(
             sort_kernel,
             out_shape=(
-                jax.ShapeDtypeStruct((slots, d_t), jnp.bfloat16),
                 jax.ShapeDtypeStruct((slots, d_s), jnp.bfloat16),
                 jax.ShapeDtypeStruct((slots, LANES), jnp.bfloat16),
             ),
             compiler_params=vmem,
             name="sort",
-        )(mine, shifted(mine, 1))
+        )(mine, other)
     else:
+        role = 0
         everything = lax.all_gather(mine, "feat", axis=1, tiled=True)
-        teacher_in, student_in, tags_in = jnp.split(
+        mine, student_in, tags_in = jnp.split(
             everything[:, : d_t + d_s + LANES], [d_t, d_t + d_s], axis=1
         )
-    student_across = across(student_in)
+        other = mine
+    head_specs = [near] + [hbm] * (n_feat - 1)
+    head_scratch = [
+        pltpu.VMEM((n_feat - 1, *head.shape), jnp.bfloat16),
+        pltpu.SemaphoreType.DMA((n_feat - 1,)),
+    ]
+    cos, sin = pl.pallas_call(
+        functools.partial(first_kernel, role, n_feat, d_s),
+        out_shape=(jax.ShapeDtypeStruct((slots, half), jnp.float32),) * 2,
+        in_specs=[near] + head_specs + [near],
+        scratch_shapes=[pltpu.VMEM((slots, d_t), jnp.bfloat16), *head_scratch],
+        compiler_params=vmem,
+        name="first",
+    )(mine, *heads, freqs_near)
+    cos, student_out = lax.optimization_barrier((cos, student_in))
+    student_across = across(student_out)
     *grads, norms = pl.pallas_call(
-        functools.partial(class_kernel, n_feat, n_dp, bits, cls_pad, permuted),
+        functools.partial(class_kernel, role, n_feat, n_dp, bits, cls_pad, permuted),
         out_shape=tuple(
-            jax.ShapeDtypeStruct((2 * block + CARRIED, slots), jnp.bfloat16)
+            jax.ShapeDtypeStruct((block + CARRIED, slots), jnp.bfloat16)
             if k
-            else jax.ShapeDtypeStruct((2 * block, slots), jnp.float32)
+            else jax.ShapeDtypeStruct((block, slots), jnp.float32)
             for k in range(n_feat)
         )
+        + (jax.ShapeDtypeStruct((block, slots), jnp.bfloat16),) * n_feat
         + (jax.ShapeDtypeStruct((1, cls_pad), jnp.float32),),
-        in_specs=[near] * 4 + [hbm] * (n_feat - 1) + [near] * (1 + len(weights)),
+        in_specs=[near] * 5 + head_specs + [near] * (1 + len(weights)),
         scratch_shapes=[
             pltpu.VMEM((slots, d_t), jnp.bfloat16),
             pltpu.VMEM((slots, half), jnp.bfloat16),
             pltpu.VMEM((2 * block, half), jnp.bfloat16),
-            pltpu.VMEM((n_feat - 1, *head.shape), jnp.bfloat16),
-            pltpu.SemaphoreType.DMA((n_feat - 1,)),
+            *head_scratch,
         ],
         compiler_params=vmem,
         name="classes",
-    )(teacher_in, student_in, tags_in, *heads, freqs_near, *weights)
-    all_grads = [grads[0]] + [shifted(grads[k], k) for k in range(1, n_feat)]
-    all_grads, student_across = lax.optimization_barrier((all_grads, student_across))
+    )(other, student_in, tags_in, cos, sin, *heads, freqs_near, *weights)
+    here = [grads[0]] + [shifted(grads[k], k) for k in range(1, n_feat)]
+    there = [across(grads[n_feat + k], k) for k in range(n_feat)]
+    here, student_across = lax.optimization_barrier((here, student_across))
     scale = 1.0 / math.sqrt(images * n_dp)
-    folded = pl.pallas_call(
-        fold_kernel,
-        out_shape=jax.ShapeDtypeStruct((block, slots), jnp.bfloat16),
-        compiler_params=vmem,
-        name="fold",
-    )(*all_grads)
-    folded, all_grads = lax.optimization_barrier((folded, all_grads))
     own, loss = pl.pallas_call(
         functools.partial(own_kernel, scale, 2.0 * half * n_feat),
         out_shape=(
@@ -399,13 +493,13 @@
         ),
         compiler_params=vmem,
         name="own",
-    )(*all_grads, norms, student_in)
+    )(*here, norms, student_in)
     partial_head = pl.pallas_call(
         functools.partial(head_kernel, scale),
         out_shape=jax.ShapeDtypeStruct((block, d_s), jnp.bfloat16),
         compiler_params=vmem,
         name="head",
-    )(own, across(folded), student_across)
+    )(*there, own, student_across)
     received = lax.all_to_all(
         partial_head.reshape(n_dp // 2, out_rows, d_s),
         ("dp", "feat"),
@@ -418,7 +512,12 @@
             for side in range(2)
         ],
     )
-    head_grad = jnp.sum(received.astype(jnp.float32), axis=0)
+    head_grad = pl.pallas_call(
+        total_kernel,
+        out_shape=jax.ShapeDtypeStruct((out_rows, d_s), jnp.float32),
+        compiler_params=vmem,
+        name="total",
+    )(received)
     return (head_grad, loss)
 
 

time: 57.2 us -> 56.6 us (0.990)
  waiting for transfers between devices: 18.7 us -> 15.9 us
  Pallas kernels: 8.67 us -> 10.2 us
  starting transfers between devices: 10.2 us -> 11 us
  other arithmetic: 0.69 us -> 0 us
  blocking collectives: 14.4 us -> 15 us
    ppermute x3, waiting for transfers between devices: 3.24 us -> 0.24 us  [shifted(): lax.ppermute(value, 'feat', [(f, (f + offset) % n_feat) for f in range(n_...]
    pallas_call x3 -> x4, Pallas kernels: 5.04 us -> 6.6 us  [the longest x1 4.21 us: on_device(): pl.pallas_call(functools.partial(class_kernel, role, n_feat, n_dp, bits,...]
    reduce_sum x1 -> x0, other arithmetic: 0.69 us -> none  [on_device(): head_grad = jnp.sum(received.astype(jnp.float32), axis=0)]
    ppermute x2 -> x3, starting transfers between devices: 1.52 us -> 2.06 us  [across(): return lax.ppermute(value, ('dp', 'feat'), moves)]
    ppermute x2 -> x3, waiting for transfers between devices: 4.04 us -> 4.19 us  [across(): return lax.ppermute(value, ('dp', 'feat'), moves)]
  transfers between devices with their start and end apart: 6 -> 7, of which waited for: 5 -> 5; matrix products, arithmetic and copies ran while one was open for 0% -> 0% of each run, Pallas kernels for 11% -> 12%
where the time goes in v4:
time: 56.6 us; the launch traced here: 56.2 us
  waiting for transfers between devices  15.9 us (28%)
  blocking collectives  15 us (27%)
  starting transfers between devices  11 us (19%)
  Pallas kernels  10.2 us (18%)
  local copies, waits for them, and re-layouts  3.41 us (6%)
  between operations  0.71 us (1%)
    all_to_all x1, blocking collectives, on_device(): lax.all_to_all(partial_head.reshape(n_dp // 2, out_rows, d_s), ('dp', 'fe...  15 us
    all_to_all x1, waiting for transfers between devices, on_device(): lax.all_to_all(sent.reshape(n_dp, capacity, width), 'dp', split_axis=0, c...  11.4 us
    all_to_all x1, starting transfers between devices, on_device(): lax.all_to_all(sent.reshape(n_dp, capacity, width), 'dp', split_axis=0, c...  8.33 us
    pallas_call x1, Pallas kernels, on_device(): pl.pallas_call(functools.partial(class_kernel, role, n_feat, n_dp, bits,...  4.21 us
    ppermute x3, waiting for transfers between devices, across(): return lax.ppermute(value, ('dp', 'feat'), moves)  4.19 us
    unnamed x6, local copies, waits for them, and re-layouts  3.41 us
    pallas_call x1, Pallas kernels, on_device(): pl.pallas_call(functools.partial(route_kernel, cls_dev, capacity), out_sh...  2.39 us
    ppermute x3, starting transfers between devices, across(): return lax.ppermute(value, ('dp', 'feat'), moves)  2.06 us
  transfers between devices with their start and end apart: 7, of which 5 were waited for; matrix products, arithmetic and copies ran while one was open for 0% of the time, Pallas kernels for 12%

profile of v4, /device:TPU:0, one launch (start us, length us, event | category | flops | bytes accessed | tf_op | source)
XLA Modules:
  0.0 56.2 jit_solution(5409925898648106174)
XLA Ops:
  0.6 2.4 %route.1 = (bf16[256,1024]{1,0:T(8,128)(2,1)}, f32[8,128]{1,0:T(8,128)}) custom-call(s32[128]{0:T(128)} %labels_in.1, s32[5456]{0:T(1024)} %table_in.1, bf16[128,1024]{1,0:T(8,128)(2,1)} %teacher.1, bf16[128,768]{1,0:T(8,128)(2,1)} %student.1), custom_call_target="tpu_custom_call" | custom-call | tf_op jit(solution)/shard_map/route/pallas_call | solution.py:388
  3.0 8.3 %all-to-all-start = ((bf16[16,16,1024]{2,1,0:T(8,128)(2,1)}), bf16[16,16,1024]{2,1,0:T(8,128)(2,1)S(1)}, u32[]{:S(2)}, u32[]{:S(2)}) async-start(bf16[16,16,1024]{2,1,0:T(8,128)(2,1)} %bitcast.7), calls=%async_computation | async-start | bytes 1048576 | tf_op jit(solution)/shard_map/all_to_all | solution.py:427
  11.4 0.0 copy-start
  11.4 1.6 %copy-done = bf16[1024,1024]{1,0:T(8,128)(2,1)S(1)} copy-done((bf16[1024,1024]{1,0:T(8,128)(2,1)S(1)}, bf16[1024,1024]{1,0:T(8,128)(2,1)}, u32[]{:S(2)}) %copy-start) | copy-done | bytes 2097176
  13.0 1.1 %copy-done.1 = bf16[768,512]{1,0:T(8,128)(2,1)S(1)} copy-done((bf16[768,512]{1,0:T(8,128)(2,1)S(1)}, bf16[768,512]{1,0:T(8,128)(2,1)}, u32[]{:S(2)}) %copy-start.1) | copy-done | bytes 786456
  14.1 0.7 %copy-done.2 = f32[8,128]{1,0:T(8,128)S(1)} copy-done((f32[8,128]{1,0:T(8,128)S(1)}, f32[8,128]{1,0:T(8,128)}, u32[]{:S(2)}) %copy-start.2) | copy-done | bytes 4120
  14.8 0.2 load.1
  15.0 0.1 collective-permute-start.1
  15.1 11.4 %all-to-all-done = bf16[16,16,1024]{2,1,0:T(8,128)(2,1)S(1)} async-done(((bf16[16,16,1024]{2,1,0:T(8,128)(2,1)}), bf16[16,16,1024]{2,1,0:T(8,128)(2,1)S(1)}, u32[]{:S(2)}, u32[]{:S(2)}) %all-to-all-start) | async-done | bytes 524320 | tf_op jit(solution)/shard_map/all_to_all | solution.py:427
  26.5 0.0 collective-permute-start
  26.5 1.7 %first.1 = (f32[256,1024]{1,0:T(8,128)S(1)}, f32[256,1024]{1,0:T(8,128)S(1)}) custom-call(bf16[256,1024]{1,0:T(8,128)(2,1)S(1)} %bitcast.4, bf16[768,512]{1,0:T(8,128)(2,1)S(1)} %get-tuple-element.26.refs_0_, bf16[768,512]{1,0:T(8,128)(2,1)} %collective-permute-done.1.refs_1_, bf16[1024,1024]{1,0:T(8,128)(2,1)S(1)} %get-tuple-element.27.refs_2_), custom_call_target="tpu_custom_call" | custom-call | tf_op jit(solution)/shard_map/first/pallas_call | solution.py:454
  28.2 0.2 collective-permute-done.other
  28.5 0.6 %collective-permute-start.5 = (bf16[256,768]{1,0:T(8,128)(2,1)S(1)}, bf16[256,768]{1,0:T(8,128)(2,1)S(1)}, u32[]{:S(2)}, u32[]{:S(2)}) collective-permute-start(bf16[256,768]{1,0:T(8,128)(2,1)S(1)} %get-tuple-element.35.student.refs_3_), channel_id=1, source_target_pairs={{0,2},{1,5},{2,0},{3,7},{4,6},{5,1},{6,4},{7,3},{8,10},{9,13},{10,... | collective-permute-start | bytes 1179656 | tf_op jit(solution)/shard_map/ppermute | solution.py:381
  29.1 4.2 %classes.1 = (f32[256,256]{1,0:T(8,128)S(1)}, bf16[272,256]{1,0:T(8,128)(2,1)S(1)}, bf16[256,256]{1,0:T(8,128)(2,1)S(1)}, bf16[256,256]{1,0:T(8,128)(2,1)S(1)}, f32[1,512]{1,0:T(1,128)S(1)}) custom-call(bf16[256,1024]{1,0:T(8,128)(2,1)S(1)} %collective-permute-done.other, bf16[256,768]{1,0:T(8,128)(2,1)S(1)} %get-tuple-element.35.student.refs_3_, ...), custom_call_target="tpu_custom_call" | custom-call | tf_op jit(solution)/shard_map/classes/pallas_call | solution.py:464
  33.3 0.6 %collective-permute-start.4 = (bf16[272,256]{1,0:T(8,128)(2,1)S(1)}, bf16[272,256]{1,0:T(8,128)(2,1)S(1)}, u32[]{:S(2)}, u32[]{:S(2)}) collective-permute-start(bf16[272,256]{1,0:T(8,128)(2,1)S(1)} %get-tuple-element.34), channel_id=1, source_target_pairs={{0,1},{1,0},{2,3},{3,2},{4,5},{5,4},{6,7},{7,6},{8,9},{9,8},{10,11... | collective-permute-start | bytes 417800 | tf_op jit(solution)/shard_map/ppermute | solution.py:384
  33.9 1.0 %collective-permute-start.2 = (bf16[256,256]{1,0:T(8,128)(2,1)S(1)}, bf16[256,256]{1,0:T(8,128)(2,1)S(1)}, u32[]{:S(2)}, u32[]{:S(2)}) collective-permute-start(bf16[256,256]{1,0:T(8,128)(2,1)S(1)} %get-tuple-element.31), channel_id=1, source_target_pairs={{0,2},{1,5},{2,0},{3,7},{4,6},{5,1},{6,4},{7,3},{8,10},{9,13},{10,... | collective-permute-start | bytes 393224 | tf_op jit(solution)/shard_map/ppermute | solution.py:381
  34.9 0.4 collective-permute-start.3
  35.3 1.0 %collective-permute-done.5.refs_3_ = bf16[256,768]{1,0:T(8,128)(2,1)S(1)} collective-permute-done((bf16[256,768]{1,0:T(8,128)(2,1)S(1)}, bf16[256,768]{1,0:T(8,128)(2,1)S(1)}, u32[]{:S(2)}, u32[]{:S(2)}) %collective-permute-start.5) | collective-permute-done | bytes 393248 | tf_op jit(solution)/shard_map/ppermute | solution.py:381
  36.3 0.7 %own.1 = (f32[256,768]{1,0:T(8,128)S(1)}, f32[341]{0:T(512)}) custom-call(f32[256,256]{1,0:T(8,128)S(1)} %get-tuple-element.36.refs_0_, bf16[272,256]{1,0:T(8,128)(2,1)S(1)} %collective-permute-done.4.refs_1_, f32[1,512]{1,0:T(1,128)S(1)} %get-tuple-element.38.refs_2_, bf16[256,768]{1,0:T(8,128)(2,1)S(1)} %get-tuple-element.35.student.refs_3_), custom_call_target="tpu_custom_call" | custom-call | tf_op jit(solution)/shard_map/own/pallas_call | solution.py:488
  37.0 2.8 %collective-permute-done.2.refs_0_ = bf16[256,256]{1,0:T(8,128)(2,1)S(1)} collective-permute-done((bf16[256,256]{1,0:T(8,128)(2,1)S(1)}, bf16[256,256]{1,0:T(8,128)(2,1)S(1)}, u32[]{:S(2)}, u32[]{:S(2)}) %collective-permute-start.2) | collective-permute-done | bytes 131104 | tf_op jit(solution)/shard_map/ppermute | solution.py:381
  39.8 0.4 collective-permute-done.3.refs_1_
  40.2 0.3 head.1
  40.5 15.0 %all_to_all.10.parts = bf16[8,32,768]{2,1,0:T(8,128)(2,1)S(1)} all-to-all(bf16[8,32,768]{2,1,0:T(8,128)(2,1)S(1)} %bitcast.6), channel_id=1, replica_groups={{0,4,8,12,16,20,24,28},{2,6,10,14,18,22,26,30},{1,3,9,11,17,19,25,27},{..., dimensions={0} | all-to-all | bytes 786432 | tf_op jit(solution)/shard_map/all_to_all | solution.py:503
  55.5 0.7 %total.1 = f32[32,768]{1,0:T(8,128)} custom-call(bf16[8,32,768]{2,1,0:T(8,128)(2,1)S(1)} %all_to_all.10.parts), custom_call_target="tpu_custom_call" | custom-call | tf_op jit(solution)/shard_map/total/pallas_call | solution.py:515
  (5 shorter events, 0.1 us)
Async XLA Ops:
  3.0 23.5 %all-to-all-start = ((bf16[16,16,1024]{2,1,0:T(8,128)(2,1)}), bf16[16,16,1024]{2,1,0:T(8,128)(2,1)S(1)}, u32[]{:S(2)}, u32[]{:S(2)}) async-start(bf16[16,16,1024]{2,1,0:T(8,128)(2,1)} %bitcast.7), calls=%async_computation | async-start | bytes 1048576 | tf_op jit(solution)/shard_map/all_to_all | solution.py:427
  11.4 1.6 %copy-start = (bf16[1024,1024]{1,0:T(8,128)(2,1)S(1)}, bf16[1024,1024]{1,0:T(8,128)(2,1)}, u32[]{:S(2)}) copy-start(bf16[1024,1024]{1,0:T(8,128)(2,1)} %freqs_in.1) | copy-start | bytes 6291460
  13.0 1.1 %copy-start.1 = (bf16[768,512]{1,0:T(8,128)(2,1)S(1)}, bf16[768,512]{1,0:T(8,128)(2,1)}, u32[]{:S(2)}) copy-start(bf16[768,512]{1,0:T(8,128)(2,1)} %head_in.1) | copy-start | bytes 2359300
  14.1 0.7 %copy-start.2 = (f32[8,128]{1,0:T(8,128)S(1)}, f32[8,128]{1,0:T(8,128)}, u32[]{:S(2)}) copy-start(f32[8,128]{1,0:T(8,128)} %get-tuple-element.25._) | copy-start | bytes 12292
  15.0 11.5 %collective-permute-start.1 = (bf16[768,512]{1,0:T(8,128)(2,1)S(1)}, bf16[768,512]{1,0:T(8,128)(2,1)}, u32[]{:S(2)}, u32[]{:S(2)}) collective-permute-start(bf16[768,512]{1,0:T(8,128)(2,1)S(1)} %get-tuple-element.26.refs_0_), channel_id=1, source_target_pairs={{0,1},{1,0},{2,3},{3,2},{4,5},{5,4},{6,7},{7,6},{8,9},{9,8},{10,11... | collective-permute-start | bytes 2359304 | tf_op jit(solution)/shard_map/ppermute | solution.py:384
  26.5 1.9 %collective-permute-start = (bf16[256,1024]{1,0:T(8,128)(2,1)S(1)}, bf16[256,1024]{1,0:T(8,128)(2,1)S(1)}, u32[]{:S(2)}, u32[]{:S(2)}) collective-permute-start(bf16[256,1024]{1,0:T(8,128)(2,1)S(1)} %bitcast.3), channel_id=1, source_target_pairs={{0,1},{1,0},{2,3},{3,2},{4,5},{5,4},{6,7},{7,6},{8,9},{9,8},{10,11... | collective-permute-start | bytes 1572872 | tf_op jit(solution)/shard_map/ppermute | solution.py:384
  28.5 7.8 %collective-permute-start.5 = (bf16[256,768]{1,0:T(8,128)(2,1)S(1)}, bf16[256,768]{1,0:T(8,128)(2,1)S(1)}, u32[]{:S(2)}, u32[]{:S(2)}) collective-permute-start(bf16[256,768]{1,0:T(8,128)(2,1)S(1)} %get-tuple-element.35.student.refs_3_), channel_id=1, source_target_pairs={{0,2},{1,5},{2,0},{3,7},{4,6},{5,1},{6,4},{7,3},{8,10},{9,13},{10,... | collective-permute-start | bytes 1179656 | tf_op jit(solution)/shard_map/ppermute | solution.py:381
  33.3 2.0 %collective-permute-start.4 = (bf16[272,256]{1,0:T(8,128)(2,1)S(1)}, bf16[272,256]{1,0:T(8,128)(2,1)S(1)}, u32[]{:S(2)}, u32[]{:S(2)}) collective-permute-start(bf16[272,256]{1,0:T(8,128)(2,1)S(1)} %get-tuple-element.34), channel_id=1, source_target_pairs={{0,1},{1,0},{2,3},{3,2},{4,5},{5,4},{6,7},{7,6},{8,9},{9,8},{10,11... | collective-permute-start | bytes 417800 | tf_op jit(solution)/shard_map/ppermute | solution.py:384
  33.9 6.0 %collective-permute-start.2 = (bf16[256,256]{1,0:T(8,128)(2,1)S(1)}, bf16[256,256]{1,0:T(8,128)(2,1)S(1)}, u32[]{:S(2)}, u32[]{:S(2)}) collective-permute-start(bf16[256,256]{1,0:T(8,128)(2,1)S(1)} %get-tuple-element.31), channel_id=1, source_target_pairs={{0,2},{1,5},{2,0},{3,7},{4,6},{5,1},{6,4},{7,3},{8,10},{9,13},{10,... | collective-permute-start | bytes 393224 | tf_op jit(solution)/shard_map/ppermute | solution.py:381
  34.9 5.3 %collective-permute-start.3 = (bf16[256,256]{1,0:T(8,128)(2,1)S(1)}, bf16[256,256]{1,0:T(8,128)(2,1)S(1)}, u32[]{:S(2)}, u32[]{:S(2)}) collective-permute-start(bf16[256,256]{1,0:T(8,128)(2,1)S(1)} %get-tuple-element.32), channel_id=1, source_target_pairs={{0,5},{1,2},{2,7},{3,0},{4,1},{5,6},{6,3},{7,4},{8,13},{9,10},{10,... | collective-permute-start | bytes 393224 | tf_op jit(solution)/shard_map/ppermute | solution.py:381

commit v5 on v4

--- a/solution.py
+++ b/solution.py
@@ -144,21 +144,13 @@
     return lax.rem(own + (count - offset), count)
 
 
-def load_heads(heads, near, sems):
-    return [
-        pltpu.make_async_copy(heads[k], near.at[k - 1], sems.at[k - 1])
-        for k in range(1, len(heads))
-    ]
-
-
-def project(student, heads, near, copies, projected):
+def project(student, head, others, projected):
     feat = lax.axis_index("feat")
-    part = projected.shape[1] // len(heads)
-    for offset in range(len(heads)):
-        if offset:
-            copies[offset - 1].wait()
-        weight = near[offset - 1] if offset else heads[0][...]
-        start = pl.multiple_of(place_of(feat, offset, len(heads)) * part, LANES)
+    part = head.shape[1]
+    count = projected.shape[1] // part
+    for offset in range(count):
+        weight = others[offset - 1] if offset else head[...]
+        start = pl.multiple_of(place_of(feat, offset, count) * part, LANES)
         projected[:, pl.ds(start, part)] = jnp.dot(
             student, weight, preferred_element_type=jnp.float32
         ).astype(jnp.bfloat16)
@@ -178,16 +170,18 @@
 
 
 def first_kernel(role, n_feat, d_s, rows, *refs):
-    heads, (freqs, cos, sin, inputs, near, sems) = refs[:n_feat], refs[n_feat:]
+    heads, (freqs, cos, sin, near, inputs, sems) = refs[:n_feat], refs[n_feat:]
     is_student = is_role(role, 1)
-    copies = load_heads(heads, near, sems)
+    copies = [
+        pltpu.make_async_copy(heads[k], near.at[k - 1], sems.at[k - 1]) for k in range(1, n_feat)
+    ]
+    for copy in copies:
+        copy.start()
     part = freqs.shape[0] // n_feat
     own = pl.multiple_of(lax.axis_index("feat") * part, LANES)
 
     @pl.when(is_student)
     def _():
-        for copy in copies:
-            copy.start()
         inputs[:, pl.ds(own, part)] = jnp.dot(
             rows[:, :d_s], heads[0][...], preferred_element_type=jnp.float32
         ).astype(jnp.bfloat16)
@@ -219,6 +213,11 @@
     for index, block in enumerate(blocks):
         cos[:, block], sin[:, block] = cos_sin(found[index])
 
+    @pl.when(jnp.logical_not(is_student))
+    def _():
+        for copy in copies:
+            copy.wait()
+
 
 def sort_kernel(mine, other, student, tags):
     d_s = student.shape[1]
@@ -240,24 +239,17 @@
 def class_kernel(
     role, n_feat, n_dp, bits, cls_pad, permuted, other, student, tags_in, cos, sin, *refs
 ):
-    heads, freqs, refs = refs[:n_feat], refs[n_feat], refs[n_feat + 1 :]
+    head, others, freqs, refs = refs[0], refs[1], refs[2], refs[3:]
     if permuted:
         weights, refs = refs[0], refs[1:]
     grads, refs = refs[: 2 * n_feat], refs[2 * n_feat :]
-    norms, inputs, grad_z, picked, near, sems = refs
+    norms, inputs, grad_z, picked = refs
     feat = lax.axis_index("feat")
     holder = lax.axis_index("dp")
     mine_student = is_role(role, 1)
     slots, d_t = inputs.shape
     half = freqs.shape[1]
 
-    copies = load_heads(heads, near, sems)
-
-    @pl.when(jnp.logical_not(mine_student))
-    def _():
-        for copy in copies:
-            copy.start()
-
     tags = tags_in[...].astype(jnp.float32)
     lane = lax.broadcasted_iota(jnp.int32, (slots, LANES), 1)
     tag = jnp.sum(
@@ -275,7 +267,7 @@
 
     @pl.when(jnp.logical_not(mine_student))
     def _():
-        project(student[...], heads, near, copies, inputs)
+        project(student[...], head, others, inputs)
 
     step = min(half, 256)
     norm = jnp.zeros((slots, 1), jnp.float32)
@@ -328,6 +320,10 @@
     for ref in refs[1:]:
         total += ref[:size, :].astype(jnp.float32)
     return total.astype(jnp.bfloat16)
+
+
+def fold_kernel(*refs):
+    refs[-1][...] = summed(refs[:-1], refs[-1].shape[0])
 
 
 def own_kernel(scale, divisor, *refs):
@@ -446,16 +442,15 @@
             everything[:, : d_t + d_s + LANES], [d_t, d_t + d_s], axis=1
         )
         other = mine
-    head_specs = [near] + [hbm] * (n_feat - 1)
-    head_scratch = [
-        pltpu.VMEM((n_feat - 1, *head.shape), jnp.bfloat16),
-        pltpu.SemaphoreType.DMA((n_feat - 1,)),
-    ]
-    cos, sin = pl.pallas_call(
+    cos, sin, head_others = pl.pallas_call(
         functools.partial(first_kernel, role, n_feat, d_s),
-        out_shape=(jax.ShapeDtypeStruct((slots, half), jnp.float32),) * 2,
-        in_specs=[near] + head_specs + [near],
-        scratch_shapes=[pltpu.VMEM((slots, d_t), jnp.bfloat16), *head_scratch],
+        out_shape=(jax.ShapeDtypeStruct((slots, half), jnp.float32),) * 2
+        + (jax.ShapeDtypeStruct((n_feat - 1, *head.shape), jnp.bfloat16),),
+        in_specs=[near] * 2 + [hbm] * (n_feat - 1) + [near],
+        scratch_shapes=[
+            pltpu.VMEM((slots, d_t), jnp.bfloat16),
+            pltpu.SemaphoreType.DMA((n_feat - 1,)),
+        ],
         compiler_params=vmem,
         name="first",
     )(mine, *heads, freqs_near)
@@ -469,20 +464,31 @@
             else jax.ShapeDtypeStruct((block, slots), jnp.float32)
             for k in range(n_feat)
         )
-        + (jax.ShapeDtypeStruct((block, slots), jnp.bfloat16),) * n_feat
+        + tuple(
+            jax.ShapeDtypeStruct((block, slots), jnp.bfloat16 if k else jnp.float32)
+            for k in range(n_feat)
+        )
         + (jax.ShapeDtypeStruct((1, cls_pad), jnp.float32),),
-        in_specs=[near] * 5 + head_specs + [near] * (1 + len(weights)),
+        in_specs=[near] * (8 + len(weights)),
         scratch_shapes=[
             pltpu.VMEM((slots, d_t), jnp.bfloat16),
             pltpu.VMEM((slots, half), jnp.bfloat16),
             pltpu.VMEM((2 * block, half), jnp.bfloat16),
-            *head_scratch,
         ],
         compiler_params=vmem,
         name="classes",
-    )(other, student_in, tags_in, cos, sin, *heads, freqs_near, *weights)
+    )(
+        other, student_in, tags_in, cos, sin, heads[0], head_others, freqs_near, *weights
+    )
     here = [grads[0]] + [shifted(grads[k], k) for k in range(1, n_feat)]
-    there = [across(grads[n_feat + k], k) for k in range(n_feat)]
+    there = [grads[n_feat]] + [shifted(grads[n_feat + k], k) for k in range(1, n_feat)]
+    folded = pl.pallas_call(
+        fold_kernel,
+        out_shape=jax.ShapeDtypeStruct((block, slots), jnp.bfloat16),
+        compiler_params=vmem,
+        name="fold",
+    )(*there)
+    there = [across(folded)]
     here, student_across = lax.optimization_barrier((here, student_across))
     scale = 1.0 / math.sqrt(images * n_dp)
     own, loss = pl.pallas_call(

time: 56.6 us -> 55.8 us (0.986)
  Pallas kernels: 10.2 us -> 9.54 us
    ppermute x3 -> x4, waiting for transfers between devices: 0.24 us -> 1.15 us  [shifted(): lax.ppermute(value, 'feat', [(f, (f + offset) % n_feat) for f in range(n_...]
    ppermute x3 -> x4, starting transfers between devices: 0.64 us -> 1.41 us  [shifted(): lax.ppermute(value, 'feat', [(f, (f + offset) % n_feat) for f in range(n_...]
    ppermute x3 -> x2, starting transfers between devices: 2.06 us -> 1.32 us  [across(): return lax.ppermute(value, ('dp', 'feat'), moves)]
    pallas_call x1, Pallas kernels: 4.21 us -> 3.5 us  [on_device(): pl.pallas_call(functools.partial(class_kernel, role, n_feat, n_dp, bits,...]
    ppermute x3 -> x2, waiting for transfers between devices: 4.19 us -> 3.59 us  [across(): return lax.ppermute(value, ('dp', 'feat'), moves)]
  transfers between devices with their start and end apart: 7 -> 7, of which waited for: 5 -> 5; matrix products, arithmetic and copies ran while one was open for 0% -> 0% of each run, Pallas kernels for 12% -> 11%
where the time goes in v5:
time: 55.8 us; the launch traced here: 55.4 us
  waiting for transfers between devices  16.2 us (29%)
  blocking collectives  14.6 us (26%)
  starting transfers between devices  11.1 us (20%)
  Pallas kernels  9.54 us (17%)
  local copies, waits for them, and re-layouts  3.41 us (6%)
  between operations  0.71 us (1%)
    all_to_all x1, blocking collectives, on_device(): lax.all_to_all(partial_head.reshape(n_dp // 2, out_rows, d_s), ('dp', 'fe...  14.6 us
    all_to_all x1, waiting for transfers between devices, on_device(): lax.all_to_all(sent.reshape(n_dp, capacity, width), 'dp', split_axis=0, c...  11.4 us
    all_to_all x1, starting transfers between devices, on_device(): lax.all_to_all(sent.reshape(n_dp, capacity, width), 'dp', split_axis=0, c...  8.33 us
    ppermute x2, waiting for transfers between devices, across(): return lax.ppermute(value, ('dp', 'feat'), moves)  3.59 us
    pallas_call x1, Pallas kernels, on_device(): pl.pallas_call(functools.partial(class_kernel, role, n_feat, n_dp, bits,...  3.5 us
    unnamed x6, local copies, waits for them, and re-layouts  3.41 us
    pallas_call x1, Pallas kernels, on_device(): pl.pallas_call(functools.partial(route_kernel, cls_dev, capacity), out_sh...  2.39 us
    pallas_call x1, Pallas kernels, on_device(): pl.pallas_call(functools.partial(first_kernel, role, n_feat, d_s), out_sh...  1.66 us
  transfers between devices with their start and end apart: 7, of which 5 were waited for; matrix products, arithmetic and copies ran while one was open for 0% of the time, Pallas kernels for 11%

profile of v5, /device:TPU:0, one launch (start us, length us, event | category | flops | bytes accessed | tf_op | source)
XLA Modules:
  0.0 55.4 jit_solution(1084162462552919738)
XLA Ops:
  0.6 2.4 %route.1 = (bf16[256,1024]{1,0:T(8,128)(2,1)}, f32[8,128]{1,0:T(8,128)}) custom-call(s32[128]{0:T(128)} %labels_in.1, s32[5456]{0:T(1024)} %table_in.1, bf16[128,1024]{1,0:T(8,128)(2,1)} %teacher.1, bf16[128,768]{1,0:T(8,128)(2,1)} %student.1), custom_call_target="tpu_custom_call" | custom-call | tf_op jit(solution)/shard_map/route/pallas_call | solution.py:384
  3.0 8.3 %all-to-all-start = ((bf16[16,16,1024]{2,1,0:T(8,128)(2,1)}), bf16[16,16,1024]{2,1,0:T(8,128)(2,1)S(1)}, u32[]{:S(2)}, u32[]{:S(2)}) async-start(bf16[16,16,1024]{2,1,0:T(8,128)(2,1)} %bitcast.7), calls=%async_computation | async-start | bytes 1048576 | tf_op jit(solution)/shard_map/all_to_all | solution.py:423
  11.4 0.0 copy-start
  11.4 1.6 %copy-done = bf16[1024,1024]{1,0:T(8,128)(2,1)S(1)} copy-done((bf16[1024,1024]{1,0:T(8,128)(2,1)S(1)}, bf16[1024,1024]{1,0:T(8,128)(2,1)}, u32[]{:S(2)}) %copy-start) | copy-done | bytes 2097176
  13.0 1.1 %copy-done.1 = bf16[768,512]{1,0:T(8,128)(2,1)S(1)} copy-done((bf16[768,512]{1,0:T(8,128)(2,1)S(1)}, bf16[768,512]{1,0:T(8,128)(2,1)}, u32[]{:S(2)}) %copy-start.1) | copy-done | bytes 786456
  14.1 0.7 %copy-done.2 = f32[8,128]{1,0:T(8,128)S(1)} copy-done((f32[8,128]{1,0:T(8,128)S(1)}, f32[8,128]{1,0:T(8,128)}, u32[]{:S(2)}) %copy-start.2) | copy-done | bytes 4120
  14.8 0.2 load.1
  15.0 0.1 collective-permute-start.1
  15.1 11.4 %all-to-all-done = bf16[16,16,1024]{2,1,0:T(8,128)(2,1)S(1)} async-done(((bf16[16,16,1024]{2,1,0:T(8,128)(2,1)}), bf16[16,16,1024]{2,1,0:T(8,128)(2,1)S(1)}, u32[]{:S(2)}, u32[]{:S(2)}) %all-to-all-start) | async-done | bytes 524320 | tf_op jit(solution)/shard_map/all_to_all | solution.py:423
  26.5 0.0 collective-permute-start
  26.5 1.7 %first.1 = (f32[256,1024]{1,0:T(8,128)S(1)}, f32[256,1024]{1,0:T(8,128)S(1)}, bf16[1,768,512]{2,1,0:T(8,128)(2,1)S(1)}) custom-call(bf16[256,1024]{1,0:T(8,128)(2,1)S(1)} %bitcast.4, bf16[768,512]{1,0:T(8,128)(2,1)S(1)} %get-tuple-element.27.refs_0_, bf16[768,512]{1,0:T(8,128)(2,1)} %collective-permute-done.1.refs_1_, ...), custom_call_target="tpu_custom_call" | custom-call | tf_op jit(solution)/shard_map/first/pallas_call | solution.py:445
  28.2 0.2 collective-permute-done.other
  28.5 0.6 %collective-permute-start.5 = (bf16[256,768]{1,0:T(8,128)(2,1)S(1)}, bf16[256,768]{1,0:T(8,128)(2,1)S(1)}, u32[]{:S(2)}, u32[]{:S(2)}) collective-permute-start(bf16[256,768]{1,0:T(8,128)(2,1)S(1)} %get-tuple-element.37.student.refs_3_), channel_id=1, source_target_pairs={{0,2},{1,5},{2,0},{3,7},{4,6},{5,1},{6,4},{7,3},{8,10},{9,13},{10,... | collective-permute-start | bytes 1179656 | tf_op jit(solution)/shard_map/ppermute | solution.py:377
  29.1 3.5 %classes.1 = (f32[256,256]{1,0:T(8,128)S(1)}, bf16[272,256]{1,0:T(8,128)(2,1)S(1)}, f32[256,256]{1,0:T(8,128)S(1)}, bf16[256,256]{1,0:T(8,128)(2,1)S(1)}, f32[1,512]{1,0:T(1,128)S(1)}) custom-call(bf16[256,1024]{1,0:T(8,128)(2,1)S(1)} %collective-permute-done.other, bf16[256,768]{1,0:T(8,128)(2,1)S(1)} %get-tuple-element.37.student.refs_3_, ...), custom_call_target="tpu_custom_call" | custom-call | tf_op jit(solution)/shard_map/classes/pallas_call | solution.py:459
  32.6 1.3 %collective-permute-start.2 = (bf16[256,256]{1,0:T(8,128)(2,1)S(1)}, bf16[256,256]{1,0:T(8,128)(2,1)S(1)}, u32[]{:S(2)}, u32[]{:S(2)}) collective-permute-start(bf16[256,256]{1,0:T(8,128)(2,1)S(1)} %get-tuple-element.34), channel_id=1, source_target_pairs={{0,1},{1,0},{2,3},{3,2},{4,5},{5,4},{6,7},{7,6},{8,9},{9,8},{10,11... | collective-permute-start | bytes 393224 | tf_op jit(solution)/shard_map/ppermute | solution.py:380
  33.8 0.1 collective-permute-start.4
  33.9 0.9 %collective-permute-done.2.refs_1_ = bf16[256,256]{1,0:T(8,128)(2,1)S(1)} collective-permute-done((bf16[256,256]{1,0:T(8,128)(2,1)S(1)}, bf16[256,256]{1,0:T(8,128)(2,1)S(1)}, u32[]{:S(2)}, u32[]{:S(2)}) %collective-permute-start.2) | collective-permute-done | bytes 131104 | tf_op jit(solution)/shard_map/ppermute | solution.py:380
  34.9 0.7 %collective-permute-start.3 = (bf16[256,256]{1,0:T(8,128)(2,1)S(1)}, bf16[256,256]{1,0:T(8,128)(2,1)S(1)}, u32[]{:S(2)}, u32[]{:S(2)}) collective-permute-start(bf16[256,256]{1,0:T(8,128)(2,1)S(1)} %fold.1), channel_id=1, source_target_pairs={{0,2},{1,5},{2,0},{3,7},{4,6},{5,1},{6,4},{7,3},{8,10},{9,13},{10,... | collective-permute-start | bytes 393224 | tf_op jit(solution)/shard_map/ppermute | solution.py:377
  35.5 0.7 %collective-permute-done.5.refs_2_ = bf16[256,768]{1,0:T(8,128)(2,1)S(1)} collective-permute-done((bf16[256,768]{1,0:T(8,128)(2,1)S(1)}, bf16[256,768]{1,0:T(8,128)(2,1)S(1)}, u32[]{:S(2)}, u32[]{:S(2)}) %collective-permute-start.5) | collective-permute-done | bytes 393248 | tf_op jit(solution)/shard_map/ppermute | solution.py:377
  36.3 0.8 %own.1 = (f32[256,768]{1,0:T(8,128)S(1)}, f32[341]{0:T(512)}) custom-call(f32[256,256]{1,0:T(8,128)S(1)} %get-tuple-element.38.refs_0_, bf16[272,256]{1,0:T(8,128)(2,1)S(1)} %collective-permute-done.4.refs_1_, f32[1,512]{1,0:T(1,128)S(1)} %get-tuple-element.40.refs_2_, bf16[256,768]{1,0:T(8,128)(2,1)S(1)} %get-tuple-element.37.student.refs_3_), custom_call_target="tpu_custom_call" | custom-call | tf_op jit(solution)/shard_map/own/pallas_call | solution.py:494
  37.0 2.8 %collective-permute-done.3.refs_0_ = bf16[256,256]{1,0:T(8,128)(2,1)S(1)} collective-permute-done((bf16[256,256]{1,0:T(8,128)(2,1)S(1)}, bf16[256,256]{1,0:T(8,128)(2,1)S(1)}, u32[]{:S(2)}, u32[]{:S(2)}) %collective-permute-start.3) | collective-permute-done | bytes 131104 | tf_op jit(solution)/shard_map/ppermute | solution.py:377
  39.9 0.3 head.1
  40.2 14.6 %all_to_all.10.parts = bf16[8,32,768]{2,1,0:T(8,128)(2,1)S(1)} all-to-all(bf16[8,32,768]{2,1,0:T(8,128)(2,1)S(1)} %bitcast.6), channel_id=1, replica_groups={{0,4,8,12,16,20,24,28},{2,6,10,14,18,22,26,30},{1,3,9,11,17,19,25,27},{..., dimensions={0} | all-to-all | bytes 786432 | tf_op jit(solution)/shard_map/all_to_all | solution.py:509
  54.7 0.7 %total.1 = f32[32,768]{1,0:T(8,128)} custom-call(bf16[8,32,768]{2,1,0:T(8,128)(2,1)S(1)} %all_to_all.10.parts), custom_call_target="tpu_custom_call" | custom-call | tf_op jit(solution)/shard_map/total/pallas_call | solution.py:521
  (6 shorter events, 0.1 us)
Async XLA Ops:
  3.0 23.5 %all-to-all-start = ((bf16[16,16,1024]{2,1,0:T(8,128)(2,1)}), bf16[16,16,1024]{2,1,0:T(8,128)(2,1)S(1)}, u32[]{:S(2)}, u32[]{:S(2)}) async-start(bf16[16,16,1024]{2,1,0:T(8,128)(2,1)} %bitcast.7), calls=%async_computation | async-start | bytes 1048576 | tf_op jit(solution)/shard_map/all_to_all | solution.py:423
  11.4 1.6 %copy-start = (bf16[1024,1024]{1,0:T(8,128)(2,1)S(1)}, bf16[1024,1024]{1,0:T(8,128)(2,1)}, u32[]{:S(2)}) copy-start(bf16[1024,1024]{1,0:T(8,128)(2,1)} %freqs_in.1) | copy-start | bytes 6291460
  13.0 1.1 %copy-start.1 = (bf16[768,512]{1,0:T(8,128)(2,1)S(1)}, bf16[768,512]{1,0:T(8,128)(2,1)}, u32[]{:S(2)}) copy-start(bf16[768,512]{1,0:T(8,128)(2,1)} %head_in.1) | copy-start | bytes 2359300
  14.1 0.7 %copy-start.2 = (f32[8,128]{1,0:T(8,128)S(1)}, f32[8,128]{1,0:T(8,128)}, u32[]{:S(2)}) copy-start(f32[8,128]{1,0:T(8,128)} %get-tuple-element.26._) | copy-start | bytes 12292
  15.0 11.5 %collective-permute-start.1 = (bf16[768,512]{1,0:T(8,128)(2,1)S(1)}, bf16[768,512]{1,0:T(8,128)(2,1)}, u32[]{:S(2)}, u32[]{:S(2)}) collective-permute-start(bf16[768,512]{1,0:T(8,128)(2,1)S(1)} %get-tuple-element.27.refs_0_), channel_id=1, source_target_pairs={{0,1},{1,0},{2,3},{3,2},{4,5},{5,4},{6,7},{7,6},{8,9},{9,8},{10,11... | collective-permute-start | bytes 2359304 | tf_op jit(solution)/shard_map/ppermute | solution.py:380
  26.5 1.9 %collective-permute-start = (bf16[256,1024]{1,0:T(8,128)(2,1)S(1)}, bf16[256,1024]{1,0:T(8,128)(2,1)S(1)}, u32[]{:S(2)}, u32[]{:S(2)}) collective-permute-start(bf16[256,1024]{1,0:T(8,128)(2,1)S(1)} %bitcast.3), channel_id=1, source_target_pairs={{0,1},{1,0},{2,3},{3,2},{4,5},{5,4},{6,7},{7,6},{8,9},{9,8},{10,11... | collective-permute-start | bytes 1572872 | tf_op jit(solution)/shard_map/ppermute | solution.py:380
  28.5 7.8 %collective-permute-start.5 = (bf16[256,768]{1,0:T(8,128)(2,1)S(1)}, bf16[256,768]{1,0:T(8,128)(2,1)S(1)}, u32[]{:S(2)}, u32[]{:S(2)}) collective-permute-start(bf16[256,768]{1,0:T(8,128)(2,1)S(1)} %get-tuple-element.37.student.refs_3_), channel_id=1, source_target_pairs={{0,2},{1,5},{2,0},{3,7},{4,6},{5,1},{6,4},{7,3},{8,10},{9,13},{10,... | collective-permute-start | bytes 1179656 | tf_op jit(solution)/shard_map/ppermute | solution.py:377
  32.6 2.2 %collective-permute-start.2 = (bf16[256,256]{1,0:T(8,128)(2,1)S(1)}, bf16[256,256]{1,0:T(8,128)(2,1)S(1)}, u32[]{:S(2)}, u32[]{:S(2)}) collective-permute-start(bf16[256,256]{1,0:T(8,128)(2,1)S(1)} %get-tuple-element.34), channel_id=1, source_target_pairs={{0,1},{1,0},{2,3},{3,2},{4,5},{5,4},{6,7},{7,6},{8,9},{9,8},{10,11... | collective-permute-start | bytes 393224 | tf_op jit(solution)/shard_map/ppermute | solution.py:380
  33.8 1.7 %collective-permute-start.4 = (bf16[272,256]{1,0:T(8,128)(2,1)S(1)}, bf16[272,256]{1,0:T(8,128)(2,1)S(1)}, u32[]{:S(2)}, u32[]{:S(2)}) collective-permute-start(bf16[272,256]{1,0:T(8,128)(2,1)S(1)} %get-tuple-element.36), channel_id=1, source_target_pairs={{0,1},{1,0},{2,3},{3,2},{4,5},{5,4},{6,7},{7,6},{8,9},{9,8},{10,11... | collective-permute-start | bytes 417800 | tf_op jit(solution)/shard_map/ppermute | solution.py:380
  34.9 5.0 %collective-permute-start.3 = (bf16[256,256]{1,0:T(8,128)(2,1)S(1)}, bf16[256,256]{1,0:T(8,128)(2,1)S(1)}, u32[]{:S(2)}, u32[]{:S(2)}) collective-permute-start(bf16[256,256]{1,0:T(8,128)(2,1)S(1)} %fold.1), channel_id=1, source_target_pairs={{0,2},{1,5},{2,0},{3,7},{4,6},{5,1},{6,4},{7,3},{8,10},{9,13},{10,... | collective-permute-start | bytes 393224 | tf_op jit(solution)/shard_map/ppermute | solution.py:377

commit v6 on v5

--- a/solution.py
+++ b/solution.py
@@ -12,7 +12,6 @@
 CARRIED = 16
 PIECES = 3
 TURN = 1.0 / (2.0 * math.pi)
-ROUNDER = 1.5 * 2.0**23
 SINE = (6.283164044217864, -41.337142357601536, 81.3407683703199, -70.9934277613874)
 
 
@@ -30,7 +29,7 @@
 
 def cos_sin(z):
     turns = z * TURN
-    part = turns - ((turns + ROUNDER) - ROUNDER)
+    part = turns - lax.round(turns, lax.RoundingMethod.TO_NEAREST_EVEN)
     wave = jnp.minimum(jnp.maximum(part, -0.5 - part), 0.5 - part)
     return quarter_sine(0.25 - jnp.abs(part)), quarter_sine(wave)
 

time: 55.8 us -> 55.7 us (level)
  no operation moved by 1% of the time
where the time goes in v6:
time: 55.7 us; the launch traced here: 55.4 us
  waiting for transfers between devices  16.1 us (29%)
  blocking collectives  14.6 us (26%)
  starting transfers between devices  11.1 us (20%)
  Pallas kernels  9.45 us (17%)
  local copies, waits for them, and re-layouts  3.41 us (6%)
  between operations  0.71 us (1%)
    all_to_all x1, blocking collectives, on_device(): lax.all_to_all(partial_head.reshape(n_dp // 2, out_rows, d_s), ('dp', 'fe...  14.6 us
    all_to_all x1, waiting for transfers between devices, on_device(): lax.all_to_all(sent.reshape(n_dp, capacity, width), 'dp', split_axis=0, c...  11.4 us
    all_to_all x1, starting transfers between devices, on_device(): lax.all_to_all(sent.reshape(n_dp, capacity, width), 'dp', split_axis=0, c...  8.33 us
    ppermute x2, waiting for transfers between devices, across(): return lax.ppermute(value, ('dp', 'feat'), moves)  3.55 us
    pallas_call x1, Pallas kernels, on_device(): pl.pallas_call(functools.partial(class_kernel, role, n_feat, n_dp, bits,...  3.43 us
    unnamed x6, local copies, waits for them, and re-layouts  3.41 us
    pallas_call x1, Pallas kernels, on_device(): pl.pallas_call(functools.partial(route_kernel, cls_dev, capacity), out_sh...  2.39 us
    pallas_call x1, Pallas kernels, on_device(): pl.pallas_call(functools.partial(first_kernel, role, n_feat, d_s), out_sh...  1.64 us
  transfers between devices with their start and end apart: 7, of which 5 were waited for; matrix products, arithmetic and copies ran while one was open for 0% of the time, Pallas kernels for 11%

profile of v6, /device:TPU:0, one launch (start us, length us, event | category | flops | bytes accessed | tf_op | source)
XLA Modules:
  0.0 55.4 jit_solution(4441466757227582988)
XLA Ops:
  0.6 2.4 %route.1 = (bf16[256,1024]{1,0:T(8,128)(2,1)}, f32[8,128]{1,0:T(8,128)}) custom-call(s32[128]{0:T(128)} %labels_in.1, s32[5456]{0:T(1024)} %table_in.1, bf16[128,1024]{1,0:T(8,128)(2,1)} %teacher.1, bf16[128,768]{1,0:T(8,128)(2,1)} %student.1), custom_call_target="tpu_custom_call" | custom-call | tf_op jit(solution)/shard_map/route/pallas_call | solution.py:383
  3.0 8.3 %all-to-all-start = ((bf16[16,16,1024]{2,1,0:T(8,128)(2,1)}), bf16[16,16,1024]{2,1,0:T(8,128)(2,1)S(1)}, u32[]{:S(2)}, u32[]{:S(2)}) async-start(bf16[16,16,1024]{2,1,0:T(8,128)(2,1)} %bitcast.7), calls=%async_computation | async-start | bytes 1048576 | tf_op jit(solution)/shard_map/all_to_all | solution.py:422
  11.4 0.0 copy-start
  11.4 1.6 %copy-done = bf16[1024,1024]{1,0:T(8,128)(2,1)S(1)} copy-done((bf16[1024,1024]{1,0:T(8,128)(2,1)S(1)}, bf16[1024,1024]{1,0:T(8,128)(2,1)}, u32[]{:S(2)}) %copy-start) | copy-done | bytes 2097176
  13.0 1.1 %copy-done.1 = bf16[768,512]{1,0:T(8,128)(2,1)S(1)} copy-done((bf16[768,512]{1,0:T(8,128)(2,1)S(1)}, bf16[768,512]{1,0:T(8,128)(2,1)}, u32[]{:S(2)}) %copy-start.1) | copy-done | bytes 786456
  14.1 0.7 %copy-done.2 = f32[8,128]{1,0:T(8,128)S(1)} copy-done((f32[8,128]{1,0:T(8,128)S(1)}, f32[8,128]{1,0:T(8,128)}, u32[]{:S(2)}) %copy-start.2) | copy-done | bytes 4120
  14.8 0.2 load.1
  15.0 0.1 collective-permute-start.1
  15.1 11.4 %all-to-all-done = bf16[16,16,1024]{2,1,0:T(8,128)(2,1)S(1)} async-done(((bf16[16,16,1024]{2,1,0:T(8,128)(2,1)}), bf16[16,16,1024]{2,1,0:T(8,128)(2,1)S(1)}, u32[]{:S(2)}, u32[]{:S(2)}) %all-to-all-start) | async-done | bytes 524320 | tf_op jit(solution)/shard_map/all_to_all | solution.py:422
  26.5 0.0 collective-permute-start
  26.5 1.6 %first.1 = (f32[256,1024]{1,0:T(8,128)S(1)}, f32[256,1024]{1,0:T(8,128)S(1)}, bf16[1,768,512]{2,1,0:T(8,128)(2,1)S(1)}) custom-call(bf16[256,1024]{1,0:T(8,128)(2,1)S(1)} %bitcast.4, bf16[768,512]{1,0:T(8,128)(2,1)S(1)} %get-tuple-element.27.refs_0_, bf16[768,512]{1,0:T(8,128)(2,1)} %collective-permute-done.1.refs_1_, ...), custom_call_target="tpu_custom_call" | custom-call | tf_op jit(solution)/shard_map/first/pallas_call | solution.py:444
  28.1 0.3 collective-permute-done.other
  28.5 0.6 %collective-permute-start.5 = (bf16[256,768]{1,0:T(8,128)(2,1)S(1)}, bf16[256,768]{1,0:T(8,128)(2,1)S(1)}, u32[]{:S(2)}, u32[]{:S(2)}) collective-permute-start(bf16[256,768]{1,0:T(8,128)(2,1)S(1)} %get-tuple-element.37.student.refs_3_), channel_id=1, source_target_pairs={{0,2},{1,5},{2,0},{3,7},{4,6},{5,1},{6,4},{7,3},{8,10},{9,13},{10,... | collective-permute-start | bytes 1179656 | tf_op jit(solution)/shard_map/ppermute | solution.py:376
  29.1 3.4 %classes.1 = (f32[256,256]{1,0:T(8,128)S(1)}, bf16[272,256]{1,0:T(8,128)(2,1)S(1)}, f32[256,256]{1,0:T(8,128)S(1)}, bf16[256,256]{1,0:T(8,128)(2,1)S(1)}, f32[1,512]{1,0:T(1,128)S(1)}) custom-call(bf16[256,1024]{1,0:T(8,128)(2,1)S(1)} %collective-permute-done.other, bf16[256,768]{1,0:T(8,128)(2,1)S(1)} %get-tuple-element.37.student.refs_3_, ...), custom_call_target="tpu_custom_call" | custom-call | tf_op jit(solution)/shard_map/classes/pallas_call | solution.py:458
  32.5 1.2 %collective-permute-start.2 = (bf16[256,256]{1,0:T(8,128)(2,1)S(1)}, bf16[256,256]{1,0:T(8,128)(2,1)S(1)}, u32[]{:S(2)}, u32[]{:S(2)}) collective-permute-start(bf16[256,256]{1,0:T(8,128)(2,1)S(1)} %get-tuple-element.34), channel_id=1, source_target_pairs={{0,1},{1,0},{2,3},{3,2},{4,5},{5,4},{6,7},{7,6},{8,9},{9,8},{10,11... | collective-permute-start | bytes 393224 | tf_op jit(solution)/shard_map/ppermute | solution.py:379
  33.7 0.1 collective-permute-start.4
  33.8 0.9 %collective-permute-done.2.refs_1_ = bf16[256,256]{1,0:T(8,128)(2,1)S(1)} collective-permute-done((bf16[256,256]{1,0:T(8,128)(2,1)S(1)}, bf16[256,256]{1,0:T(8,128)(2,1)S(1)}, u32[]{:S(2)}, u32[]{:S(2)}) %collective-permute-start.2) | collective-permute-done | bytes 131104 | tf_op jit(solution)/shard_map/ppermute | solution.py:379
  34.8 0.7 %collective-permute-start.3 = (bf16[256,256]{1,0:T(8,128)(2,1)S(1)}, bf16[256,256]{1,0:T(8,128)(2,1)S(1)}, u32[]{:S(2)}, u32[]{:S(2)}) collective-permute-start(bf16[256,256]{1,0:T(8,128)(2,1)S(1)} %fold.1), channel_id=1, source_target_pairs={{0,2},{1,5},{2,0},{3,7},{4,6},{5,1},{6,4},{7,3},{8,10},{9,13},{10,... | collective-permute-start | bytes 393224 | tf_op jit(solution)/shard_map/ppermute | solution.py:376
  35.5 0.8 %collective-permute-done.5.refs_2_ = bf16[256,768]{1,0:T(8,128)(2,1)S(1)} collective-permute-done((bf16[256,768]{1,0:T(8,128)(2,1)S(1)}, bf16[256,768]{1,0:T(8,128)(2,1)S(1)}, u32[]{:S(2)}, u32[]{:S(2)}) %collective-permute-start.5) | collective-permute-done | bytes 393248 | tf_op jit(solution)/shard_map/ppermute | solution.py:376
  36.3 0.8 %own.1 = (f32[256,768]{1,0:T(8,128)S(1)}, f32[341]{0:T(512)}) custom-call(f32[256,256]{1,0:T(8,128)S(1)} %get-tuple-element.38.refs_0_, bf16[272,256]{1,0:T(8,128)(2,1)S(1)} %collective-permute-done.4.refs_1_, f32[1,512]{1,0:T(1,128)S(1)} %get-tuple-element.40.refs_2_, bf16[256,768]{1,0:T(8,128)(2,1)S(1)} %get-tuple-element.37.student.refs_3_), custom_call_target="tpu_custom_call" | custom-call | tf_op jit(solution)/shard_map/own/pallas_call | solution.py:493
  37.0 2.7 %collective-permute-done.3.refs_0_ = bf16[256,256]{1,0:T(8,128)(2,1)S(1)} collective-permute-done((bf16[256,256]{1,0:T(8,128)(2,1)S(1)}, bf16[256,256]{1,0:T(8,128)(2,1)S(1)}, u32[]{:S(2)}, u32[]{:S(2)}) %collective-permute-start.3) | collective-permute-done | bytes 131104 | tf_op jit(solution)/shard_map/ppermute | solution.py:376
  39.8 0.3 head.1
  40.1 14.6 %all_to_all.10.parts = bf16[8,32,768]{2,1,0:T(8,128)(2,1)S(1)} all-to-all(bf16[8,32,768]{2,1,0:T(8,128)(2,1)S(1)} %bitcast.6), channel_id=1, replica_groups={{0,4,8,12,16,20,24,28},{2,6,10,14,18,22,26,30},{1,3,9,11,17,19,25,27},{..., dimensions={0} | all-to-all | bytes 786432 | tf_op jit(solution)/shard_map/all_to_all | solution.py:508
  54.7 0.7 %total.1 = f32[32,768]{1,0:T(8,128)} custom-call(bf16[8,32,768]{2,1,0:T(8,128)(2,1)S(1)} %all_to_all.10.parts), custom_call_target="tpu_custom_call" | custom-call | tf_op jit(solution)/shard_map/total/pallas_call | solution.py:520
  (6 shorter events, 0.1 us)
Async XLA Ops:
  3.0 23.5 %all-to-all-start = ((bf16[16,16,1024]{2,1,0:T(8,128)(2,1)}), bf16[16,16,1024]{2,1,0:T(8,128)(2,1)S(1)}, u32[]{:S(2)}, u32[]{:S(2)}) async-start(bf16[16,16,1024]{2,1,0:T(8,128)(2,1)} %bitcast.7), calls=%async_computation | async-start | bytes 1048576 | tf_op jit(solution)/shard_map/all_to_all | solution.py:422
  11.4 1.6 %copy-start = (bf16[1024,1024]{1,0:T(8,128)(2,1)S(1)}, bf16[1024,1024]{1,0:T(8,128)(2,1)}, u32[]{:S(2)}) copy-start(bf16[1024,1024]{1,0:T(8,128)(2,1)} %freqs_in.1) | copy-start | bytes 6291460
  13.0 1.1 %copy-start.1 = (bf16[768,512]{1,0:T(8,128)(2,1)S(1)}, bf16[768,512]{1,0:T(8,128)(2,1)}, u32[]{:S(2)}) copy-start(bf16[768,512]{1,0:T(8,128)(2,1)} %head_in.1) | copy-start | bytes 2359300
  14.1 0.7 %copy-start.2 = (f32[8,128]{1,0:T(8,128)S(1)}, f32[8,128]{1,0:T(8,128)}, u32[]{:S(2)}) copy-start(f32[8,128]{1,0:T(8,128)} %get-tuple-element.26._) | copy-start | bytes 12292
  15.0 11.5 %collective-permute-start.1 = (bf16[768,512]{1,0:T(8,128)(2,1)S(1)}, bf16[768,512]{1,0:T(8,128)(2,1)}, u32[]{:S(2)}, u32[]{:S(2)}) collective-permute-start(bf16[768,512]{1,0:T(8,128)(2,1)S(1)} %get-tuple-element.27.refs_0_), channel_id=1, source_target_pairs={{0,1},{1,0},{2,3},{3,2},{4,5},{5,4},{6,7},{7,6},{8,9},{9,8},{10,11... | collective-permute-start | bytes 2359304 | tf_op jit(solution)/shard_map/ppermute | solution.py:379
  26.5 1.9 %collective-permute-start = (bf16[256,1024]{1,0:T(8,128)(2,1)S(1)}, bf16[256,1024]{1,0:T(8,128)(2,1)S(1)}, u32[]{:S(2)}, u32[]{:S(2)}) collective-permute-start(bf16[256,1024]{1,0:T(8,128)(2,1)S(1)} %bitcast.3), channel_id=1, source_target_pairs={{0,1},{1,0},{2,3},{3,2},{4,5},{5,4},{6,7},{7,6},{8,9},{9,8},{10,11... | collective-permute-start | bytes 1572872 | tf_op jit(solution)/shard_map/ppermute | solution.py:379
  28.5 7.8 %collective-permute-start.5 = (bf16[256,768]{1,0:T(8,128)(2,1)S(1)}, bf16[256,768]{1,0:T(8,128)(2,1)S(1)}, u32[]{:S(2)}, u32[]{:S(2)}) collective-permute-start(bf16[256,768]{1,0:T(8,128)(2,1)S(1)} %get-tuple-element.37.student.refs_3_), channel_id=1, source_target_pairs={{0,2},{1,5},{2,0},{3,7},{4,6},{5,1},{6,4},{7,3},{8,10},{9,13},{10,... | collective-permute-start | bytes 1179656 | tf_op jit(solution)/shard_map/ppermute | solution.py:376
  32.5 2.2 %collective-permute-start.2 = (bf16[256,256]{1,0:T(8,128)(2,1)S(1)}, bf16[256,256]{1,0:T(8,128)(2,1)S(1)}, u32[]{:S(2)}, u32[]{:S(2)}) collective-permute-start(bf16[256,256]{1,0:T(8,128)(2,1)S(1)} %get-tuple-element.34), channel_id=1, source_target_pairs={{0,1},{1,0},{2,3},{3,2},{4,5},{5,4},{6,7},{7,6},{8,9},{9,8},{10,11... | collective-permute-start | bytes 393224 | tf_op jit(solution)/shard_map/ppermute | solution.py:379
  33.7 1.7 %collective-permute-start.4 = (bf16[272,256]{1,0:T(8,128)(2,1)S(1)}, bf16[272,256]{1,0:T(8,128)(2,1)S(1)}, u32[]{:S(2)}, u32[]{:S(2)}) collective-permute-start(bf16[272,256]{1,0:T(8,128)(2,1)S(1)} %get-tuple-element.36), channel_id=1, source_target_pairs={{0,1},{1,0},{2,3},{3,2},{4,5},{5,4},{6,7},{7,6},{8,9},{9,8},{10,11... | collective-permute-start | bytes 417800 | tf_op jit(solution)/shard_map/ppermute | solution.py:379
  34.8 5.0 %collective-permute-start.3 = (bf16[256,256]{1,0:T(8,128)(2,1)S(1)}, bf16[256,256]{1,0:T(8,128)(2,1)S(1)}, u32[]{:S(2)}, u32[]{:S(2)}) collective-permute-start(bf16[256,256]{1,0:T(8,128)(2,1)S(1)} %fold.1), channel_id=1, source_target_pairs={{0,2},{1,5},{2,0},{3,7},{4,6},{5,1},{6,4},{7,3},{8,10},{9,13},{10,... | collective-permute-start | bytes 393224 | tf_op jit(solution)/shard_map/ppermute | solution.py:376

commit v7 on v6

--- a/solution.py
+++ b/solution.py
@@ -235,16 +235,35 @@
     return jnp.where(bit == 0, low, high)
 
 
+def grad_rows(offset, n_feat, n_dp, bits, weight, freqs, grad_z, picked):
+    holder = lax.axis_index("dp")
+    target = lax.rem(lax.axis_index("feat") + offset, n_feat)
+    bit = lax.rem(target, bits)
+    side = jnp.where(bit == 0, lax.rem(holder, 2), lax.rem(holder // 2, 2))
+    out_rows = picked.shape[0] // n_dp
+    if weight is not None:
+        picked[...] = weight
+    else:
+        for index in range(n_dp):
+            across, group = divmod(index, n_dp // 2)
+            member = member_of(group, bit, 1 - side if across else side)
+            start = pl.multiple_of((member * n_feat + target) * out_rows, out_rows)
+            picked[index * out_rows : (index + 1) * out_rows, :] = freqs[
+                pl.ds(start, out_rows), :
+            ]
+    return lax.dot_general(
+        picked[...], grad_z[...], (((1,), (1,)), ((), ())), preferred_element_type=jnp.float32
+    )
+
+
 def class_kernel(
     role, n_feat, n_dp, bits, cls_pad, permuted, other, student, tags_in, cos, sin, *refs
 ):
     head, others, freqs, refs = refs[0], refs[1], refs[2], refs[3:]
     if permuted:
         weights, refs = refs[0], refs[1:]
-    grads, refs = refs[: 2 * n_feat], refs[2 * n_feat :]
-    norms, inputs, grad_z, picked = refs
-    feat = lax.axis_index("feat")
-    holder = lax.axis_index("dp")
+    grads, refs = refs[: 2 * n_feat - 2], refs[2 * n_feat - 2 :]
+    norms, grad_z, inputs, picked = refs
     mine_student = is_role(role, 1)
     slots, d_t = inputs.shape
     half = freqs.shape[1]
@@ -288,30 +307,23 @@
     total_norm = jnp.sum(jnp.where(cls == tag, norm, 0.0), axis=0, keepdims=True)
     norms[...] = total_norm
     carried = carry(total_norm, slots)
-    out_rows = d_t // (n_dp * n_feat)
-    block = n_dp // 2 * out_rows
-    for offset in range(n_feat):
-        target = lax.rem(feat + offset, n_feat)
-        bit = lax.rem(target, bits)
-        side = jnp.where(bit == 0, lax.rem(holder, 2), lax.rem(holder // 2, 2))
-        if permuted:
-            picked[...] = weights[offset]
-        else:
-            for index in range(n_dp):
-                across, group = divmod(index, n_dp // 2)
-                member = member_of(group, bit, 1 - side if across else side)
-                start = pl.multiple_of((member * n_feat + target) * out_rows, out_rows)
-                picked[index * out_rows : (index + 1) * out_rows, :] = freqs[
-                    pl.ds(start, out_rows), :
-                ]
-        product = lax.dot_general(
-            picked[...], grad_z[...], (((1,), (1,)), ((), ())), preferred_element_type=jnp.float32
-        )
-        here, there = grads[offset], grads[n_feat + offset]
+    block = picked.shape[0] // 2
+    for offset in range(1, n_feat):
+        weight = weights[offset] if permuted else None
+        product = grad_rows(offset, n_feat, n_dp, bits, weight, freqs, grad_z, picked)
+        here, there = grads[offset - 1], grads[n_feat + offset - 2]
         here[:block, :] = product[:block].astype(here.dtype)
+        here[block:, :] = carried
         there[...] = product[block:].astype(there.dtype)
-        if offset:
-            here[block:, :] = carried
+
+
+def keep_kernel(n_feat, n_dp, bits, permuted, *refs):
+    weights, (freqs, grad_z, here, there, picked) = refs[:-5], refs[-5:]
+    weight = weights[0][0] if permuted else None
+    product = grad_rows(0, n_feat, n_dp, bits, weight, freqs, grad_z, picked)
+    block = picked.shape[0] // 2
+    here[...] = product[:block]
+    there[...] = product[block:]
 
 
 def summed(refs, size):
@@ -455,23 +467,17 @@
     )(mine, *heads, freqs_near)
     cos, student_out = lax.optimization_barrier((cos, student_in))
     student_across = across(student_out)
-    *grads, norms = pl.pallas_call(
+    *grads, norms, grad_z = pl.pallas_call(
         functools.partial(class_kernel, role, n_feat, n_dp, bits, cls_pad, permuted),
-        out_shape=tuple(
-            jax.ShapeDtypeStruct((block + CARRIED, slots), jnp.bfloat16)
-            if k
-            else jax.ShapeDtypeStruct((block, slots), jnp.float32)
-            for k in range(n_feat)
-        )
-        + tuple(
-            jax.ShapeDtypeStruct((block, slots), jnp.bfloat16 if k else jnp.float32)
-            for k in range(n_feat)
-        )
-        + (jax.ShapeDtypeStruct((1, cls_pad), jnp.float32),),
+        out_shape=(jax.ShapeDtypeStruct((block + CARRIED, slots), jnp.bfloat16),) * (n_feat - 1)
+        + (jax.ShapeDtypeStruct((block, slots), jnp.bfloat16),) * (n_feat - 1)
+        + (
+            jax.ShapeDtypeStruct((1, cls_pad), jnp.float32),
+            jax.ShapeDtypeStruct((slots, half), jnp.bfloat16),
+        ),
         in_specs=[near] * (8 + len(weights)),
         scratch_shapes=[
             pltpu.VMEM((slots, d_t), jnp.bfloat16),
-            pltpu.VMEM((slots, half), jnp.bfloat16),
             pltpu.VMEM((2 * block, half), jnp.bfloat16),
         ],
         compiler_params=vmem,
@@ -479,8 +485,15 @@
     )(
         other, student_in, tags_in, cos, sin, heads[0], head_others, freqs_near, *weights
     )
-    here = [grads[0]] + [shifted(grads[k], k) for k in range(1, n_feat)]
-    there = [grads[n_feat]] + [shifted(grads[n_feat + k], k) for k in range(1, n_feat)]
+    here_own, there_own = pl.pallas_call(
+        functools.partial(keep_kernel, n_feat, n_dp, bits, permuted),
+        out_shape=(jax.ShapeDtypeStruct((block, slots), jnp.float32),) * 2,
+        scratch_shapes=[pltpu.VMEM((2 * block, half), jnp.bfloat16)],
+        compiler_params=vmem,
+        name="keep",
+    )(*weights, freqs_near, grad_z)
+    here = [here_own] + [shifted(grads[k - 1], k) for k in range(1, n_feat)]
+    there = [there_own] + [shifted(grads[n_feat + k - 2], k) for k in range(1, n_feat)]
     folded = pl.pallas_call(
         fold_kernel,
         out_shape=jax.ShapeDtypeStruct((block, slots), jnp.bfloat16),

time: 55.7 us -> 55.5 us (level)
  no operation moved by 1% of the time
where the time goes in v7:
time: 55.5 us; the launch traced here: 55.1 us
  waiting for transfers between devices  15.7 us (28%)
  blocking collectives  14.6 us (26%)
  starting transfers between devices  11.1 us (20%)
  Pallas kernels  9.69 us (17%)
  local copies, waits for them, and re-layouts  3.41 us (6%)
  between operations  0.71 us (1%)
    all_to_all x1, blocking collectives, on_device(): lax.all_to_all(partial_head.reshape(n_dp // 2, out_rows, d_s), ('dp', 'fe...  14.6 us
    all_to_all x1, waiting for transfers between devices, on_device(): lax.all_to_all(sent.reshape(n_dp, capacity, width), 'dp', split_axis=0, c...  11.4 us
    all_to_all x1, starting transfers between devices, on_device(): lax.all_to_all(sent.reshape(n_dp, capacity, width), 'dp', split_axis=0, c...  8.33 us
    ppermute x2, waiting for transfers between devices, across(): return lax.ppermute(value, ('dp', 'feat'), moves)  3.55 us
    unnamed x6, local copies, waits for them, and re-layouts  3.41 us
    pallas_call x1, Pallas kernels, on_device(): pl.pallas_call(functools.partial(class_kernel, role, n_feat, n_dp, bits,...  3.2 us
    pallas_call x1, Pallas kernels, on_device(): pl.pallas_call(functools.partial(route_kernel, cls_dev, capacity), out_sh...  2.38 us
    pallas_call x1, Pallas kernels, on_device(): pl.pallas_call(functools.partial(first_kernel, role, n_feat, d_s), out_sh...  1.64 us
  transfers between devices with their start and end apart: 7, of which 5 were waited for; matrix products, arithmetic and copies ran while one was open for 0% of the time, Pallas kernels for 11%

profile of v7, /device:TPU:0, one launch (start us, length us, event | category | flops | bytes accessed | tf_op | source)
XLA Modules:
  0.0 55.1 jit_solution(7370960613766754410)
XLA Ops:
  0.6 2.4 %route.1 = (bf16[256,1024]{1,0:T(8,128)(2,1)}, f32[8,128]{1,0:T(8,128)}) custom-call(s32[128]{0:T(128)} %labels_in.1, s32[5456]{0:T(1024)} %table_in.1, bf16[128,1024]{1,0:T(8,128)(2,1)} %teacher.1, bf16[128,768]{1,0:T(8,128)(2,1)} %student.1), custom_call_target="tpu_custom_call" | custom-call | tf_op jit(solution)/shard_map/route/pallas_call | solution.py:395
  3.0 8.3 %all-to-all-start = ((bf16[16,16,1024]{2,1,0:T(8,128)(2,1)}), bf16[16,16,1024]{2,1,0:T(8,128)(2,1)S(1)}, u32[]{:S(2)}, u32[]{:S(2)}) async-start(bf16[16,16,1024]{2,1,0:T(8,128)(2,1)} %bitcast.7), calls=%async_computation | async-start | bytes 1048576 | tf_op jit(solution)/shard_map/all_to_all | solution.py:434
  11.4 0.0 copy-start
  11.4 1.6 %copy-done = bf16[1024,1024]{1,0:T(8,128)(2,1)S(1)} copy-done((bf16[1024,1024]{1,0:T(8,128)(2,1)S(1)}, bf16[1024,1024]{1,0:T(8,128)(2,1)}, u32[]{:S(2)}) %copy-start) | copy-done | bytes 2097176
  13.0 1.1 %copy-done.1 = bf16[768,512]{1,0:T(8,128)(2,1)S(1)} copy-done((bf16[768,512]{1,0:T(8,128)(2,1)S(1)}, bf16[768,512]{1,0:T(8,128)(2,1)}, u32[]{:S(2)}) %copy-start.1) | copy-done | bytes 786456
  14.1 0.7 %copy-done.2 = f32[8,128]{1,0:T(8,128)S(1)} copy-done((f32[8,128]{1,0:T(8,128)S(1)}, f32[8,128]{1,0:T(8,128)}, u32[]{:S(2)}) %copy-start.2) | copy-done | bytes 4120
  14.8 0.2 load.1
  15.0 0.1 collective-permute-start.1
  15.1 11.4 %all-to-all-done = bf16[16,16,1024]{2,1,0:T(8,128)(2,1)S(1)} async-done(((bf16[16,16,1024]{2,1,0:T(8,128)(2,1)}), bf16[16,16,1024]{2,1,0:T(8,128)(2,1)S(1)}, u32[]{:S(2)}, u32[]{:S(2)}) %all-to-all-start) | async-done | bytes 524320 | tf_op jit(solution)/shard_map/all_to_all | solution.py:434
  26.5 1.6 %first.1 = (f32[256,1024]{1,0:T(8,128)S(1)}, f32[256,1024]{1,0:T(8,128)S(1)}, bf16[1,768,512]{2,1,0:T(8,128)(2,1)S(1)}) custom-call(bf16[256,1024]{1,0:T(8,128)(2,1)S(1)} %bitcast.4, bf16[768,512]{1,0:T(8,128)(2,1)S(1)} %get-tuple-element.29.refs_0_, bf16[768,512]{1,0:T(8,128)(2,1)} %collective-permute-done.1.refs_1_, ...), custom_call_target="tpu_custom_call" | custom-call | tf_op jit(solution)/shard_map/first/pallas_call | solution.py:456
  28.1 0.3 collective-permute-done.other
  28.4 0.6 %collective-permute-start.5 = (bf16[256,768]{1,0:T(8,128)(2,1)S(1)}, bf16[256,768]{1,0:T(8,128)(2,1)S(1)}, u32[]{:S(2)}, u32[]{:S(2)}) collective-permute-start(bf16[256,768]{1,0:T(8,128)(2,1)S(1)} %get-tuple-element.39.student.refs_3_), channel_id=1, source_target_pairs={{0,2},{1,5},{2,0},{3,7},{4,6},{5,1},{6,4},{7,3},{8,10},{9,13},{10,... | collective-permute-start | bytes 1179656 | tf_op jit(solution)/shard_map/ppermute | solution.py:388
  29.1 3.2 %classes.1 = (bf16[272,256]{1,0:T(8,128)(2,1)S(1)}, bf16[256,256]{1,0:T(8,128)(2,1)S(1)}, f32[1,512]{1,0:T(1,128)S(1)}, bf16[256,1024]{1,0:T(8,128)(2,1)S(1)}) custom-call(bf16[256,1024]{1,0:T(8,128)(2,1)S(1)} %collective-permute-done.other, bf16[256,768]{1,0:T(8,128)(2,1)S(1)} %get-tuple-element.39.student.refs_3_, ...), custom_call_target="tpu_custom_call" | custom-call | tf_op jit(solution)/shard_map/classes/pallas_call | solution.py:470
  32.3 1.2 %collective-permute-start.2 = (bf16[256,256]{1,0:T(8,128)(2,1)S(1)}, bf16[256,256]{1,0:T(8,128)(2,1)S(1)}, u32[]{:S(2)}, u32[]{:S(2)}) collective-permute-start(bf16[256,256]{1,0:T(8,128)(2,1)S(1)} %get-tuple-element.36), channel_id=1, source_target_pairs={{0,1},{1,0},{2,3},{3,2},{4,5},{5,4},{6,7},{7,6},{8,9},{9,8},{10,11... | collective-permute-start | bytes 393224 | tf_op jit(solution)/shard_map/ppermute | solution.py:391
  33.5 0.1 collective-permute-start.4
  33.6 0.5 keep.1
  34.1 0.4 collective-permute-done.2.refs_1_
  34.5 0.7 %collective-permute-start.3 = (bf16[256,256]{1,0:T(8,128)(2,1)S(1)}, bf16[256,256]{1,0:T(8,128)(2,1)S(1)}, u32[]{:S(2)}, u32[]{:S(2)}) collective-permute-start(bf16[256,256]{1,0:T(8,128)(2,1)S(1)} %fold.1), channel_id=1, source_target_pairs={{0,2},{1,5},{2,0},{3,7},{4,6},{5,1},{6,4},{7,3},{8,10},{9,13},{10,... | collective-permute-start | bytes 393224 | tf_op jit(solution)/shard_map/ppermute | solution.py:388
  35.3 1.0 %collective-permute-done.5.refs_2_ = bf16[256,768]{1,0:T(8,128)(2,1)S(1)} collective-permute-done((bf16[256,768]{1,0:T(8,128)(2,1)S(1)}, bf16[256,768]{1,0:T(8,128)(2,1)S(1)}, u32[]{:S(2)}, u32[]{:S(2)}) %collective-permute-start.5) | collective-permute-done | bytes 393248 | tf_op jit(solution)/shard_map/ppermute | solution.py:388
  36.3 0.8 %own.1 = (f32[256,768]{1,0:T(8,128)S(1)}, f32[341]{0:T(512)}) custom-call(f32[256,256]{1,0:T(8,128)S(1)} %get-tuple-element.40.refs_0_, bf16[272,256]{1,0:T(8,128)(2,1)S(1)} %collective-permute-done.4.refs_1_, f32[1,512]{1,0:T(1,128)S(1)} %get-tuple-element.42.refs_2_, bf16[256,768]{1,0:T(8,128)(2,1)S(1)} %get-tuple-element.39.student.refs_3_), custom_call_target="tpu_custom_call" | custom-call | tf_op jit(solution)/shard_map/own/pallas_call | solution.py:506
  37.0 2.5 %collective-permute-done.3.refs_0_ = bf16[256,256]{1,0:T(8,128)(2,1)S(1)} collective-permute-done((bf16[256,256]{1,0:T(8,128)(2,1)S(1)}, bf16[256,256]{1,0:T(8,128)(2,1)S(1)}, u32[]{:S(2)}, u32[]{:S(2)}) %collective-permute-start.3) | collective-permute-done | bytes 131104 | tf_op jit(solution)/shard_map/ppermute | solution.py:388
  39.6 0.3 head.1
  39.8 14.6 %all_to_all.10.parts = bf16[8,32,768]{2,1,0:T(8,128)(2,1)S(1)} all-to-all(bf16[8,32,768]{2,1,0:T(8,128)(2,1)S(1)} %bitcast.6), channel_id=1, replica_groups={{0,4,8,12,16,20,24,28},{2,6,10,14,18,22,26,30},{1,3,9,11,17,19,25,27},{..., dimensions={0} | all-to-all | bytes 786432 | tf_op jit(solution)/shard_map/all_to_all | solution.py:521
  54.4 0.7 %total.1 = f32[32,768]{1,0:T(8,128)} custom-call(bf16[8,32,768]{2,1,0:T(8,128)(2,1)S(1)} %all_to_all.10.parts), custom_call_target="tpu_custom_call" | custom-call | tf_op jit(solution)/shard_map/total/pallas_call | solution.py:533
  (7 shorter events, 0.1 us)
Async XLA Ops:
  3.0 23.5 %all-to-all-start = ((bf16[16,16,1024]{2,1,0:T(8,128)(2,1)}), bf16[16,16,1024]{2,1,0:T(8,128)(2,1)S(1)}, u32[]{:S(2)}, u32[]{:S(2)}) async-start(bf16[16,16,1024]{2,1,0:T(8,128)(2,1)} %bitcast.7), calls=%async_computation | async-start | bytes 1048576 | tf_op jit(solution)/shard_map/all_to_all | solution.py:434
  11.4 1.6 %copy-start = (bf16[1024,1024]{1,0:T(8,128)(2,1)S(1)}, bf16[1024,1024]{1,0:T(8,128)(2,1)}, u32[]{:S(2)}) copy-start(bf16[1024,1024]{1,0:T(8,128)(2,1)} %freqs_in.1) | copy-start | bytes 6291460
  13.0 1.1 %copy-start.1 = (bf16[768,512]{1,0:T(8,128)(2,1)S(1)}, bf16[768,512]{1,0:T(8,128)(2,1)}, u32[]{:S(2)}) copy-start(bf16[768,512]{1,0:T(8,128)(2,1)} %head_in.1) | copy-start | bytes 2359300
  14.1 0.7 %copy-start.2 = (f32[8,128]{1,0:T(8,128)S(1)}, f32[8,128]{1,0:T(8,128)}, u32[]{:S(2)}) copy-start(f32[8,128]{1,0:T(8,128)} %get-tuple-element.24._) | copy-start | bytes 12292
  15.0 11.5 %collective-permute-start.1 = (bf16[768,512]{1,0:T(8,128)(2,1)S(1)}, bf16[768,512]{1,0:T(8,128)(2,1)}, u32[]{:S(2)}, u32[]{:S(2)}) collective-permute-start(bf16[768,512]{1,0:T(8,128)(2,1)S(1)} %get-tuple-element.29.refs_0_), channel_id=1, source_target_pairs={{0,1},{1,0},{2,3},{3,2},{4,5},{5,4},{6,7},{7,6},{8,9},{9,8},{10,11... | collective-permute-start | bytes 2359304 | tf_op jit(solution)/shard_map/ppermute | solution.py:391
  26.5 1.9 %collective-permute-start = (bf16[256,1024]{1,0:T(8,128)(2,1)S(1)}, bf16[256,1024]{1,0:T(8,128)(2,1)S(1)}, u32[]{:S(2)}, u32[]{:S(2)}) collective-permute-start(bf16[256,1024]{1,0:T(8,128)(2,1)S(1)} %bitcast.3), channel_id=1, source_target_pairs={{0,1},{1,0},{2,3},{3,2},{4,5},{5,4},{6,7},{7,6},{8,9},{9,8},{10,11... | collective-permute-start | bytes 1572872 | tf_op jit(solution)/shard_map/ppermute | solution.py:391
  28.4 7.8 %collective-permute-start.5 = (bf16[256,768]{1,0:T(8,128)(2,1)S(1)}, bf16[256,768]{1,0:T(8,128)(2,1)S(1)}, u32[]{:S(2)}, u32[]{:S(2)}) collective-permute-start(bf16[256,768]{1,0:T(8,128)(2,1)S(1)} %get-tuple-element.39.student.refs_3_), channel_id=1, source_target_pairs={{0,2},{1,5},{2,0},{3,7},{4,6},{5,1},{6,4},{7,3},{8,10},{9,13},{10,... | collective-permute-start | bytes 1179656 | tf_op jit(solution)/shard_map/ppermute | solution.py:388
  32.3 2.2 %collective-permute-start.2 = (bf16[256,256]{1,0:T(8,128)(2,1)S(1)}, bf16[256,256]{1,0:T(8,128)(2,1)S(1)}, u32[]{:S(2)}, u32[]{:S(2)}) collective-permute-start(bf16[256,256]{1,0:T(8,128)(2,1)S(1)} %get-tuple-element.36), channel_id=1, source_target_pairs={{0,1},{1,0},{2,3},{3,2},{4,5},{5,4},{6,7},{7,6},{8,9},{9,8},{10,11... | collective-permute-start | bytes 393224 | tf_op jit(solution)/shard_map/ppermute | solution.py:391
  33.5 1.7 %collective-permute-start.4 = (bf16[272,256]{1,0:T(8,128)(2,1)S(1)}, bf16[272,256]{1,0:T(8,128)(2,1)S(1)}, u32[]{:S(2)}, u32[]{:S(2)}) collective-permute-start(bf16[272,256]{1,0:T(8,128)(2,1)S(1)} %get-tuple-element.38), channel_id=1, source_target_pairs={{0,1},{1,0},{2,3},{3,2},{4,5},{5,4},{6,7},{7,6},{8,9},{9,8},{10,11... | collective-permute-start | bytes 417800 | tf_op jit(solution)/shard_map/ppermute | solution.py:391
  34.5 5.0 %collective-permute-start.3 = (bf16[256,256]{1,0:T(8,128)(2,1)S(1)}, bf16[256,256]{1,0:T(8,128)(2,1)S(1)}, u32[]{:S(2)}, u32[]{:S(2)}) collective-permute-start(bf16[256,256]{1,0:T(8,128)(2,1)S(1)} %fold.1), channel_id=1, source_target_pairs={{0,2},{1,5},{2,0},{3,7},{4,6},{5,1},{6,4},{7,3},{8,10},{9,13},{10,... | collective-permute-start | bytes 393224 | tf_op jit(solution)/shard_map/ppermute | solution.py:388

commit v8 on v7

--- a/solution.py
+++ b/solution.py
@@ -268,6 +268,14 @@
     slots, d_t = inputs.shape
     half = freqs.shape[1]
 
+    @pl.when(mine_student)
+    def _():
+        inputs[...] = other[...]
+
+    @pl.when(jnp.logical_not(mine_student))
+    def _():
+        project(student[...], head, others, inputs)
+
     tags = tags_in[...].astype(jnp.float32)
     lane = lax.broadcasted_iota(jnp.int32, (slots, LANES), 1)
     tag = jnp.sum(
@@ -278,15 +286,6 @@
     inverse = 1.0 / jnp.maximum(jnp.sum(same, axis=1, keepdims=True), 1.0)
     inverse = jnp.where(mine_student, -inverse, inverse)
     same = same.astype(jnp.bfloat16)
-
-    @pl.when(mine_student)
-    def _():
-        inputs[...] = other[...]
-
-    @pl.when(jnp.logical_not(mine_student))
-    def _():
-        project(student[...], head, others, inputs)
-
     step = min(half, 256)
     norm = jnp.zeros((slots, 1), jnp.float32)
     for index, z in enumerate(products(inputs, freqs, step)):

time: 55.5 us -> 55.3 us (level)
  no operation moved by 1% of the time
where the time goes in v8:
time: 55.3 us; the launch traced here: 55 us
  waiting for transfers between devices  15.7 us (28%)
  blocking collectives  14.6 us (26%)
  starting transfers between devices  11.1 us (20%)
  Pallas kernels  9.54 us (17%)
  local copies, waits for them, and re-layouts  3.41 us (6%)
  between operations  0.71 us (1%)
    all_to_all x1, blocking collectives, on_device(): lax.all_to_all(partial_head.reshape(n_dp // 2, out_rows, d_s), ('dp', 'fe...  14.6 us
    all_to_all x1, waiting for transfers between devices, on_device(): lax.all_to_all(sent.reshape(n_dp, capacity, width), 'dp', split_axis=0, c...  11.4 us
    all_to_all x1, starting transfers between devices, on_device(): lax.all_to_all(sent.reshape(n_dp, capacity, width), 'dp', split_axis=0, c...  8.33 us
    ppermute x2, waiting for transfers between devices, across(): return lax.ppermute(value, ('dp', 'feat'), moves)  3.56 us
    unnamed x6, local copies, waits for them, and re-layouts  3.41 us
    pallas_call x1, Pallas kernels, on_device(): pl.pallas_call(functools.partial(class_kernel, role, n_feat, n_dp, bits,...  3.05 us
    pallas_call x1, Pallas kernels, on_device(): pl.pallas_call(functools.partial(route_kernel, cls_dev, capacity), out_sh...  2.38 us
    pallas_call x1, Pallas kernels, on_device(): pl.pallas_call(functools.partial(first_kernel, role, n_feat, d_s), out_sh...  1.64 us
  transfers between devices with their start and end apart: 7, of which 5 were waited for; matrix products, arithmetic and copies ran while one was open for 0% of the time, Pallas kernels for 11%

profile of v8, /device:TPU:0, one launch (start us, length us, event | category | flops | bytes accessed | tf_op | source)
XLA Modules:
  0.0 55.0 jit_solution(16161340102100375881)
XLA Ops:
  0.6 2.4 %route.1 = (bf16[256,1024]{1,0:T(8,128)(2,1)}, f32[8,128]{1,0:T(8,128)}) custom-call(s32[128]{0:T(128)} %labels_in.1, s32[5456]{0:T(1024)} %table_in.1, bf16[128,1024]{1,0:T(8,128)(2,1)} %teacher.1, bf16[128,768]{1,0:T(8,128)(2,1)} %student.1), custom_call_target="tpu_custom_call" | custom-call | tf_op jit(solution)/shard_map/route/pallas_call | solution.py:394
  3.0 8.3 %all-to-all-start = ((bf16[16,16,1024]{2,1,0:T(8,128)(2,1)}), bf16[16,16,1024]{2,1,0:T(8,128)(2,1)S(1)}, u32[]{:S(2)}, u32[]{:S(2)}) async-start(bf16[16,16,1024]{2,1,0:T(8,128)(2,1)} %bitcast.7), calls=%async_computation | async-start | bytes 1048576 | tf_op jit(solution)/shard_map/all_to_all | solution.py:433
  11.4 0.0 copy-start
  11.4 1.6 %copy-done = bf16[1024,1024]{1,0:T(8,128)(2,1)S(1)} copy-done((bf16[1024,1024]{1,0:T(8,128)(2,1)S(1)}, bf16[1024,1024]{1,0:T(8,128)(2,1)}, u32[]{:S(2)}) %copy-start) | copy-done | bytes 2097176
  13.0 1.1 %copy-done.1 = bf16[768,512]{1,0:T(8,128)(2,1)S(1)} copy-done((bf16[768,512]{1,0:T(8,128)(2,1)S(1)}, bf16[768,512]{1,0:T(8,128)(2,1)}, u32[]{:S(2)}) %copy-start.1) | copy-done | bytes 786456
  14.1 0.7 %copy-done.2 = f32[8,128]{1,0:T(8,128)S(1)} copy-done((f32[8,128]{1,0:T(8,128)S(1)}, f32[8,128]{1,0:T(8,128)}, u32[]{:S(2)}) %copy-start.2) | copy-done | bytes 4120
  14.8 0.2 load.1
  15.0 0.1 collective-permute-start.1
  15.1 11.4 %all-to-all-done = bf16[16,16,1024]{2,1,0:T(8,128)(2,1)S(1)} async-done(((bf16[16,16,1024]{2,1,0:T(8,128)(2,1)}), bf16[16,16,1024]{2,1,0:T(8,128)(2,1)S(1)}, u32[]{:S(2)}, u32[]{:S(2)}) %all-to-all-start) | async-done | bytes 524320 | tf_op jit(solution)/shard_map/all_to_all | solution.py:433
  26.5 1.6 %first.1 = (f32[256,1024]{1,0:T(8,128)S(1)}, f32[256,1024]{1,0:T(8,128)S(1)}, bf16[1,768,512]{2,1,0:T(8,128)(2,1)S(1)}) custom-call(bf16[256,1024]{1,0:T(8,128)(2,1)S(1)} %bitcast.4, bf16[768,512]{1,0:T(8,128)(2,1)S(1)} %get-tuple-element.29.refs_0_, bf16[768,512]{1,0:T(8,128)(2,1)} %collective-permute-done.1.refs_1_, ...), custom_call_target="tpu_custom_call" | custom-call | tf_op jit(solution)/shard_map/first/pallas_call | solution.py:455
  28.1 0.3 collective-permute-done.other
  28.4 0.6 %collective-permute-start.5 = (bf16[256,768]{1,0:T(8,128)(2,1)S(1)}, bf16[256,768]{1,0:T(8,128)(2,1)S(1)}, u32[]{:S(2)}, u32[]{:S(2)}) collective-permute-start(bf16[256,768]{1,0:T(8,128)(2,1)S(1)} %get-tuple-element.39.student.refs_3_), channel_id=1, source_target_pairs={{0,2},{1,5},{2,0},{3,7},{4,6},{5,1},{6,4},{7,3},{8,10},{9,13},{10,... | collective-permute-start | bytes 1179656 | tf_op jit(solution)/shard_map/ppermute | solution.py:387
  29.1 3.0 %classes.1 = (bf16[272,256]{1,0:T(8,128)(2,1)S(1)}, bf16[256,256]{1,0:T(8,128)(2,1)S(1)}, f32[1,512]{1,0:T(1,128)S(1)}, bf16[256,1024]{1,0:T(8,128)(2,1)S(1)}) custom-call(bf16[256,1024]{1,0:T(8,128)(2,1)S(1)} %collective-permute-done.other, bf16[256,768]{1,0:T(8,128)(2,1)S(1)} %get-tuple-element.39.student.refs_3_, ...), custom_call_target="tpu_custom_call" | custom-call | tf_op jit(solution)/shard_map/classes/pallas_call | solution.py:469
  32.1 1.2 %collective-permute-start.2 = (bf16[256,256]{1,0:T(8,128)(2,1)S(1)}, bf16[256,256]{1,0:T(8,128)(2,1)S(1)}, u32[]{:S(2)}, u32[]{:S(2)}) collective-permute-start(bf16[256,256]{1,0:T(8,128)(2,1)S(1)} %get-tuple-element.36), channel_id=1, source_target_pairs={{0,1},{1,0},{2,3},{3,2},{4,5},{5,4},{6,7},{7,6},{8,9},{9,8},{10,11... | collective-permute-start | bytes 393224 | tf_op jit(solution)/shard_map/ppermute | solution.py:390
  33.4 0.1 collective-permute-start.4
  33.4 0.5 keep.1
  33.9 0.4 collective-permute-done.2.refs_1_
  34.4 0.7 %collective-permute-start.3 = (bf16[256,256]{1,0:T(8,128)(2,1)S(1)}, bf16[256,256]{1,0:T(8,128)(2,1)S(1)}, u32[]{:S(2)}, u32[]{:S(2)}) collective-permute-start(bf16[256,256]{1,0:T(8,128)(2,1)S(1)} %fold.1), channel_id=1, source_target_pairs={{0,2},{1,5},{2,0},{3,7},{4,6},{5,1},{6,4},{7,3},{8,10},{9,13},{10,... | collective-permute-start | bytes 393224 | tf_op jit(solution)/shard_map/ppermute | solution.py:387
  35.1 1.2 %collective-permute-done.5.refs_2_ = bf16[256,768]{1,0:T(8,128)(2,1)S(1)} collective-permute-done((bf16[256,768]{1,0:T(8,128)(2,1)S(1)}, bf16[256,768]{1,0:T(8,128)(2,1)S(1)}, u32[]{:S(2)}, u32[]{:S(2)}) %collective-permute-start.5) | collective-permute-done | bytes 393248 | tf_op jit(solution)/shard_map/ppermute | solution.py:387
  36.3 0.8 %own.1 = (f32[256,768]{1,0:T(8,128)S(1)}, f32[341]{0:T(512)}) custom-call(f32[256,256]{1,0:T(8,128)S(1)} %get-tuple-element.40.refs_0_, bf16[272,256]{1,0:T(8,128)(2,1)S(1)} %collective-permute-done.4.refs_1_, f32[1,512]{1,0:T(1,128)S(1)} %get-tuple-element.42.refs_2_, bf16[256,768]{1,0:T(8,128)(2,1)S(1)} %get-tuple-element.39.student.refs_3_), custom_call_target="tpu_custom_call" | custom-call | tf_op jit(solution)/shard_map/own/pallas_call | solution.py:505
  37.0 2.4 %collective-permute-done.3.refs_0_ = bf16[256,256]{1,0:T(8,128)(2,1)S(1)} collective-permute-done((bf16[256,256]{1,0:T(8,128)(2,1)S(1)}, bf16[256,256]{1,0:T(8,128)(2,1)S(1)}, u32[]{:S(2)}, u32[]{:S(2)}) %collective-permute-start.3) | collective-permute-done | bytes 131104 | tf_op jit(solution)/shard_map/ppermute | solution.py:387
  39.4 0.3 head.1
  39.7 14.6 %all_to_all.10.parts = bf16[8,32,768]{2,1,0:T(8,128)(2,1)S(1)} all-to-all(bf16[8,32,768]{2,1,0:T(8,128)(2,1)S(1)} %bitcast.6), channel_id=1, replica_groups={{0,4,8,12,16,20,24,28},{2,6,10,14,18,22,26,30},{1,3,9,11,17,19,25,27},{..., dimensions={0} | all-to-all | bytes 786432 | tf_op jit(solution)/shard_map/all_to_all | solution.py:520
  54.3 0.7 %total.1 = f32[32,768]{1,0:T(8,128)} custom-call(bf16[8,32,768]{2,1,0:T(8,128)(2,1)S(1)} %all_to_all.10.parts), custom_call_target="tpu_custom_call" | custom-call | tf_op jit(solution)/shard_map/total/pallas_call | solution.py:532
  (7 shorter events, 0.1 us)
Async XLA Ops:
  3.0 23.5 %all-to-all-start = ((bf16[16,16,1024]{2,1,0:T(8,128)(2,1)}), bf16[16,16,1024]{2,1,0:T(8,128)(2,1)S(1)}, u32[]{:S(2)}, u32[]{:S(2)}) async-start(bf16[16,16,1024]{2,1,0:T(8,128)(2,1)} %bitcast.7), calls=%async_computation | async-start | bytes 1048576 | tf_op jit(solution)/shard_map/all_to_all | solution.py:433
  11.4 1.6 %copy-start = (bf16[1024,1024]{1,0:T(8,128)(2,1)S(1)}, bf16[1024,1024]{1,0:T(8,128)(2,1)}, u32[]{:S(2)}) copy-start(bf16[1024,1024]{1,0:T(8,128)(2,1)} %freqs_in.1) | copy-start | bytes 6291460
  13.0 1.1 %copy-start.1 = (bf16[768,512]{1,0:T(8,128)(2,1)S(1)}, bf16[768,512]{1,0:T(8,128)(2,1)}, u32[]{:S(2)}) copy-start(bf16[768,512]{1,0:T(8,128)(2,1)} %head_in.1) | copy-start | bytes 2359300
  14.1 0.7 %copy-start.2 = (f32[8,128]{1,0:T(8,128)S(1)}, f32[8,128]{1,0:T(8,128)}, u32[]{:S(2)}) copy-start(f32[8,128]{1,0:T(8,128)} %get-tuple-element.24._) | copy-start | bytes 12292
  15.0 11.5 %collective-permute-start.1 = (bf16[768,512]{1,0:T(8,128)(2,1)S(1)}, bf16[768,512]{1,0:T(8,128)(2,1)}, u32[]{:S(2)}, u32[]{:S(2)}) collective-permute-start(bf16[768,512]{1,0:T(8,128)(2,1)S(1)} %get-tuple-element.29.refs_0_), channel_id=1, source_target_pairs={{0,1},{1,0},{2,3},{3,2},{4,5},{5,4},{6,7},{7,6},{8,9},{9,8},{10,11... | collective-permute-start | bytes 2359304 | tf_op jit(solution)/shard_map/ppermute | solution.py:390
  26.5 1.9 %collective-permute-start = (bf16[256,1024]{1,0:T(8,128)(2,1)S(1)}, bf16[256,1024]{1,0:T(8,128)(2,1)S(1)}, u32[]{:S(2)}, u32[]{:S(2)}) collective-permute-start(bf16[256,1024]{1,0:T(8,128)(2,1)S(1)} %bitcast.3), channel_id=1, source_target_pairs={{0,1},{1,0},{2,3},{3,2},{4,5},{5,4},{6,7},{7,6},{8,9},{9,8},{10,11... | collective-permute-start | bytes 1572872 | tf_op jit(solution)/shard_map/ppermute | solution.py:390
  28.4 7.8 %collective-permute-start.5 = (bf16[256,768]{1,0:T(8,128)(2,1)S(1)}, bf16[256,768]{1,0:T(8,128)(2,1)S(1)}, u32[]{:S(2)}, u32[]{:S(2)}) collective-permute-start(bf16[256,768]{1,0:T(8,128)(2,1)S(1)} %get-tuple-element.39.student.refs_3_), channel_id=1, source_target_pairs={{0,2},{1,5},{2,0},{3,7},{4,6},{5,1},{6,4},{7,3},{8,10},{9,13},{10,... | collective-permute-start | bytes 1179656 | tf_op jit(solution)/shard_map/ppermute | solution.py:387
  32.1 2.2 %collective-permute-start.2 = (bf16[256,256]{1,0:T(8,128)(2,1)S(1)}, bf16[256,256]{1,0:T(8,128)(2,1)S(1)}, u32[]{:S(2)}, u32[]{:S(2)}) collective-permute-start(bf16[256,256]{1,0:T(8,128)(2,1)S(1)} %get-tuple-element.36), channel_id=1, source_target_pairs={{0,1},{1,0},{2,3},{3,2},{4,5},{5,4},{6,7},{7,6},{8,9},{9,8},{10,11... | collective-permute-start | bytes 393224 | tf_op jit(solution)/shard_map/ppermute | solution.py:390
  33.4 1.7 %collective-permute-start.4 = (bf16[272,256]{1,0:T(8,128)(2,1)S(1)}, bf16[272,256]{1,0:T(8,128)(2,1)S(1)}, u32[]{:S(2)}, u32[]{:S(2)}) collective-permute-start(bf16[272,256]{1,0:T(8,128)(2,1)S(1)} %get-tuple-element.38), channel_id=1, source_target_pairs={{0,1},{1,0},{2,3},{3,2},{4,5},{5,4},{6,7},{7,6},{8,9},{9,8},{10,11... | collective-permute-start | bytes 417800 | tf_op jit(solution)/shard_map/ppermute | solution.py:390
  34.4 5.0 %collective-permute-start.3 = (bf16[256,256]{1,0:T(8,128)(2,1)S(1)}, bf16[256,256]{1,0:T(8,128)(2,1)S(1)}, u32[]{:S(2)}, u32[]{:S(2)}) collective-permute-start(bf16[256,256]{1,0:T(8,128)(2,1)S(1)} %fold.1), channel_id=1, source_target_pairs={{0,2},{1,5},{2,0},{3,7},{4,6},{5,1},{6,4},{7,3},{8,10},{9,13},{10,... | collective-permute-start | bytes 393224 | tf_op jit(solution)/shard_map/ppermute | solution.py:387

commit v9 on v8

--- a/solution.py
+++ b/solution.py
@@ -139,17 +139,22 @@
     return jnp.concatenate(found, axis=1) if width > 1 else found[0]
 
 
-def place_of(own, offset, count):
-    return lax.rem(own + (count - offset), count)
-
-
-def project(student, head, others, projected):
-    feat = lax.axis_index("feat")
+def lane_start(own, offset, count, part):
+    if isinstance(own, int):
+        return (own - offset) % count * part
+    return pl.multiple_of(lax.rem(own + (count - offset), count) * part, LANES)
+
+
+def holder_of(role, index):
+    return index if role is None else lax.axis_index("feat")
+
+
+def project(feat, student, head, others, projected):
     part = head.shape[1]
     count = projected.shape[1] // part
     for offset in range(count):
         weight = others[offset - 1] if offset else head[...]
-        start = pl.multiple_of(place_of(feat, offset, count) * part, LANES)
+        start = lane_start(feat, offset, count, part)
         projected[:, pl.ds(start, part)] = jnp.dot(
             student, weight, preferred_element_type=jnp.float32
         ).astype(jnp.bfloat16)
@@ -171,13 +176,24 @@
 def first_kernel(role, n_feat, d_s, rows, *refs):
     heads, (freqs, cos, sin, near, inputs, sems) = refs[:n_feat], refs[n_feat:]
     is_student = is_role(role, 1)
+    rows_each = d_s // PIECES
     copies = [
-        pltpu.make_async_copy(heads[k], near.at[k - 1], sems.at[k - 1]) for k in range(1, n_feat)
+        [
+            pltpu.make_async_copy(
+                heads[k].at[pl.ds(piece * rows_each, rows_each)],
+                near.at[k - 1, pl.ds(piece * rows_each, rows_each)],
+                sems.at[k - 1, piece],
+            )
+            for piece in range(PIECES)
+        ]
+        for k in range(1, n_feat)
     ]
-    for copy in copies:
-        copy.start()
+    for group in copies:
+        for copy in group:
+            copy.start()
     part = freqs.shape[0] // n_feat
-    own = pl.multiple_of(lax.axis_index("feat") * part, LANES)
+    feat = holder_of(role, 1)
+    own = lane_start(feat, 0, n_feat, part)
 
     @pl.when(is_student)
     def _():
@@ -193,12 +209,13 @@
     blocks = [slice(c, c + step) for c in range(0, freqs.shape[1], step)]
     found = [0.0] * len(blocks)
     for offset in range(n_feat):
-        start = pl.multiple_of(place_of(lax.axis_index("feat"), offset, n_feat) * part, LANES)
+        start = lane_start(feat, offset, n_feat, part)
         if offset:
 
             @pl.when(is_student)
             def _():
-                copies[offset - 1].wait()
+                for copy in copies[offset - 1]:
+                    copy.wait()
                 inputs[:, pl.ds(start, part)] = jnp.dot(
                     rows[:, :d_s], near[offset - 1], preferred_element_type=jnp.float32
                 ).astype(jnp.bfloat16)
@@ -214,8 +231,9 @@
 
     @pl.when(jnp.logical_not(is_student))
     def _():
-        for copy in copies:
-            copy.wait()
+        for group in copies:
+            for copy in group:
+                copy.wait()
 
 
 def sort_kernel(mine, other, student, tags):
@@ -274,7 +292,7 @@
 
     @pl.when(jnp.logical_not(mine_student))
     def _():
-        project(student[...], head, others, inputs)
+        project(holder_of(role, 0), student[...], head, others, inputs)
 
     tags = tags_in[...].astype(jnp.float32)
     lane = lax.broadcasted_iota(jnp.int32, (slots, LANES), 1)
@@ -459,7 +477,7 @@
         in_specs=[near] * 2 + [hbm] * (n_feat - 1) + [near],
         scratch_shapes=[
             pltpu.VMEM((slots, d_t), jnp.bfloat16),
-            pltpu.SemaphoreType.DMA((n_feat - 1,)),
+            pltpu.SemaphoreType.DMA((n_feat - 1, PIECES)),
         ],
         compiler_params=vmem,
         name="first",

time: 55.3 us -> 55.3 us (level)
  no operation moved by 1% of the time
where the time goes in v9:
time: 55.3 us; the launch traced here: 55 us
  waiting for transfers between devices  15.6 us (28%)
  blocking collectives  14.6 us (26%)
  starting transfers between devices  11.1 us (20%)
  Pallas kernels  9.57 us (17%)
  local copies, waits for them, and re-layouts  3.41 us (6%)
  between operations  0.71 us (1%)
    all_to_all x1, blocking collectives, on_device(): lax.all_to_all(partial_head.reshape(n_dp // 2, out_rows, d_s), ('dp', 'fe...  14.6 us
    all_to_all x1, waiting for transfers between devices, on_device(): lax.all_to_all(sent.reshape(n_dp, capacity, width), 'dp', split_axis=0, c...  11.4 us
    all_to_all x1, starting transfers between devices, on_device(): lax.all_to_all(sent.reshape(n_dp, capacity, width), 'dp', split_axis=0, c...  8.33 us
    ppermute x2, waiting for transfers between devices, across(): return lax.ppermute(value, ('dp', 'feat'), moves)  3.55 us
    unnamed x6, local copies, waits for them, and re-layouts  3.41 us
    pallas_call x1, Pallas kernels, on_device(): pl.pallas_call(functools.partial(class_kernel, role, n_feat, n_dp, bits,...  3.05 us
    pallas_call x1, Pallas kernels, on_device(): pl.pallas_call(functools.partial(route_kernel, cls_dev, capacity), out_sh...  2.38 us
    pallas_call x1, Pallas kernels, on_device(): pl.pallas_call(functools.partial(first_kernel, role, n_feat, d_s), out_sh...  1.67 us
  transfers between devices with their start and end apart: 7, of which 5 were waited for; matrix products, arithmetic and copies ran while one was open for 0% of the time, Pallas kernels for 11%

profile of v9, /device:TPU:0, one launch (start us, length us, event | category | flops | bytes accessed | tf_op | source)
XLA Modules:
  0.0 55.0 jit_solution(7384364845076063660)
XLA Ops:
  0.6 2.4 %route.1 = (bf16[256,1024]{1,0:T(8,128)(2,1)}, f32[8,128]{1,0:T(8,128)}) custom-call(s32[128]{0:T(128)} %labels_in.1, s32[5456]{0:T(1024)} %table_in.1, bf16[128,1024]{1,0:T(8,128)(2,1)} %teacher.1, bf16[128,768]{1,0:T(8,128)(2,1)} %student.1), custom_call_target="tpu_custom_call" | custom-call | tf_op jit(solution)/shard_map/route/pallas_call | solution.py:412
  3.0 8.3 %all-to-all-start = ((bf16[16,16,1024]{2,1,0:T(8,128)(2,1)}), bf16[16,16,1024]{2,1,0:T(8,128)(2,1)S(1)}, u32[]{:S(2)}, u32[]{:S(2)}) async-start(bf16[16,16,1024]{2,1,0:T(8,128)(2,1)} %bitcast.7), calls=%async_computation | async-start | bytes 1048576 | tf_op jit(solution)/shard_map/all_to_all | solution.py:451
  11.4 0.0 copy-start
  11.4 1.6 %copy-done = bf16[1024,1024]{1,0:T(8,128)(2,1)S(1)} copy-done((bf16[1024,1024]{1,0:T(8,128)(2,1)S(1)}, bf16[1024,1024]{1,0:T(8,128)(2,1)}, u32[]{:S(2)}) %copy-start) | copy-done | bytes 2097176
  13.0 1.1 %copy-done.1 = bf16[768,512]{1,0:T(8,128)(2,1)S(1)} copy-done((bf16[768,512]{1,0:T(8,128)(2,1)S(1)}, bf16[768,512]{1,0:T(8,128)(2,1)}, u32[]{:S(2)}) %copy-start.1) | copy-done | bytes 786456
  14.1 0.7 %copy-done.2 = f32[8,128]{1,0:T(8,128)S(1)} copy-done((f32[8,128]{1,0:T(8,128)S(1)}, f32[8,128]{1,0:T(8,128)}, u32[]{:S(2)}) %copy-start.2) | copy-done | bytes 4120
  14.8 0.2 load.1
  15.0 0.1 collective-permute-start.1
  15.1 11.4 %all-to-all-done = bf16[16,16,1024]{2,1,0:T(8,128)(2,1)S(1)} async-done(((bf16[16,16,1024]{2,1,0:T(8,128)(2,1)}), bf16[16,16,1024]{2,1,0:T(8,128)(2,1)S(1)}, u32[]{:S(2)}, u32[]{:S(2)}) %all-to-all-start) | async-done | bytes 524320 | tf_op jit(solution)/shard_map/all_to_all | solution.py:451
  26.5 1.7 %first.1 = (f32[256,1024]{1,0:T(8,128)S(1)}, f32[256,1024]{1,0:T(8,128)S(1)}, bf16[1,768,512]{2,1,0:T(8,128)(2,1)S(1)}) custom-call(bf16[256,1024]{1,0:T(8,128)(2,1)S(1)} %bitcast.4, bf16[768,512]{1,0:T(8,128)(2,1)S(1)} %get-tuple-element.29.refs_0_, bf16[768,512]{1,0:T(8,128)(2,1)} %collective-permute-done.1.refs_1_, ...), custom_call_target="tpu_custom_call" | custom-call | tf_op jit(solution)/shard_map/first/pallas_call | solution.py:473
  28.2 0.2 collective-permute-done.other
  28.4 0.6 %collective-permute-start.5 = (bf16[256,768]{1,0:T(8,128)(2,1)S(1)}, bf16[256,768]{1,0:T(8,128)(2,1)S(1)}, u32[]{:S(2)}, u32[]{:S(2)}) collective-permute-start(bf16[256,768]{1,0:T(8,128)(2,1)S(1)} %get-tuple-element.39.student.refs_3_), channel_id=1, source_target_pairs={{0,2},{1,5},{2,0},{3,7},{4,6},{5,1},{6,4},{7,3},{8,10},{9,13},{10,... | collective-permute-start | bytes 1179656 | tf_op jit(solution)/shard_map/ppermute | solution.py:405
  29.1 3.0 %classes.1 = (bf16[272,256]{1,0:T(8,128)(2,1)S(1)}, bf16[256,256]{1,0:T(8,128)(2,1)S(1)}, f32[1,512]{1,0:T(1,128)S(1)}, bf16[256,1024]{1,0:T(8,128)(2,1)S(1)}) custom-call(bf16[256,1024]{1,0:T(8,128)(2,1)S(1)} %collective-permute-done.other, bf16[256,768]{1,0:T(8,128)(2,1)S(1)} %get-tuple-element.39.student.refs_3_, ...), custom_call_target="tpu_custom_call" | custom-call | tf_op jit(solution)/shard_map/classes/pallas_call | solution.py:487
  32.1 1.2 %collective-permute-start.2 = (bf16[256,256]{1,0:T(8,128)(2,1)S(1)}, bf16[256,256]{1,0:T(8,128)(2,1)S(1)}, u32[]{:S(2)}, u32[]{:S(2)}) collective-permute-start(bf16[256,256]{1,0:T(8,128)(2,1)S(1)} %get-tuple-element.36), channel_id=1, source_target_pairs={{0,1},{1,0},{2,3},{3,2},{4,5},{5,4},{6,7},{7,6},{8,9},{9,8},{10,11... | collective-permute-start | bytes 393224 | tf_op jit(solution)/shard_map/ppermute | solution.py:408
  33.4 0.1 collective-permute-start.4
  33.4 0.5 keep.1
  33.9 0.4 collective-permute-done.2.refs_1_
  34.4 0.7 %collective-permute-start.3 = (bf16[256,256]{1,0:T(8,128)(2,1)S(1)}, bf16[256,256]{1,0:T(8,128)(2,1)S(1)}, u32[]{:S(2)}, u32[]{:S(2)}) collective-permute-start(bf16[256,256]{1,0:T(8,128)(2,1)S(1)} %fold.1), channel_id=1, source_target_pairs={{0,2},{1,5},{2,0},{3,7},{4,6},{5,1},{6,4},{7,3},{8,10},{9,13},{10,... | collective-permute-start | bytes 393224 | tf_op jit(solution)/shard_map/ppermute | solution.py:405
  35.1 1.2 %collective-permute-done.5.refs_2_ = bf16[256,768]{1,0:T(8,128)(2,1)S(1)} collective-permute-done((bf16[256,768]{1,0:T(8,128)(2,1)S(1)}, bf16[256,768]{1,0:T(8,128)(2,1)S(1)}, u32[]{:S(2)}, u32[]{:S(2)}) %collective-permute-start.5) | collective-permute-done | bytes 393248 | tf_op jit(solution)/shard_map/ppermute | solution.py:405
  36.3 0.8 %own.1 = (f32[256,768]{1,0:T(8,128)S(1)}, f32[341]{0:T(512)}) custom-call(f32[256,256]{1,0:T(8,128)S(1)} %get-tuple-element.40.refs_0_, bf16[272,256]{1,0:T(8,128)(2,1)S(1)} %collective-permute-done.4.refs_1_, f32[1,512]{1,0:T(1,128)S(1)} %get-tuple-element.42.refs_2_, bf16[256,768]{1,0:T(8,128)(2,1)S(1)} %get-tuple-element.39.student.refs_3_), custom_call_target="tpu_custom_call" | custom-call | tf_op jit(solution)/shard_map/own/pallas_call | solution.py:523
  37.0 2.4 %collective-permute-done.3.refs_0_ = bf16[256,256]{1,0:T(8,128)(2,1)S(1)} collective-permute-done((bf16[256,256]{1,0:T(8,128)(2,1)S(1)}, bf16[256,256]{1,0:T(8,128)(2,1)S(1)}, u32[]{:S(2)}, u32[]{:S(2)}) %collective-permute-start.3) | collective-permute-done | bytes 131104 | tf_op jit(solution)/shard_map/ppermute | solution.py:405
  39.4 0.3 head.1
  39.7 14.6 %all_to_all.10.parts = bf16[8,32,768]{2,1,0:T(8,128)(2,1)S(1)} all-to-all(bf16[8,32,768]{2,1,0:T(8,128)(2,1)S(1)} %bitcast.6), channel_id=1, replica_groups={{0,4,8,12,16,20,24,28},{2,6,10,14,18,22,26,30},{1,3,9,11,17,19,25,27},{..., dimensions={0} | all-to-all | bytes 786432 | tf_op jit(solution)/shard_map/all_to_all | solution.py:538
  54.3 0.7 %total.1 = f32[32,768]{1,0:T(8,128)} custom-call(bf16[8,32,768]{2,1,0:T(8,128)(2,1)S(1)} %all_to_all.10.parts), custom_call_target="tpu_custom_call" | custom-call | tf_op jit(solution)/shard_map/total/pallas_call | solution.py:550
  (7 shorter events, 0.1 us)
Async XLA Ops:
  3.0 23.5 %all-to-all-start = ((bf16[16,16,1024]{2,1,0:T(8,128)(2,1)}), bf16[16,16,1024]{2,1,0:T(8,128)(2,1)S(1)}, u32[]{:S(2)}, u32[]{:S(2)}) async-start(bf16[16,16,1024]{2,1,0:T(8,128)(2,1)} %bitcast.7), calls=%async_computation | async-start | bytes 1048576 | tf_op jit(solution)/shard_map/all_to_all | solution.py:451
  11.4 1.6 %copy-start = (bf16[1024,1024]{1,0:T(8,128)(2,1)S(1)}, bf16[1024,1024]{1,0:T(8,128)(2,1)}, u32[]{:S(2)}) copy-start(bf16[1024,1024]{1,0:T(8,128)(2,1)} %freqs_in.1) | copy-start | bytes 6291460
  13.0 1.1 %copy-start.1 = (bf16[768,512]{1,0:T(8,128)(2,1)S(1)}, bf16[768,512]{1,0:T(8,128)(2,1)}, u32[]{:S(2)}) copy-start(bf16[768,512]{1,0:T(8,128)(2,1)} %head_in.1) | copy-start | bytes 2359300
  14.1 0.7 %copy-start.2 = (f32[8,128]{1,0:T(8,128)S(1)}, f32[8,128]{1,0:T(8,128)}, u32[]{:S(2)}) copy-start(f32[8,128]{1,0:T(8,128)} %get-tuple-element.24._) | copy-start | bytes 12292
  15.0 11.5 %collective-permute-start.1 = (bf16[768,512]{1,0:T(8,128)(2,1)S(1)}, bf16[768,512]{1,0:T(8,128)(2,1)}, u32[]{:S(2)}, u32[]{:S(2)}) collective-permute-start(bf16[768,512]{1,0:T(8,128)(2,1)S(1)} %get-tuple-element.29.refs_0_), channel_id=1, source_target_pairs={{0,1},{1,0},{2,3},{3,2},{4,5},{5,4},{6,7},{7,6},{8,9},{9,8},{10,11... | collective-permute-start | bytes 2359304 | tf_op jit(solution)/shard_map/ppermute | solution.py:408
  26.5 1.9 %collective-permute-start = (bf16[256,1024]{1,0:T(8,128)(2,1)S(1)}, bf16[256,1024]{1,0:T(8,128)(2,1)S(1)}, u32[]{:S(2)}, u32[]{:S(2)}) collective-permute-start(bf16[256,1024]{1,0:T(8,128)(2,1)S(1)} %bitcast.3), channel_id=1, source_target_pairs={{0,1},{1,0},{2,3},{3,2},{4,5},{5,4},{6,7},{7,6},{8,9},{9,8},{10,11... | collective-permute-start | bytes 1572872 | tf_op jit(solution)/shard_map/ppermute | solution.py:408
  28.4 7.8 %collective-permute-start.5 = (bf16[256,768]{1,0:T(8,128)(2,1)S(1)}, bf16[256,768]{1,0:T(8,128)(2,1)S(1)}, u32[]{:S(2)}, u32[]{:S(2)}) collective-permute-start(bf16[256,768]{1,0:T(8,128)(2,1)S(1)} %get-tuple-element.39.student.refs_3_), channel_id=1, source_target_pairs={{0,2},{1,5},{2,0},{3,7},{4,6},{5,1},{6,4},{7,3},{8,10},{9,13},{10,... | collective-permute-start | bytes 1179656 | tf_op jit(solution)/shard_map/ppermute | solution.py:405
  32.1 2.2 %collective-permute-start.2 = (bf16[256,256]{1,0:T(8,128)(2,1)S(1)}, bf16[256,256]{1,0:T(8,128)(2,1)S(1)}, u32[]{:S(2)}, u32[]{:S(2)}) collective-permute-start(bf16[256,256]{1,0:T(8,128)(2,1)S(1)} %get-tuple-element.36), channel_id=1, source_target_pairs={{0,1},{1,0},{2,3},{3,2},{4,5},{5,4},{6,7},{7,6},{8,9},{9,8},{10,11... | collective-permute-start | bytes 393224 | tf_op jit(solution)/shard_map/ppermute | solution.py:408
  33.4 1.7 %collective-permute-start.4 = (bf16[272,256]{1,0:T(8,128)(2,1)S(1)}, bf16[272,256]{1,0:T(8,128)(2,1)S(1)}, u32[]{:S(2)}, u32[]{:S(2)}) collective-permute-start(bf16[272,256]{1,0:T(8,128)(2,1)S(1)} %get-tuple-element.38), channel_id=1, source_target_pairs={{0,1},{1,0},{2,3},{3,2},{4,5},{5,4},{6,7},{7,6},{8,9},{9,8},{10,11... | collective-permute-start | bytes 417800 | tf_op jit(solution)/shard_map/ppermute | solution.py:408
  34.4 5.0 %collective-permute-start.3 = (bf16[256,256]{1,0:T(8,128)(2,1)S(1)}, bf16[256,256]{1,0:T(8,128)(2,1)S(1)}, u32[]{:S(2)}, u32[]{:S(2)}) collective-permute-start(bf16[256,256]{1,0:T(8,128)(2,1)S(1)} %fold.1), channel_id=1, source_target_pairs={{0,2},{1,5},{2,0},{3,7},{4,6},{5,1},{6,4},{7,3},{8,10},{9,13},{10,... | collective-permute-start | bytes 393224 | tf_op jit(solution)/shard_map/ppermute | solution.py:405

commit v10 on v9

--- a/solution.py
+++ b/solution.py
@@ -253,24 +253,26 @@
     return jnp.where(bit == 0, low, high)
 
 
-def grad_rows(offset, n_feat, n_dp, bits, weight, freqs, grad_z, picked):
+def grad_rows(offset, sides, n_feat, n_dp, bits, weight, freqs, grad_z, picked):
     holder = lax.axis_index("dp")
     target = lax.rem(lax.axis_index("feat") + offset, n_feat)
     bit = lax.rem(target, bits)
     side = jnp.where(bit == 0, lax.rem(holder, 2), lax.rem(holder // 2, 2))
+    half = n_dp // 2
     out_rows = picked.shape[0] // n_dp
+    span = slice(sides[0] * half * out_rows, (sides[-1] + 1) * half * out_rows)
     if weight is not None:
-        picked[...] = weight
+        picked[span, :] = weight[span]
     else:
-        for index in range(n_dp):
-            across, group = divmod(index, n_dp // 2)
+        for index in range(sides[0] * half, (sides[-1] + 1) * half):
+            across, group = divmod(index, half)
             member = member_of(group, bit, 1 - side if across else side)
             start = pl.multiple_of((member * n_feat + target) * out_rows, out_rows)
             picked[index * out_rows : (index + 1) * out_rows, :] = freqs[
                 pl.ds(start, out_rows), :
             ]
     return lax.dot_general(
-        picked[...], grad_z[...], (((1,), (1,)), ((), ())), preferred_element_type=jnp.float32
+        picked[span, :], grad_z[...], (((1,), (1,)), ((), ())), preferred_element_type=jnp.float32
     )
 
 
@@ -280,7 +282,7 @@
     head, others, freqs, refs = refs[0], refs[1], refs[2], refs[3:]
     if permuted:
         weights, refs = refs[0], refs[1:]
-    grads, refs = refs[: 2 * n_feat - 2], refs[2 * n_feat - 2 :]
+    grads, refs = refs[: n_feat - 1], refs[n_feat - 1 :]
     norms, grad_z, inputs, picked = refs
     mine_student = is_role(role, 1)
     slots, d_t = inputs.shape
@@ -323,24 +325,25 @@
     cls = lax.broadcasted_iota(jnp.int32, (slots, cls_pad), 1).astype(jnp.float32) + 1.0
     total_norm = jnp.sum(jnp.where(cls == tag, norm, 0.0), axis=0, keepdims=True)
     norms[...] = total_norm
-    carried = carry(total_norm, slots)
-    block = picked.shape[0] // 2
     for offset in range(1, n_feat):
         weight = weights[offset] if permuted else None
-        product = grad_rows(offset, n_feat, n_dp, bits, weight, freqs, grad_z, picked)
-        here, there = grads[offset - 1], grads[n_feat + offset - 2]
+        product = grad_rows(offset, (1,), n_feat, n_dp, bits, weight, freqs, grad_z, picked)
+        grads[offset - 1][...] = product.astype(jnp.bfloat16)
+
+
+def keep_kernel(n_feat, n_dp, bits, permuted, *refs):
+    weights, (freqs, grad_z, norms, *heres, there, picked) = refs[:permuted], refs[permuted:]
+    block = picked.shape[0] // 2
+    for offset in range(n_feat):
+        weight = weights[0][offset] if permuted else None
+        sides = (0,) if offset else (0, 1)
+        product = grad_rows(offset, sides, n_feat, n_dp, bits, weight, freqs, grad_z, picked)
+        here = heres[offset]
         here[:block, :] = product[:block].astype(here.dtype)
-        here[block:, :] = carried
-        there[...] = product[block:].astype(there.dtype)
-
-
-def keep_kernel(n_feat, n_dp, bits, permuted, *refs):
-    weights, (freqs, grad_z, here, there, picked) = refs[:-5], refs[-5:]
-    weight = weights[0][0] if permuted else None
-    product = grad_rows(0, n_feat, n_dp, bits, weight, freqs, grad_z, picked)
-    block = picked.shape[0] // 2
-    here[...] = product[:block]
-    there[...] = product[block:]
+        if offset:
+            here[block:, :] = carry(norms[...], here.shape[1])
+        else:
+            there[...] = product[block:]
 
 
 def summed(refs, size):
@@ -486,8 +489,7 @@
     student_across = across(student_out)
     *grads, norms, grad_z = pl.pallas_call(
         functools.partial(class_kernel, role, n_feat, n_dp, bits, cls_pad, permuted),
-        out_shape=(jax.ShapeDtypeStruct((block + CARRIED, slots), jnp.bfloat16),) * (n_feat - 1)
-        + (jax.ShapeDtypeStruct((block, slots), jnp.bfloat16),) * (n_feat - 1)
+        out_shape=(jax.ShapeDtypeStruct((block, slots), jnp.bfloat16),) * (n_feat - 1)
         + (
             jax.ShapeDtypeStruct((1, cls_pad), jnp.float32),
             jax.ShapeDtypeStruct((slots, half), jnp.bfloat16),
@@ -502,15 +504,17 @@
     )(
         other, student_in, tags_in, cos, sin, heads[0], head_others, freqs_near, *weights
     )
-    here_own, there_own = pl.pallas_call(
-        functools.partial(keep_kernel, n_feat, n_dp, bits, permuted),
-        out_shape=(jax.ShapeDtypeStruct((block, slots), jnp.float32),) * 2,
+    own_block = jax.ShapeDtypeStruct((block, slots), jnp.float32)
+    sent_block = jax.ShapeDtypeStruct((block + CARRIED, slots), jnp.bfloat16)
+    here_own, *here_others, there_own = pl.pallas_call(
+        functools.partial(keep_kernel, n_feat, n_dp, bits, int(permuted)),
+        out_shape=(own_block,) + (sent_block,) * (n_feat - 1) + (own_block,),
         scratch_shapes=[pltpu.VMEM((2 * block, half), jnp.bfloat16)],
         compiler_params=vmem,
         name="keep",
-    )(*weights, freqs_near, grad_z)
-    here = [here_own] + [shifted(grads[k - 1], k) for k in range(1, n_feat)]
-    there = [there_own] + [shifted(grads[n_feat + k - 2], k) for k in range(1, n_feat)]
+    )(*weights, freqs_near, grad_z, norms)
+    here = [here_own] + [shifted(here_others[k - 1], k) for k in range(1, n_feat)]
+    there = [there_own] + [shifted(grads[k - 1], k) for k in range(1, n_feat)]
     folded = pl.pallas_call(
         fold_kernel,
         out_shape=jax.ShapeDtypeStruct((block, slots), jnp.bfloat16),

time: 55.3 us -> 55.1 us (level)
  transfers between devices with their start and end apart: 7 -> 7, of which waited for: 5 -> 6; matrix products, arithmetic and copies ran while one was open for 0% -> 0% of each run, Pallas kernels for 11% -> 11%
where the time goes in v10:
time: 55.1 us; the launch traced here: 54.7 us
  waiting for transfers between devices  15.5 us (28%)
  blocking collectives  14.6 us (26%)
  starting transfers between devices  11.1 us (20%)
  Pallas kernels  9.46 us (17%)
  local copies, waits for them, and re-layouts  3.41 us (6%)
  between operations  0.72 us (1%)
    all_to_all x1, blocking collectives, on_device(): lax.all_to_all(partial_head.reshape(n_dp // 2, out_rows, d_s), ('dp', 'fe...  14.6 us
    all_to_all x1, waiting for transfers between devices, on_device(): lax.all_to_all(sent.reshape(n_dp, capacity, width), 'dp', split_axis=0, c...  11.4 us
    all_to_all x1, starting transfers between devices, on_device(): lax.all_to_all(sent.reshape(n_dp, capacity, width), 'dp', split_axis=0, c...  8.33 us
    unnamed x6, local copies, waits for them, and re-layouts  3.41 us
    ppermute x2, waiting for transfers between devices, across(): return lax.ppermute(value, ('dp', 'feat'), moves)  3.26 us
    pallas_call x1, Pallas kernels, on_device(): pl.pallas_call(functools.partial(class_kernel, role, n_feat, n_dp, bits,...  2.79 us
    pallas_call x1, Pallas kernels, on_device(): pl.pallas_call(functools.partial(route_kernel, cls_dev, capacity), out_sh...  2.38 us
    pallas_call x1, Pallas kernels, on_device(): pl.pallas_call(functools.partial(first_kernel, role, n_feat, d_s), out_sh...  1.67 us
  transfers between devices with their start and end apart: 7, of which 6 were waited for; matrix products, arithmetic and copies ran while one was open for 0% of the time, Pallas kernels for 11%

profile of v10, /device:TPU:0, one launch (start us, length us, event | category | flops | bytes accessed | tf_op | source)
XLA Modules:
  0.0 54.7 jit_solution(3503328255376444659)
XLA Ops:
  0.6 2.4 %route.1 = (bf16[256,1024]{1,0:T(8,128)(2,1)}, f32[8,128]{1,0:T(8,128)}) custom-call(s32[128]{0:T(128)} %labels_in.1, s32[5456]{0:T(1024)} %table_in.1, bf16[128,1024]{1,0:T(8,128)(2,1)} %teacher.1, bf16[128,768]{1,0:T(8,128)(2,1)} %student.1), custom_call_target="tpu_custom_call" | custom-call | tf_op jit(solution)/shard_map/route/pallas_call | solution.py:415
  3.0 8.3 %all-to-all-start = ((bf16[16,16,1024]{2,1,0:T(8,128)(2,1)}), bf16[16,16,1024]{2,1,0:T(8,128)(2,1)S(1)}, u32[]{:S(2)}, u32[]{:S(2)}) async-start(bf16[16,16,1024]{2,1,0:T(8,128)(2,1)} %bitcast.7), calls=%async_computation | async-start | bytes 1048576 | tf_op jit(solution)/shard_map/all_to_all | solution.py:454
  11.4 1.6 %copy-done = bf16[1024,1024]{1,0:T(8,128)(2,1)S(1)} copy-done((bf16[1024,1024]{1,0:T(8,128)(2,1)S(1)}, bf16[1024,1024]{1,0:T(8,128)(2,1)}, u32[]{:S(2)}) %copy-start) | copy-done | bytes 2097176
  13.0 1.1 %copy-done.1 = bf16[768,512]{1,0:T(8,128)(2,1)S(1)} copy-done((bf16[768,512]{1,0:T(8,128)(2,1)S(1)}, bf16[768,512]{1,0:T(8,128)(2,1)}, u32[]{:S(2)}) %copy-start.1) | copy-done | bytes 786456
  14.1 0.7 %copy-done.2 = f32[8,128]{1,0:T(8,128)S(1)} copy-done((f32[8,128]{1,0:T(8,128)S(1)}, f32[8,128]{1,0:T(8,128)}, u32[]{:S(2)}) %copy-start.2) | copy-done | bytes 4120
  14.8 0.2 load.1
  15.0 0.1 collective-permute-start.1
  15.1 11.4 %all-to-all-done = bf16[16,16,1024]{2,1,0:T(8,128)(2,1)S(1)} async-done(((bf16[16,16,1024]{2,1,0:T(8,128)(2,1)}), bf16[16,16,1024]{2,1,0:T(8,128)(2,1)S(1)}, u32[]{:S(2)}, u32[]{:S(2)}) %all-to-all-start) | async-done | bytes 524320 | tf_op jit(solution)/shard_map/all_to_all | solution.py:454
  26.5 1.7 %first.1 = (f32[256,1024]{1,0:T(8,128)S(1)}, f32[256,1024]{1,0:T(8,128)S(1)}, bf16[1,768,512]{2,1,0:T(8,128)(2,1)S(1)}) custom-call(bf16[256,1024]{1,0:T(8,128)(2,1)S(1)} %bitcast.4, bf16[768,512]{1,0:T(8,128)(2,1)S(1)} %get-tuple-element.29.refs_0_, bf16[768,512]{1,0:T(8,128)(2,1)} %collective-permute-done.1.refs_1_, ...), custom_call_target="tpu_custom_call" | custom-call | tf_op jit(solution)/shard_map/first/pallas_call | solution.py:476
  28.2 0.2 collective-permute-done.other
  28.4 0.6 %collective-permute-start.5 = (bf16[256,768]{1,0:T(8,128)(2,1)S(1)}, bf16[256,768]{1,0:T(8,128)(2,1)S(1)}, u32[]{:S(2)}, u32[]{:S(2)}) collective-permute-start(bf16[256,768]{1,0:T(8,128)(2,1)S(1)} %get-tuple-element.40.student.refs_3_), channel_id=1, source_target_pairs={{0,2},{1,5},{2,0},{3,7},{4,6},{5,1},{6,4},{7,3},{8,10},{9,13},{10,... | collective-permute-start | bytes 1179656 | tf_op jit(solution)/shard_map/ppermute | solution.py:408
  29.1 2.8 %classes.1 = (bf16[256,256]{1,0:T(8,128)(2,1)S(1)}, f32[1,512]{1,0:T(1,128)S(1)}, bf16[256,1024]{1,0:T(8,128)(2,1)S(1)}) custom-call(bf16[256,1024]{1,0:T(8,128)(2,1)S(1)} %collective-permute-done.other, bf16[256,768]{1,0:T(8,128)(2,1)S(1)} %get-tuple-element.40.student.refs_3_, bf16[256,128]{1,0:T(8,128)(2,1)S(1)} %get-tuple-element.28.tags_in, ...), custom_call_target="tpu_custom_call" | custom-call | tf_op jit(solution)/shard_map/classes/pallas_call | solution.py:490
  31.9 1.2 %collective-permute-start.2 = (bf16[256,256]{1,0:T(8,128)(2,1)S(1)}, bf16[256,256]{1,0:T(8,128)(2,1)S(1)}, u32[]{:S(2)}, u32[]{:S(2)}) collective-permute-start(bf16[256,256]{1,0:T(8,128)(2,1)S(1)} %get-tuple-element.37), channel_id=1, source_target_pairs={{0,1},{1,0},{2,3},{3,2},{4,5},{5,4},{6,7},{7,6},{8,9},{9,8},{10,11... | collective-permute-start | bytes 393224 | tf_op jit(solution)/shard_map/ppermute | solution.py:411
  33.1 0.6 %keep.1 = (f32[256,256]{1,0:T(8,128)S(1)}, bf16[272,256]{1,0:T(8,128)(2,1)S(1)}, f32[256,256]{1,0:T(8,128)S(1)}) custom-call(bf16[1024,1024]{1,0:T(8,128)(2,1)S(1)} %get-tuple-element.25.refs_2_.refs_0_, bf16[256,1024]{1,0:T(8,128)(2,1)S(1)} %get-tuple-element.34.refs_1_, f32[1,512]{1,0:T(1,128)S(1)} %get-tuple-element.35.refs_2_), custom_call_target="tpu_custom_call" | custom-call | tf_op jit(solution)/shard_map/keep/pallas_call | solution.py:509
  33.7 0.1 collective-permute-start.4
  33.8 0.3 collective-permute-done.2.refs_1_
  34.1 0.7 %collective-permute-start.3 = (bf16[256,256]{1,0:T(8,128)(2,1)S(1)}, bf16[256,256]{1,0:T(8,128)(2,1)S(1)}, u32[]{:S(2)}, u32[]{:S(2)}) collective-permute-start(bf16[256,256]{1,0:T(8,128)(2,1)S(1)} %fold.1), channel_id=1, source_target_pairs={{0,2},{1,5},{2,0},{3,7},{4,6},{5,1},{6,4},{7,3},{8,10},{9,13},{10,... | collective-permute-start | bytes 393224 | tf_op jit(solution)/shard_map/ppermute | solution.py:408
  34.9 0.3 collective-permute-done.4.refs_1_
  35.1 1.1 %collective-permute-done.5.refs_2_ = bf16[256,768]{1,0:T(8,128)(2,1)S(1)} collective-permute-done((bf16[256,768]{1,0:T(8,128)(2,1)S(1)}, bf16[256,768]{1,0:T(8,128)(2,1)S(1)}, u32[]{:S(2)}, u32[]{:S(2)}) %collective-permute-start.5) | collective-permute-done | bytes 393248 | tf_op jit(solution)/shard_map/ppermute | solution.py:408
  36.3 0.8 %own.1 = (f32[256,768]{1,0:T(8,128)S(1)}, f32[341]{0:T(512)}) custom-call(f32[256,256]{1,0:T(8,128)S(1)} %get-tuple-element.41.refs_0_, bf16[272,256]{1,0:T(8,128)(2,1)S(1)} %collective-permute-done.4.refs_1_, f32[1,512]{1,0:T(1,128)S(1)} %get-tuple-element.35.refs_2_, bf16[256,768]{1,0:T(8,128)(2,1)S(1)} %get-tuple-element.40.student.refs_3_), custom_call_target="tpu_custom_call" | custom-call | tf_op jit(solution)/shard_map/own/pallas_call | solution.py:527
  37.0 2.1 %collective-permute-done.3.refs_0_ = bf16[256,256]{1,0:T(8,128)(2,1)S(1)} collective-permute-done((bf16[256,256]{1,0:T(8,128)(2,1)S(1)}, bf16[256,256]{1,0:T(8,128)(2,1)S(1)}, u32[]{:S(2)}, u32[]{:S(2)}) %collective-permute-start.3) | collective-permute-done | bytes 131104 | tf_op jit(solution)/shard_map/ppermute | solution.py:408
  39.2 0.3 head.1
  39.4 14.6 %all_to_all.10.parts = bf16[8,32,768]{2,1,0:T(8,128)(2,1)S(1)} all-to-all(bf16[8,32,768]{2,1,0:T(8,128)(2,1)S(1)} %bitcast.6), channel_id=1, replica_groups={{0,4,8,12,16,20,24,28},{2,6,10,14,18,22,26,30},{1,3,9,11,17,19,25,27},{..., dimensions={0} | all-to-all | bytes 786432 | tf_op jit(solution)/shard_map/all_to_all | solution.py:542
  54.0 0.7 %total.1 = f32[32,768]{1,0:T(8,128)} custom-call(bf16[8,32,768]{2,1,0:T(8,128)(2,1)S(1)} %all_to_all.10.parts), custom_call_target="tpu_custom_call" | custom-call | tf_op jit(solution)/shard_map/total/pallas_call | solution.py:554
  (7 shorter events, 0.1 us)
Async XLA Ops:
  3.0 23.5 %all-to-all-start = ((bf16[16,16,1024]{2,1,0:T(8,128)(2,1)}), bf16[16,16,1024]{2,1,0:T(8,128)(2,1)S(1)}, u32[]{:S(2)}, u32[]{:S(2)}) async-start(bf16[16,16,1024]{2,1,0:T(8,128)(2,1)} %bitcast.7), calls=%async_computation | async-start | bytes 1048576 | tf_op jit(solution)/shard_map/all_to_all | solution.py:454
  11.4 1.6 %copy-start = (bf16[1024,1024]{1,0:T(8,128)(2,1)S(1)}, bf16[1024,1024]{1,0:T(8,128)(2,1)}, u32[]{:S(2)}) copy-start(bf16[1024,1024]{1,0:T(8,128)(2,1)} %freqs_in.1) | copy-start | bytes 6291460
  13.0 1.1 %copy-start.1 = (bf16[768,512]{1,0:T(8,128)(2,1)S(1)}, bf16[768,512]{1,0:T(8,128)(2,1)}, u32[]{:S(2)}) copy-start(bf16[768,512]{1,0:T(8,128)(2,1)} %head_in.1) | copy-start | bytes 2359300
  14.1 0.7 %copy-start.2 = (f32[8,128]{1,0:T(8,128)S(1)}, f32[8,128]{1,0:T(8,128)}, u32[]{:S(2)}) copy-start(f32[8,128]{1,0:T(8,128)} %get-tuple-element.24._) | copy-start | bytes 12292
  15.0 11.5 %collective-permute-start.1 = (bf16[768,512]{1,0:T(8,128)(2,1)S(1)}, bf16[768,512]{1,0:T(8,128)(2,1)}, u32[]{:S(2)}, u32[]{:S(2)}) collective-permute-start(bf16[768,512]{1,0:T(8,128)(2,1)S(1)} %get-tuple-element.29.refs_0_), channel_id=1, source_target_pairs={{0,1},{1,0},{2,3},{3,2},{4,5},{5,4},{6,7},{7,6},{8,9},{9,8},{10,11... | collective-permute-start | bytes 2359304 | tf_op jit(solution)/shard_map/ppermute | solution.py:411
  26.5 1.9 %collective-permute-start = (bf16[256,1024]{1,0:T(8,128)(2,1)S(1)}, bf16[256,1024]{1,0:T(8,128)(2,1)S(1)}, u32[]{:S(2)}, u32[]{:S(2)}) collective-permute-start(bf16[256,1024]{1,0:T(8,128)(2,1)S(1)} %bitcast.3), channel_id=1, source_target_pairs={{0,1},{1,0},{2,3},{3,2},{4,5},{5,4},{6,7},{7,6},{8,9},{9,8},{10,11... | collective-permute-start | bytes 1572872 | tf_op jit(solution)/shard_map/ppermute | solution.py:411
  28.4 7.8 %collective-permute-start.5 = (bf16[256,768]{1,0:T(8,128)(2,1)S(1)}, bf16[256,768]{1,0:T(8,128)(2,1)S(1)}, u32[]{:S(2)}, u32[]{:S(2)}) collective-permute-start(bf16[256,768]{1,0:T(8,128)(2,1)S(1)} %get-tuple-element.40.student.refs_3_), channel_id=1, source_target_pairs={{0,2},{1,5},{2,0},{3,7},{4,6},{5,1},{6,4},{7,3},{8,10},{9,13},{10,... | collective-permute-start | bytes 1179656 | tf_op jit(solution)/shard_map/ppermute | solution.py:408
  31.9 2.2 %collective-permute-start.2 = (bf16[256,256]{1,0:T(8,128)(2,1)S(1)}, bf16[256,256]{1,0:T(8,128)(2,1)S(1)}, u32[]{:S(2)}, u32[]{:S(2)}) collective-permute-start(bf16[256,256]{1,0:T(8,128)(2,1)S(1)} %get-tuple-element.37), channel_id=1, source_target_pairs={{0,1},{1,0},{2,3},{3,2},{4,5},{5,4},{6,7},{7,6},{8,9},{9,8},{10,11... | collective-permute-start | bytes 393224 | tf_op jit(solution)/shard_map/ppermute | solution.py:411
  33.7 1.4 %collective-permute-start.4 = (bf16[272,256]{1,0:T(8,128)(2,1)S(1)}, bf16[272,256]{1,0:T(8,128)(2,1)S(1)}, u32[]{:S(2)}, u32[]{:S(2)}) collective-permute-start(bf16[272,256]{1,0:T(8,128)(2,1)S(1)} %get-tuple-element.39), channel_id=1, source_target_pairs={{0,1},{1,0},{2,3},{3,2},{4,5},{5,4},{6,7},{7,6},{8,9},{9,8},{10,11... | collective-permute-start | bytes 417800 | tf_op jit(solution)/shard_map/ppermute | solution.py:411
  34.1 5.0 %collective-permute-start.3 = (bf16[256,256]{1,0:T(8,128)(2,1)S(1)}, bf16[256,256]{1,0:T(8,128)(2,1)S(1)}, u32[]{:S(2)}, u32[]{:S(2)}) collective-permute-start(bf16[256,256]{1,0:T(8,128)(2,1)S(1)} %fold.1), channel_id=1, source_target_pairs={{0,2},{1,5},{2,0},{3,7},{4,6},{5,1},{6,4},{7,3},{8,10},{9,13},{10,... | collective-permute-start | bytes 393224 | tf_op jit(solution)/shard_map/ppermute | solution.py:408
